TPU v7x, 32 devices: a whole 2x2x4 slice. The times are simulated.
32 devices in a mesh: img: 4 (over y, x), tile: 8 (over z, core).
Axes of the slice: x: 2, y: 2, z: 4, core: 2. Of those that a mesh axis runs over, the one named last changes fastest.
Arguments:
- patches: bfloat16 [32, 32, 32, 768], P(('img', 'tile')), may hold values from -6 to 6
- norm_gain: float32 [768], replicated, may hold values from 0.1 to 1.9
- norm_bias: float32 [768], replicated, may hold values from -3 to 3
- up_weight: bfloat16 [768, 3072], replicated, may hold values from -0.21875 to 0.21875
- up_bias: float32 [3072], replicated, may hold values from -3 to 3
- down_weight: bfloat16 [3072, 768], replicated, may hold values from -0.109375 to 0.109375
- down_bias: float32 [768], replicated, may hold values from -3 to 3
- final_gain: float32 [768], replicated, may hold values from 0.1 to 1.9
- final_bias: float32 [768], replicated, may hold values from -3 to 3
- head_weight: bfloat16 [768, 512], replicated, may hold values from -0.21875 to 0.21875
- gauss_rows: bfloat16 [65536, 512], P(('img', 'tile')), may hold values from -48 to 48
- tile_lists: int32 [32, 32, 128], P('img', 'tile'), may hold values from 0 to 65535, as said below
- alphas: float32 [32, 32, 32, 128], P('img', 'tile'), may hold values from 0.002 to 0.05
Outputs:
- rendered: bfloat16 [32, 32, 32, 512], P('img', 'tile')
- feature_grad: float32 [65536, 512], P(('img', 'tile'))
Inputs may be any that keep to these rules, and one draw needn't show every extreme that they name: `tile_lists`: among the 4096 entries of the tiles held by one device (one index of img and of tile), at most 256 name Gaussians held by any one device, the holder of id g being index g // 2048 of img+tile.
All inputs are finite; a program needn't handle non-finite values.
Results may differ from a plain program's by a relative error of at most 0.0049.
Values may be sent and summed in bfloat16 or wider, within the bound.
No kernel may reach another device: no remote copies, remote signals or barrier semaphores. Data moves between devices by JAX's collectives and lax.ppermute only.
A program may use at most 128 MiB of HBM per device.

v0:
```python
import functools

import jax
import jax.numpy as jnp
from jax import lax
from jax.experimental import pallas as pl
from jax.experimental.pallas import tpu as pltpu
from jax.sharding import PartitionSpec as P

F32 = jnp.float32
BF16 = jnp.bfloat16
I32 = jnp.int32
VMEM_BYTES = 50 * 1024 * 1024
LANES = (((1,), (1,)), ((), ()))
ROWS = (((0,), (0,)), ((), ()))


def params():
    return pltpu.CompilerParams(vmem_limit_bytes=VMEM_BYTES)


def index_kernel(peers, cap, rows_held, ids_ref, req_ref, own_ref, rank_ref):
    tiles, length = ids_ref.shape
    earlier = lax.broadcasted_iota(I32, (length, length), 0)
    later = lax.broadcasted_iota(I32, (length, length), 1)
    upper = (earlier < later).astype(BF16)
    every = jnp.ones((length, length), BF16)
    peer_id = lax.broadcasted_iota(I32, (peers, length), 0)
    slot_id = lax.broadcasted_iota(I32, (cap, length), 0)
    hots = []
    for t in range(tiles):
        owner = ids_ref[t : t + 1, :] // rows_held
        own_ref[t : t + 1, :] = owner.astype(F32).astype(BF16)
        hots.append((jnp.broadcast_to(owner, (peers, length)) == peer_id).astype(F32))
    stack = jnp.concatenate(hots, 0).astype(BF16)
    within = jnp.dot(stack, upper, preferred_element_type=F32)
    totals = jnp.dot(stack, every, preferred_element_type=F32)
    offset = jnp.zeros((peers, length), F32)
    found = jnp.zeros((2 * peers, cap), F32)
    for t in range(tiles):
        own_rows = slice(t * peers, (t + 1) * peers)
        rank = jnp.sum(hots[t] * (within[own_rows] + offset), axis=0, keepdims=True).astype(I32)
        offset = offset + totals[own_rows]
        rank_ref[t : t + 1, :] = rank.astype(F32).astype(BF16)
        ids = ids_ref[t : t + 1, :]
        row = ids - (ids // rows_held) * rows_held + 1
        high = (row >> 6).astype(F32)
        low = (row & 63).astype(F32)
        digits = jnp.concatenate([hots[t] * high, hots[t] * low], 0).astype(BF16)
        slots = (jnp.broadcast_to(rank, (cap, length)) == slot_id).astype(F32).astype(BF16)
        found = found + lax.dot_general(digits, slots, LANES, preferred_element_type=F32)
    req_ref[...] = (found[:peers] * 64.0 + found[peers:]).astype(I32) - 1


def index(ids, peers, cap, rows_held):
    like = jax.ShapeDtypeStruct(ids.shape, BF16)
    return pl.pallas_call(
        functools.partial(index_kernel, peers, cap, rows_held),
        out_shape=(jax.ShapeDtypeStruct((peers, cap), I32), like, like),
        compiler_params=params(),
        cost_estimate=pl.CostEstimate(flops=10**9, bytes_accessed=10**7, transcendentals=0),
        name="index",
    )(ids)


def weights_kernel(alpha_ref, out_ref):
    alpha = alpha_ref[...]
    length = alpha.shape[1]
    logs = jnp.log1p(-alpha)
    earlier = lax.broadcasted_iota(I32, (length, length), 0)
    later = lax.broadcasted_iota(I32, (length, length), 1)
    upper = (earlier < later).astype(F32)
    before = jnp.dot(logs, upper, preferred_element_type=F32, precision=lax.Precision.HIGHEST)
    out_ref[...] = (alpha * jnp.exp(before)).astype(BF16)


def weights(alphas):
    return pl.pallas_call(
        weights_kernel,
        out_shape=jax.ShapeDtypeStruct(alphas.shape, BF16),
        compiler_params=params(),
        cost_estimate=pl.CostEstimate(flops=10**8, bytes_accessed=10**6, transcendentals=0),
        name="weights",
    )(alphas)


def spread_kernel(near, cap, packs, base_ref, *refs):
    out_ref = refs[-1]
    own_all, rank_all, weight_all = (sum(ref[...].astype(F32) for ref in refs[k : 3 * packs : 3]) for k in range(3))
    tiles, length = own_all.shape
    cells = weight_all.shape[0] // tiles
    slot_id = lax.broadcasted_iota(I32, (cap, length), 0)
    for t in range(tiles):
        own = own_all[t : t + 1, :].astype(I32)
        rank = rank_all[t : t + 1, :].astype(I32)
        here = slice(t * cells, (t + 1) * cells)
        weight = weight_all[here, :]
        by_owner = [jnp.where(own == base_ref[o], weight, 0.0) for o in range(near)]
        slots = (jnp.broadcast_to(rank, (cap, length)) == slot_id).astype(F32).astype(BF16)
        moved = lax.dot_general(
            jnp.concatenate(by_owner, 0).astype(BF16), slots, LANES, preferred_element_type=F32
        ).astype(BF16)
        if cap % 128 == 0:
            for o in range(near):
                out_ref[here, o * cap : (o + 1) * cap] = moved[o * cells : (o + 1) * cells]
        else:
            out_ref[here, :] = jnp.concatenate([moved[o * cells : (o + 1) * cells] for o in range(near)], 1)


def spread(owners, packs, tiles, cells, cap):
    length = packs[0].shape[1]
    near = owners.shape[0]
    step = 16
    first = tiles * cells // step
    specs = [
        pl.BlockSpec((step, length), lambda t: (first + t, 0)),
        pl.BlockSpec((step, length), lambda t: (first + tiles // step + t, 0)),
        pl.BlockSpec((step * cells, length), lambda t: (t, 0)),
    ]
    return pl.pallas_call(
        functools.partial(spread_kernel, near, cap, len(packs)),
        grid=(tiles // step,),
        in_specs=[pl.BlockSpec(memory_space=pltpu.SMEM)] + specs * len(packs),
        out_specs=pl.BlockSpec((step * cells, near * cap), lambda t: (t, 0)),
        out_shape=jax.ShapeDtypeStruct((tiles * cells, near * cap), BF16),
        compiler_params=params(),
        cost_estimate=pl.CostEstimate(flops=10**8, bytes_accessed=10**6, transcendentals=0),
        name="spread",
    )(owners, *[pack for pack in packs for _ in range(3)])


def gather_kernel(group, cap, asked_ref, rows_ref, out_ref):
    first = pl.program_id(0) * group
    asked = asked_ref[...]
    peer = lax.broadcasted_iota(I32, asked.shape, 1)
    held = rows_ref.shape[0]
    row_id = lax.broadcasted_iota(I32, (cap, held), 1)
    picks = []
    for q in range(group):
        column = jnp.sum(jnp.where(peer == first + q, asked, 0), axis=1, keepdims=True)
        picks.append((jnp.broadcast_to(column, (cap, held)) == row_id).astype(F32).astype(BF16))
    pick = jnp.concatenate(picks, 0)
    out_ref[...] = jnp.dot(pick, rows_ref[...], preferred_element_type=F32).astype(BF16)


def gather(asked, rows):
    near, cap = asked.shape
    held, feat = rows.shape
    group = max(1, min(near, 1024 // cap))
    return pl.pallas_call(
        functools.partial(gather_kernel, group, cap),
        grid=(near // group,),
        in_specs=[pl.BlockSpec((cap, near), lambda i: (0, 0)), pl.BlockSpec((held, feat), lambda i: (0, 0))],
        out_specs=pl.BlockSpec((group * cap, feat), lambda i: (i, 0)),
        out_shape=jax.ShapeDtypeStruct((near * cap, feat), BF16),
        compiler_params=params(),
        cost_estimate=pl.CostEstimate(flops=10**8, bytes_accessed=10**6, transcendentals=0),
        name="gather",
    )(asked.T, rows)


def blend_kernel(n_parts, weight_ref, rows_ref, *rest):
    color = jnp.dot(weight_ref[...], rows_ref[...], preferred_element_type=F32)
    for part_ref in rest[:n_parts]:
        color = color + part_ref[...].astype(F32)
    rest[n_parts][...] = color.astype(BF16)


def last_blend_kernel(n_parts, place_ref, weight_ref, rows_ref, *rest):
    parts, target_ref = rest[:n_parts], rest[n_parts]
    color_ref, diff_ref = rest[-2:]
    color = jnp.dot(weight_ref[...], rows_ref[...], preferred_element_type=F32)
    for part_ref in parts:
        color = color + part_ref[...].astype(F32)
    color_ref[...] = color.astype(BF16)
    cells = target_ref.shape[1]
    per_step = color.shape[0] // cells
    for k in range(per_step):
        at = place_ref[pl.program_id(0) * per_step + k]
        here = slice(k * cells, (k + 1) * cells)
        diff_ref[here, :] = (color[here] - target_ref[at].astype(F32)).astype(BF16)


def blend(weight, rows, parts=(), place=None, target=None):
    cells, slots = weight.shape
    feat = rows.shape[1]
    block = min(cells, 256)
    cell_block = pl.BlockSpec((block, feat), lambda i: (i, 0))
    out = jax.ShapeDtypeStruct((cells, feat), BF16)
    last = place is not None
    in_specs = [pl.BlockSpec((block, slots), lambda i: (i, 0)), pl.BlockSpec((slots, feat), lambda i: (0, 0))]
    in_specs += [cell_block] * len(parts)
    args = [weight, rows, *parts]
    if last:
        in_specs = [pl.BlockSpec(memory_space=pltpu.SMEM)] + in_specs + [pl.BlockSpec(target.shape, lambda i: (0, 0, 0))]
        args = [place, *args, target]
    return pl.pallas_call(
        functools.partial(last_blend_kernel if last else blend_kernel, len(parts)),
        grid=(cells // block,),
        in_specs=in_specs,
        out_specs=(cell_block, cell_block) if last else cell_block,
        out_shape=(out, out) if last else out,
        compiler_params=params(),
        cost_estimate=pl.CostEstimate(flops=4 * 10**9, bytes_accessed=10**7, transcendentals=0),
        name="blend",
    )(*args)


def terms_kernel(weight_ref, *refs):
    diff = refs[0][...]
    for more_ref in refs[1:-1]:
        diff = diff + more_ref[...]
    refs[-1][...] = lax.dot_general(weight_ref[...], diff, ROWS, preferred_element_type=F32).astype(BF16)


def terms(weight, *diffs):
    cells, slots = weight.shape
    feat = diffs[0].shape[1]
    block = min(slots, 1024)
    return pl.pallas_call(
        terms_kernel,
        grid=(slots // block,),
        in_specs=[pl.BlockSpec((cells, block), lambda i: (0, i))]
        + [pl.BlockSpec((cells, feat), lambda i: (0, 0))] * len(diffs),
        out_specs=pl.BlockSpec((block, feat), lambda i: (i, 0)),
        out_shape=jax.ShapeDtypeStruct((slots, feat), BF16),
        compiler_params=params(),
        cost_estimate=pl.CostEstimate(flops=10**11, bytes_accessed=10**7, transcendentals=0),
        name="terms",
    )(weight, *diffs)


def add_rows_kernel(count, *refs):
    out_ref = refs[-1]
    block = out_ref.shape[0]
    total = None if len(refs) == 2 * count + 1 else refs[2 * count][...]
    for n in range(count):
        asked_ref, terms_ref = refs[n], refs[count + n]
        near, cap = asked_ref.shape
        row_id = lax.broadcasted_iota(I32, (block, cap), 0) + pl.program_id(0) * block
        picks = []
        for o in range(near):
            asked = jnp.broadcast_to(asked_ref[o : o + 1, :], (block, cap))
            picks.append((asked == row_id).astype(F32).astype(BF16))
        got = jnp.dot(jnp.concatenate(picks, 1), terms_ref[...], preferred_element_type=F32)
        total = got if total is None else total + got
    out_ref[...] = total


def add_rows(askeds, arrivals, held, before=None):
    near, cap = askeds[0].shape
    feat = arrivals[0].shape[1]
    count = len(askeds)
    block = min(held, 512)
    row_block = pl.BlockSpec((block, feat), lambda i: (i, 0))
    more = before is not None
    in_specs = [pl.BlockSpec((near, cap), lambda i: (0, 0))] * count
    in_specs += [pl.BlockSpec((near * cap, feat), lambda i: (0, 0))] * count
    return pl.pallas_call(
        functools.partial(add_rows_kernel, count),
        grid=(held // block,),
        in_specs=in_specs + [row_block] * more,
        out_specs=row_block,
        out_shape=jax.ShapeDtypeStruct((held, feat), F32),
        compiler_params=params(),
        cost_estimate=pl.CostEstimate(flops=5 * count * 10**9, bytes_accessed=10**7, transcendentals=0),
        name="add_rows",
    )(*askeds, *arrivals, *((before,) if more else ()))


def layer_norm(rows, gain, bias):
    mean = jnp.mean(rows, axis=-1, keepdims=True)
    centred = rows - mean
    var = jnp.mean(centred * centred, axis=-1, keepdims=True)
    return centred * lax.rsqrt(var + 1e-05) * gain + bias


def encode_kernel(strips, *refs):
    gain, bias, up, up_bias, down, down_bias, last_gain, last_bias, head = refs[strips:-1]
    out_ref = refs[-1]
    hidden = up.shape[1]
    step = 768 if hidden % 768 == 0 else hidden
    group = max(1, strips // 2)
    for first in range(0, strips, group):
        wide = jnp.concatenate([ref[...] for ref in refs[first : first + group]], 0).astype(F32)
        normed = layer_norm(wide, gain[...], bias[...]).astype(BF16)
        block_out = wide + down_bias[...]
        for k in range(0, hidden, step):
            inner = jnp.dot(normed, up[:, k : k + step], preferred_element_type=F32) + up_bias[k : k + step]
            act = (inner * jax.nn.sigmoid(1.702 * inner)).astype(BF16)
            block_out = block_out + jnp.dot(act, down[k : k + step, :], preferred_element_type=F32)
        final = layer_norm(block_out, last_gain[...], last_bias[...]).astype(BF16)
        embed = jnp.dot(final, head[...], preferred_element_type=F32)
        scale = lax.rsqrt(jnp.mean(embed * embed, axis=-1, keepdims=True) + 1e-06)
        target = (embed * scale).astype(BF16)
        cells = target.shape[0] // group
        for n in range(group):
            out_ref[first + n] = target[n * cells : (n + 1) * cells]


def encode(strips, *weights_and_biases):
    cells = strips[0].shape[0]
    return pl.pallas_call(
        functools.partial(encode_kernel, len(strips)),
        out_shape=jax.ShapeDtypeStruct((len(strips), cells, weights_and_biases[-1].shape[1]), BF16),
        compiler_params=params(),
        cost_estimate=pl.CostEstimate(flops=10**11, bytes_accessed=10**7, transcendentals=0),
        name="encode",
    )(*strips, *weights_and_biases)


def on_device(
    patches,
    norm_gain,
    norm_bias,
    up_weight,
    up_bias,
    down_weight,
    down_bias,
    final_gain,
    final_bias,
    head_weight,
    gauss_rows,
    tile_lists,
    alphas,
):
    view_count, tiles_view, cells, width = patches.shape
    feat = head_weight.shape[1]
    n_img = lax.axis_size("img")
    n_tile = lax.axis_size("tile")
    peers = n_img * n_tile
    both = ("img", "tile")
    held = gauss_rows.shape[0]
    group_views, strip_tiles, list_len = tile_lists.shape
    tiles = group_views * strip_tiles
    cap = 2 * tiles * list_len // peers

    wide_layer = n_tile // 4
    near = n_img * wide_layer
    tile = lax.axis_index("tile")
    layer = tile // wide_layer
    low = layer < 2
    groups = [[i * n_tile + z * wide_layer + k for i in range(n_img) for k in range(wide_layer)] for z in range(4)]

    def moves(*pairs):
        return [(a * wide_layer + k, b * wide_layer + k) for a, b in pairs for k in range(wide_layer)]

    beside = moves((0, 1), (1, 0), (2, 3), (3, 2))
    middle = moves((1, 2), (2, 1))
    inwards = moves((0, 1), (3, 2))
    outwards = moves((1, 0), (2, 3))

    def move(x, pairs):
        return lax.ppermute(x, "tile", pairs)

    def exchange(x):
        return lax.all_to_all(x, both, split_axis=0, concat_axis=0, axis_index_groups=groups, tiled=True)

    def tie(*values):
        return lax.optimization_barrier(values)

    request, own, rank = index(tile_lists.reshape(tiles, list_len), peers, cap, held)
    weight = weights(alphas.reshape(tiles * cells, list_len))
    packed = jnp.concatenate([weight, own, rank], 0)
    request, patches = tie(request, patches)
    asked = lax.all_to_all(request, both, split_axis=0, concat_axis=0, tiled=True)
    chips = n_tile // 2
    core = tile % 2
    chip = tile // 2
    patches = patches.reshape(chips, 2, -1, width)
    others = lax.dynamic_index_in_dim(patches, 1 - core, 1, keepdims=False)
    others = move(others, [(a, a ^ 1) for a in range(n_tile)])
    asked, others, packed = tie(asked, others, packed)
    far_to_outer = move(packed, moves((0, 3), (3, 0)))
    far_to_inner = move(packed, moves((0, 2), (3, 1)))
    pairs = jnp.concatenate([lax.dynamic_index_in_dim(patches, core, 1, keepdims=False), others], 1)
    strips = []
    for n in range(chips):
        pair = lax.dynamic_index_in_dim(pairs, lax.rem(chip + n, chips), 0, keepdims=False)
        strips.append(move(pair, [(a, (a + 2 * n) % n_tile) for a in range(n_tile)]) if n else pair)
    view = jnp.arange(n_tile, dtype=I32)
    place = lax.rem(chip + chips - view // 2, chips) * 2 + (view % 2 != core).astype(I32)
    asked = asked.reshape(n_img, 4, wide_layer, cap)
    sets = (jnp.where(low, 3, 0), jnp.where(low, 2, 1), layer ^ 1, layer)
    lists = [lax.dynamic_index_in_dim(asked, s, 1, keepdims=False).reshape(near, cap) for s in sets]
    owners = (
        jnp.arange(n_img, dtype=I32)[:, None] * n_tile
        + layer * wide_layer
        + jnp.arange(wide_layer, dtype=I32)[None, :]
    ).reshape(near)

    def spread_of(*packs):
        return spread(owners, packs, tiles, cells, cap)

    looked, lists[1] = tie(gather(lists[0], gauss_rows), lists[1])
    rows_1 = exchange(looked)
    looked_2 = gather(lists[1], gauss_rows)
    looked_2, lists[2] = tie(looked_2, lists[2])
    spread_1 = spread_of(far_to_outer, far_to_inner)
    looked_3 = gather(lists[2], gauss_rows)
    looked_2, looked_3, spread_1, rows_1, packed = tie(looked_2, looked_3, spread_1, rows_1, packed)

    rows_2 = exchange(looked_2)
    part_1 = blend(spread_1, rows_1)
    moved_1 = move(part_1, inwards)
    near_to_outer = move(packed, moves((1, 3), (2, 0)))
    near_to_inner = move(packed, middle)
    from_beside = move(packed, beside)
    part_1, *strips = tie(part_1, *strips)
    target = encode(
        strips, norm_gain, norm_bias, up_weight, up_bias, down_weight, down_bias, final_gain, final_bias, head_weight
    )
    looked_3, rows_2, part_1, target, lists[3], near_to_outer, near_to_inner, from_beside = tie(
        looked_3, rows_2, part_1, target, lists[3], near_to_outer, near_to_inner, from_beside
    )

    rows_3 = exchange(looked_3)
    far = move(part_1 + moved_1, middle)
    spread_2 = spread_of(near_to_outer, near_to_inner)
    part_2 = blend(spread_2, rows_2)
    moved_2 = move(part_2, inwards)
    part_2, lists[3], from_beside = tie(part_2, lists[3], from_beside)
    looked_4 = gather(lists[3], gauss_rows)
    spread_3 = spread_of(from_beside)
    looked_4, rows_3, far, spread_3, packed = tie(looked_4, rows_3, far, spread_3, packed)

    rows_4 = exchange(looked_4)
    part_3 = blend(spread_3, rows_3, (far,))
    beside_part = move(part_3, beside)
    part_2, moved_2, part_3, packed = tie(part_2, moved_2, part_3, packed)
    middle_part = move(part_2 + moved_2, middle)
    spread_4 = spread_of(packed)
    color, diff = blend(spread_4, rows_4, (beside_part, middle_part), place, target.reshape(n_tile, -1, feat))
    spreads = (spread_1, spread_2, spread_3, spread_4)

    diff_beside = move(diff, beside)
    diff_middle = move(diff, middle)
    far_middle = move(diff_beside, middle)
    diff_out = move(diff_middle, outwards)
    far_out = move(far_middle, outwards)
    back = []
    for n, diffs in ((3, (diff,)), (2, (diff_beside,)), (1, (diff_middle, diff_out)), (0, (far_middle, far_out))):
        term = terms(spreads[n], *diffs)
        if back:
            term, back[-1] = lax.optimization_barrier((term, back[-1]))
        back.append(exchange(term))
    grad = add_rows([lists[3], lists[2], lists[1]], back[:3], held)
    grad = add_rows([lists[0]], back[3:], held, grad)
    return (color.reshape(group_views, strip_tiles, cells, feat), grad)


def solution(mesh):
    placed = (
        P(("img", "tile"), None, None, None),
        P(),
        P(),
        P(),
        P(),
        P(),
        P(),
        P(),
        P(),
        P(),
        P(("img", "tile"), None),
        P("img", "tile", None),
        P("img", "tile", None, None),
    )
    return jax.shard_map(
        on_device,
        mesh=mesh,
        in_specs=placed,
        out_specs=(P("img", "tile", None, None), P(("img", "tile"), None)),
        check_vma=False,
    )
```

profile of v0, /device:TPU:0, one launch (start us, length us, event | category | flops | bytes accessed | tf_op | source)
XLA Modules:
  0.0 322.3 jit_solution(3954392208135889323)
XLA Ops:
  0.7 0.7 copy-done.6
  1.4 1.3 index.1
  2.8 1.0 dynamic-slice_bitcast_fusion
  4.2 0.6 copy.31
  4.9 7.0 %all-to-all-start = ((s32[32,1,256]{2,1,0:T(1,128)}), s32[32,1,256]{2,1,0:T(1,128)S(1)}, u32[]{:S(2)}, u32[]{:S(2)}) async-start(s32[32,1,256]{2,1,0:T(1,128)} %copy.31), calls=%async_computation | async-start | bytes 65536 | tf_op jit(solution)/shard_map/all_to_all | solution.py:366
  11.8 0.7 weights.1
  12.6 6.5 %all-to-all-done = s32[32,1,256]{2,1,0:T(1,128)S(1)} async-done(((s32[32,1,256]{2,1,0:T(1,128)}), s32[32,1,256]{2,1,0:T(1,128)S(1)}, u32[]{:S(2)}, u32[]{:S(2)}) %all-to-all-start) | async-done | bytes 32800 | tf_op jit(solution)/shard_map/all_to_all | solution.py:366
  19.3 7.5 %gather.4 = bf16[2048,512]{1,0:T(8,128)(2,1)} custom-call(s32[256,8]{1,0:T(8,128)S(1)} %copy.33.asked_ref, bf16[2048,512]{1,0:T(8,128)(2,1)} %rows_ref.7), custom_call_target="tpu_custom_call" | custom-call | flops 100000000 | bytes 1000000 | tf_op jit(solution)/shard_map/gather/pallas_call | solution.py:150
  26.8 3.6 %all-to-all-start.1 = ((bf16[8,256,512]{2,1,0:T(8,128)(2,1)}), bf16[8,256,512]{2,1,0:T(8,128)(2,1)S(1)}, u32[]{:S(2)}, u32[]{:S(2)}) async-start(bf16[8,256,512]{2,1,0:T(8,128)(2,1)} %bitcast.8), calls=%async_computation.1 | async-start | bytes 4194304 | tf_op jit(solution)/shard_map/all_to_all | solution.py:357
  30.4 2.4 collective-permute-start.2
  32.8 4.3 %collective-permute-start.1 = (bf16[1088,128]{1,0:T(8,128)(2,1)S(1)}, bf16[1088,128]{1,0:T(8,128)(2,1)S(1)}, u32[]{:S(2)}, u32[]{:S(2)}) collective-permute-start(bf16[1088,128]{1,0:T(8,128)(2,1)S(1)} %pad_maximum_fusion.refs_0_.refs_1_.refs_2_), channel_id=1, source_target_pairs={{0,6},{1,7},{6,0},{7,1},{8,14},{9,15},{14,8},{15,9},{16,22},{17,23... | collective-permute-start | bytes 835592 | tf_op jit(solution)/shard_map/ppermute | solution.py:354
  37.3 2.6 fusion.1
  39.9 1.4 collective-permute-start.5
  42.1 7.4 %gather.5 = bf16[2048,512]{1,0:T(8,128)(2,1)} custom-call(s32[256,8]{1,0:T(8,128)S(1)} %copy.35.asked_ref, bf16[2048,512]{1,0:T(8,128)(2,1)} %rows_ref.7), custom_call_target="tpu_custom_call" | custom-call | flops 100000000 | bytes 1000000 | tf_op jit(solution)/shard_map/gather/pallas_call | solution.py:150
  49.6 7.4 %gather.6 = bf16[2048,512]{1,0:T(8,128)(2,1)} custom-call(s32[256,8]{1,0:T(8,128)S(1)} %copy.37.asked_ref, bf16[2048,512]{1,0:T(8,128)(2,1)} %rows_ref.7), custom_call_target="tpu_custom_call" | custom-call | flops 100000000 | bytes 1000000 | tf_op jit(solution)/shard_map/gather/pallas_call | solution.py:150
  57.0 3.4 %spread.4.weight_ref = bf16[1024,2048]{1,0:T(8,128)(2,1)} custom-call(s32[8]{0:T(128)S(1)} %add.99.base_ref, bf16[1088,128]{1,0:T(8,128)(2,1)S(1)} %collective-permute-done.1.refs_0_.refs_1_.refs_2_, bf16[1088,128]{1,0:T(8,128)(2,1)S(1)} %collective-permute-done.1.refs_0_.refs_1_.refs_2_, ...), custom_call_target="tpu_custom_call" | custom-call | flops 100000000 | bytes 1000000 | tf_op jit(solution)/shard_map/spread/pallas_call | solution.py:120
  60.4 3.8 %collective-permute-start.8 = (bf16[1088,128]{1,0:T(8,128)(2,1)S(1)}, bf16[1088,128]{1,0:T(8,128)(2,1)S(1)}, u32[]{:S(2)}, u32[]{:S(2)}) collective-permute-start(bf16[1088,128]{1,0:T(8,128)(2,1)S(1)} %pad_maximum_fusion.refs_0_.refs_1_.refs_2_), channel_id=1, source_target_pairs={{0,2},{1,3},{2,0},{3,1},{4,6},{5,7},{6,4},{7,5},{8,10},{9,11},{10,... | collective-permute-start | bytes 835592 | tf_op jit(solution)/shard_map/ppermute | solution.py:354
  64.2 0.7 collective-permute-start.7
  64.9 4.4 %all-to-all-start.2 = ((bf16[8,256,512]{2,1,0:T(8,128)(2,1)}), bf16[8,256,512]{2,1,0:T(8,128)(2,1)}, u32[]{:S(2)}, u32[]{:S(2)}) async-start(bf16[8,256,512]{2,1,0:T(8,128)(2,1)} %bitcast.10), calls=%async_computation.2 | async-start | bytes 4194304 | tf_op jit(solution)/shard_map/all_to_all | solution.py:357
  69.3 5.5 %blend.4 = bf16[1024,512]{1,0:T(8,128)(2,1)} custom-call(bf16[1024,2048]{1,0:T(8,128)(2,1)} %spread.4.weight_ref, bf16[2048,512]{1,0:T(8,128)(2,1)S(1)} %bitcast.57), custom_call_target="tpu_custom_call" | custom-call | flops 4000000000 | bytes 10000000 | tf_op jit(solution)/shard_map/blend/pallas_call | solution.py:197
  74.9 1.3 collective-permute-start.6
  76.2 4.7 %collective-permute-start.10 = (bf16[1024,512]{1,0:T(8,128)(2,1)}, bf16[1024,512]{1,0:T(8,128)(2,1)}, u32[]{:S(2)}, u32[]{:S(2)}) collective-permute-start(bf16[1024,512]{1,0:T(8,128)(2,1)} %blend.4), channel_id=1, source_target_pairs={{0,2},{1,3},{6,4},{7,5},{8,10},{9,11},{14,12},{15,13},{16,18},{17,... | collective-permute-start | bytes 3145736 | tf_op jit(solution)/shard_map/ppermute | solution.py:354
  80.9 1.1 collective-permute-done.4.refs_2_
  82.0 16.5 %encode.1 = bf16[4,256,512]{2,1,0:T(8,128)(2,1)S(1)} custom-call(bf16[256,768]{1,0:T(8,128)(2,1)S(1)} %get-tuple-element.68.refs_0_, bf16[256,768]{1,0:T(8,128)(2,1)} %collective-permute-done.3.refs_1_, bf16[256,768]{1,0:T(8,128)(2,1)} %collective-permute-done.4.refs_2_, bf16[256,768]{1,0:T(8,128)(2,1)} %collective-permute-done.5.refs_3_, ...), custom_call_target="tpu_custom_call" | custom-call | flops 99999997952 | bytes 10000000 | tf_op jit(solution)/shard_map/encode/pallas_call | solution.py:303
  98.5 0.9 copy-done.13
  99.5 4.4 %all-to-all-start.3 = ((bf16[8,256,512]{2,1,0:T(8,128)(2,1)}), bf16[8,256,512]{2,1,0:T(8,128)(2,1)}, u32[]{:S(2)}, u32[]{:S(2)}) async-start(bf16[8,256,512]{2,1,0:T(8,128)(2,1)} %bitcast.18), calls=%async_computation.3 | async-start | bytes 4194304 | tf_op jit(solution)/shard_map/all_to_all | solution.py:357
  103.8 2.8 add.110
  106.6 1.6 collective-permute-start.11
  108.3 3.4 %spread.5.weight_ref = bf16[1024,2048]{1,0:T(8,128)(2,1)} custom-call(s32[8]{0:T(128)S(1)} %add.99.base_ref, bf16[1088,128]{1,0:T(8,128)(2,1)S(1)} %collective-permute-done.6.refs_0_.refs_1_.refs_2_, bf16[1088,128]{1,0:T(8,128)(2,1)S(1)} %collective-permute-done.6.refs_0_.refs_1_.refs_2_, ...), custom_call_target="tpu_custom_call" | custom-call | flops 100000000 | bytes 1000000 | tf_op jit(solution)/shard_map/spread/pallas_call | solution.py:120
  111.6 5.4 %blend.5 = bf16[1024,512]{1,0:T(8,128)(2,1)S(1)} custom-call(bf16[1024,2048]{1,0:T(8,128)(2,1)} %spread.5.weight_ref, bf16[2048,512]{1,0:T(8,128)(2,1)} %bitcast.11.rows_ref), custom_call_target="tpu_custom_call" | custom-call | flops 4000000000 | bytes 10000000 | tf_op jit(solution)/shard_map/blend/pallas_call | solution.py:197
  117.0 7.2 %collective-permute-start.9 = (bf16[1024,512]{1,0:T(8,128)(2,1)S(1)}, bf16[1024,512]{1,0:T(8,128)(2,1)}, u32[]{:S(2)}, u32[]{:S(2)}) collective-permute-start(bf16[1024,512]{1,0:T(8,128)(2,1)S(1)} %blend.5), channel_id=1, source_target_pairs={{0,2},{1,3},{6,4},{7,5},{8,10},{9,11},{14,12},{15,13},{16,18},{17,... | collective-permute-start | bytes 3145736 | tf_op jit(solution)/shard_map/ppermute | solution.py:354
  124.4 7.4 %gather.7 = bf16[2048,512]{1,0:T(8,128)(2,1)} custom-call(s32[256,8]{1,0:T(8,128)S(1)} %copy.39.asked_ref, bf16[2048,512]{1,0:T(8,128)(2,1)} %rows_ref.7), custom_call_target="tpu_custom_call" | custom-call | flops 100000000 | bytes 1000000 | tf_op jit(solution)/shard_map/gather/pallas_call | solution.py:150
  131.8 3.4 %spread.6.weight_ref = bf16[1024,2048]{1,0:T(8,128)(2,1)} custom-call(s32[8]{0:T(128)S(1)} %add.99.base_ref, bf16[1088,128]{1,0:T(8,128)(2,1)S(1)} %collective-permute-done.8.refs_0_.refs_1_.refs_2_, bf16[1088,128]{1,0:T(8,128)(2,1)S(1)} %collective-permute-done.8.refs_0_.refs_1_.refs_2_, bf16[1088,128]{1,0:T(8,128)(2,1)S(1)} %collective-permute-done.8.refs_0_.refs_1_.refs_2_), custom_call_target="tpu_custom_call" | custom-call | flops 100000000 | bytes 1000000 | tf_op jit(solution)/shard_map/spread/pallas_call | solution.py:120
  135.2 4.4 %all-to-all-start.4 = ((bf16[8,256,512]{2,1,0:T(8,128)(2,1)}), bf16[8,256,512]{2,1,0:T(8,128)(2,1)}, u32[]{:S(2)}, u32[]{:S(2)}) async-start(bf16[8,256,512]{2,1,0:T(8,128)(2,1)} %bitcast.20), calls=%async_computation.4 | async-start | bytes 4194304 | tf_op jit(solution)/shard_map/all_to_all | solution.py:357
  139.6 5.5 %blend.6 = bf16[1024,512]{1,0:T(8,128)(2,1)S(1)} custom-call(bf16[1024,2048]{1,0:T(8,128)(2,1)} %spread.6.weight_ref, bf16[2048,512]{1,0:T(8,128)(2,1)} %bitcast.19.rows_ref, bf16[1024,512]{1,0:T(8,128)(2,1)} %collective-permute-done.11.rest_0_), custom_call_target="tpu_custom_call" | custom-call | flops 4000000000 | bytes 10000000 | tf_op jit(solution)/shard_map/blend/pallas_call | solution.py:197
  145.1 1.5 add.111
  146.6 0.7 collective-permute-start.13
  147.4 3.8 %collective-permute-start.12 = (bf16[1024,512]{1,0:T(8,128)(2,1)S(1)}, bf16[1024,512]{1,0:T(8,128)(2,1)S(1)}, u32[]{:S(2)}, u32[]{:S(2)}) collective-permute-start(bf16[1024,512]{1,0:T(8,128)(2,1)S(1)} %blend.6), channel_id=1, source_target_pairs={{0,2},{1,3},{2,0},{3,1},{4,6},{5,7},{6,4},{7,5},{8,10},{9,11},{10,... | collective-permute-start | bytes 3145736 | tf_op jit(solution)/shard_map/ppermute | solution.py:354
  151.2 3.3 %spread.7.weight_ref = bf16[1024,2048]{1,0:T(8,128)(2,1)} custom-call(s32[8]{0:T(128)S(1)} %add.99.base_ref, bf16[1088,128]{1,0:T(8,128)(2,1)S(1)} %pad_maximum_fusion.refs_0_.refs_1_.refs_2_, bf16[1088,128]{1,0:T(8,128)(2,1)S(1)} %pad_maximum_fusion.refs_0_.refs_1_.refs_2_, bf16[1088,128]{1,0:T(8,128)(2,1)S(1)} %pad_maximum_fusion.refs_0_.refs_1_.refs_2_), custom_call_target="tpu_custom_call" | custom-call | flops 100000000 | bytes 1000000 | tf_op jit(solution)/shard_map/spread/pallas_call | solution.py:120
  154.5 19.2 %collective-permute-done.12.rest_0_ = bf16[1024,512]{1,0:T(8,128)(2,1)S(1)} collective-permute-done((bf16[1024,512]{1,0:T(8,128)(2,1)S(1)}, bf16[1024,512]{1,0:T(8,128)(2,1)S(1)}, u32[]{:S(2)}, u32[]{:S(2)}) %collective-permute-start.12) | collective-permute-done | bytes 1048608 | tf_op jit(solution)/shard_map/ppermute | solution.py:354
  173.7 6.8 %blend.7 = (bf16[1024,512]{1,0:T(8,128)(2,1)}, bf16[1024,512]{1,0:T(8,128)(2,1)}) custom-call(s32[8]{0:T(128)S(1)} %fusion.8.place_ref, bf16[1024,2048]{1,0:T(8,128)(2,1)} %spread.7.weight_ref, bf16[2048,512]{1,0:T(8,128)(2,1)} %bitcast.21.rows_ref, bf16[1024,512]{1,0:T(8,128)(2,1)S(1)} %collective-permute-done.12.rest_0_, ...), custom_call_target="tpu_custom_call" | custom-call | flops 4000000000 | bytes 10000000 | tf_op jit(solution)/shard_map/blend/pallas_call | solution.py:197
  180.6 0.7 collective-permute-start.17
  181.3 3.3 %collective-permute-start.14 = (bf16[1024,512]{1,0:T(8,128)(2,1)}, bf16[1024,512]{1,0:T(8,128)(2,1)}, u32[]{:S(2)}, u32[]{:S(2)}) collective-permute-start(bf16[1024,512]{1,0:T(8,128)(2,1)} %get-tuple-element.93.refs_0_), channel_id=1, source_target_pairs={{0,2},{1,3},{2,0},{3,1},{4,6},{5,7},{6,4},{7,5},{8,10},{9,11},{10,... | collective-permute-start | bytes 3145736 | tf_op jit(solution)/shard_map/ppermute | solution.py:354
  184.6 4.5 %terms.7 = bf16[2048,512]{1,0:T(8,128)(2,1)S(1)} custom-call(bf16[1024,2048]{1,0:T(8,128)(2,1)} %spread.7.weight_ref, bf16[1024,512]{1,0:T(8,128)(2,1)} %get-tuple-element.93.refs_0_), custom_call_target="tpu_custom_call" | custom-call | flops 99999997952 | bytes 10000000 | tf_op jit(solution)/shard_map/terms/pallas_call | solution.py:220
  189.1 1.3 copy-done.1
  190.4 3.9 %all-to-all-start.5 = ((bf16[8,256,512]{2,1,0:T(8,128)(2,1)}), bf16[8,256,512]{2,1,0:T(8,128)(2,1)S(1)}, u32[]{:S(2)}, u32[]{:S(2)}) async-start(bf16[8,256,512]{2,1,0:T(8,128)(2,1)} %bitcast.60), calls=%async_computation.5 | async-start | bytes 4194304 | tf_op jit(solution)/shard_map/all_to_all | solution.py:357
  194.3 1.3 collective-permute-start.18
  195.6 10.9 %collective-permute-done.14.refs_0_ = bf16[1024,512]{1,0:T(8,128)(2,1)} collective-permute-done((bf16[1024,512]{1,0:T(8,128)(2,1)}, bf16[1024,512]{1,0:T(8,128)(2,1)}, u32[]{:S(2)}, u32[]{:S(2)}) %collective-permute-start.14) | collective-permute-done | bytes 1048608 | tf_op jit(solution)/shard_map/ppermute | solution.py:354
  206.5 1.7 collective-permute-start.15
  208.1 4.5 %terms.6 = bf16[2048,512]{1,0:T(8,128)(2,1)S(1)} custom-call(bf16[1024,2048]{1,0:T(8,128)(2,1)} %spread.6.weight_ref, bf16[1024,512]{1,0:T(8,128)(2,1)} %collective-permute-done.14.refs_0_), custom_call_target="tpu_custom_call" | custom-call | flops 99999997952 | bytes 10000000 | tf_op jit(solution)/shard_map/terms/pallas_call | solution.py:220
  212.6 1.3 copy-done
  213.9 7.0 %all-to-all-done.5 = bf16[8,256,512]{2,1,0:T(8,128)(2,1)S(1)} async-done(((bf16[8,256,512]{2,1,0:T(8,128)(2,1)}), bf16[8,256,512]{2,1,0:T(8,128)(2,1)S(1)}, u32[]{:S(2)}, u32[]{:S(2)}) %all-to-all-start.5) | async-done | bytes 2097184 | tf_op jit(solution)/shard_map/all_to_all | solution.py:357
  220.9 4.3 %all-to-all-start.6 = ((bf16[8,256,512]{2,1,0:T(8,128)(2,1)}), bf16[8,256,512]{2,1,0:T(8,128)(2,1)}, u32[]{:S(2)}, u32[]{:S(2)}) async-start(bf16[8,256,512]{2,1,0:T(8,128)(2,1)} %bitcast.59), calls=%async_computation.6 | async-start | bytes 4194304 | tf_op jit(solution)/shard_map/all_to_all | solution.py:357
  225.3 1.3 collective-permute-start.16
  226.6 3.4 %collective-permute-done.18.refs_1_ = bf16[1024,512]{1,0:T(8,128)(2,1)} collective-permute-done((bf16[1024,512]{1,0:T(8,128)(2,1)S(1)}, bf16[1024,512]{1,0:T(8,128)(2,1)}, u32[]{:S(2)}, u32[]{:S(2)}) %collective-permute-start.18) | collective-permute-done | bytes 1048608 | tf_op jit(solution)/shard_map/ppermute | solution.py:354
  230.0 5.5 %terms.5 = bf16[2048,512]{1,0:T(8,128)(2,1)} custom-call(bf16[1024,2048]{1,0:T(8,128)(2,1)} %spread.5.weight_ref, bf16[1024,512]{1,0:T(8,128)(2,1)S(1)} %collective-permute-done.17.refs_0_, bf16[1024,512]{1,0:T(8,128)(2,1)} %collective-permute-done.18.refs_1_), custom_call_target="tpu_custom_call" | custom-call | flops 99999997952 | bytes 10000000 | tf_op jit(solution)/shard_map/terms/pallas_call | solution.py:220
  235.5 16.4 %all-to-all-done.6 = bf16[8,256,512]{2,1,0:T(8,128)(2,1)} async-done(((bf16[8,256,512]{2,1,0:T(8,128)(2,1)}), bf16[8,256,512]{2,1,0:T(8,128)(2,1)}, u32[]{:S(2)}, u32[]{:S(2)}) %all-to-all-start.6) | async-done | bytes 2097184 | tf_op jit(solution)/shard_map/all_to_all | solution.py:357
  251.9 4.3 %all-to-all-start.7 = ((bf16[8,256,512]{2,1,0:T(8,128)(2,1)}), bf16[8,256,512]{2,1,0:T(8,128)(2,1)}, u32[]{:S(2)}, u32[]{:S(2)}) async-start(bf16[8,256,512]{2,1,0:T(8,128)(2,1)} %bitcast.69), calls=%async_computation.7 | async-start | bytes 4194304 | tf_op jit(solution)/shard_map/all_to_all | solution.py:357
  256.3 5.7 %terms.4 = bf16[2048,512]{1,0:T(8,128)(2,1)} custom-call(bf16[1024,2048]{1,0:T(8,128)(2,1)} %spread.4.weight_ref, bf16[1024,512]{1,0:T(8,128)(2,1)} %collective-permute-done.15.refs_0_, bf16[1024,512]{1,0:T(8,128)(2,1)} %collective-permute-done.16.refs_1_), custom_call_target="tpu_custom_call" | custom-call | flops 99999997952 | bytes 10000000 | tf_op jit(solution)/shard_map/terms/pallas_call | solution.py:220
  262.0 20.9 %all-to-all-done.7 = bf16[8,256,512]{2,1,0:T(8,128)(2,1)} async-done(((bf16[8,256,512]{2,1,0:T(8,128)(2,1)}), bf16[8,256,512]{2,1,0:T(8,128)(2,1)}, u32[]{:S(2)}, u32[]{:S(2)}) %all-to-all-start.7) | async-done | bytes 2097184 | tf_op jit(solution)/shard_map/all_to_all | solution.py:357
  282.9 4.6 %all-to-all-start.8 = ((bf16[8,256,512]{2,1,0:T(8,128)(2,1)}), bf16[8,256,512]{2,1,0:T(8,128)(2,1)}, u32[]{:S(2)}, u32[]{:S(2)}) async-start(bf16[8,256,512]{2,1,0:T(8,128)(2,1)} %bitcast.70), calls=%async_computation.8 | async-start | bytes 4194304 | tf_op jit(solution)/shard_map/all_to_all | solution.py:357
  287.6 16.9 %add_rows.2.refs_2_ = f32[2048,512]{1,0:T(8,128)} custom-call(s32[8,256]{1,0:T(8,128)S(1)} %reshape.74.refs_0_, s32[8,256]{1,0:T(8,128)S(1)} %reshape.73.refs_1_, s32[8,256]{1,0:T(8,128)S(1)} %reshape.72.refs_2_, bf16[2048,512]{1,0:T(8,128)(2,1)S(1)} %bitcast.58, bf16[2048,512]{1,0:T(8,128)(2,1)} %bitcast.27.refs_4_, bf16[2048,512]{1,0:T(8,128)(2,1)} %bitcast.29.refs_5_), custom_call_target="tpu_custom_call" | custom-call | flops 15000000512 | bytes 10000000 | tf_op jit(solution)/shard_map/add_rows/pallas_call | solution.py:259
  304.4 9.5 %all-to-all-done.8 = bf16[8,256,512]{2,1,0:T(8,128)(2,1)} async-done(((bf16[8,256,512]{2,1,0:T(8,128)(2,1)}), bf16[8,256,512]{2,1,0:T(8,128)(2,1)}, u32[]{:S(2)}, u32[]{:S(2)}) %all-to-all-start.8) | async-done | bytes 2097184 | tf_op jit(solution)/shard_map/all_to_all | solution.py:357
  314.0 8.3 %add_rows.3 = f32[2048,512]{1,0:T(8,128)} custom-call(s32[8,256]{1,0:T(8,128)S(1)} %copy-done.4, bf16[2048,512]{1,0:T(8,128)(2,1)} %bitcast.31.refs_1_, f32[2048,512]{1,0:T(8,128)} %add_rows.2.refs_2_), custom_call_target="tpu_custom_call" | custom-call | flops 5000000000 | bytes 10000000 | tf_op jit(solution)/shard_map/add_rows/pallas_call | solution.py:259
  (66 shorter events, 2.0 us)
Async XLA Ops:
  0.6 0.7 copy-start.6
  1.4 1.4 copy-start.14
  2.7 9.1 %copy-start.2 = (f32[8,4,32,128]{3,2,1,0:T(8,128)S(1)}, f32[8,4,32,128]{3,2,1,0:T(8,128)}, u32[]{:S(2)}) copy-start(f32[8,4,32,128]{3,2,1,0:T(8,128)} %param.25) | copy-start | bytes 1572868
  3.8 15.3 %collective-permute-start = (bf16[4,128,768]{2,1,0:T(8,128)(2,1)S(1)}, bf16[4,128,768]{2,1,0:T(8,128)(2,1)S(1)}, u32[]{:S(2)}, u32[]{:S(2)}) collective-permute-start(bf16[4,128,768]{2,1,0:T(8,128)(2,1)S(1)} %get-tuple-element.105), channel_id=1, source_target_pairs={{0,1},{1,0},{2,3},{3,2},{4,5},{5,4},{6,7},{7,6},{8,9},{9,8},{10,11... | collective-permute-start | bytes 2359304 | tf_op jit(solution)/shard_map/ppermute | solution.py:354
  4.9 14.2 %all-to-all-start = ((s32[32,1,256]{2,1,0:T(1,128)}), s32[32,1,256]{2,1,0:T(1,128)S(1)}, u32[]{:S(2)}, u32[]{:S(2)}) async-start(s32[32,1,256]{2,1,0:T(1,128)} %copy.31), calls=%async_computation | async-start | bytes 65536 | tf_op jit(solution)/shard_map/all_to_all | solution.py:366
  19.1 7.7 %copy-start.15 = (bf16[4,128,768]{2,1,0:T(8,128)(2,1)}, bf16[4,128,768]{2,1,0:T(8,128)(2,1)S(1)}, u32[]{:S(2)}) copy-start(bf16[4,128,768]{2,1,0:T(8,128)(2,1)S(1)} %collective-permute-done) | copy-start | bytes 2359300
  19.2 7.7 %copy-start.3 = (s32[8,256]{1,0:T(8,128)}, s32[8,256]{1,0:T(8,128)S(1)}, u32[]{:S(2)}) copy-start(s32[8,256]{1,0:T(8,128)S(1)} %reshape.71.refs_0_) | copy-start | bytes 24580
  26.8 33.6 %all-to-all-start.1 = ((bf16[8,256,512]{2,1,0:T(8,128)(2,1)}), bf16[8,256,512]{2,1,0:T(8,128)(2,1)S(1)}, u32[]{:S(2)}, u32[]{:S(2)}) async-start(bf16[8,256,512]{2,1,0:T(8,128)(2,1)} %bitcast.8), calls=%async_computation.1 | async-start | bytes 4194304 | tf_op jit(solution)/shard_map/all_to_all | solution.py:357
  30.4 26.6 %collective-permute-start.2 = (bf16[1088,128]{1,0:T(8,128)(2,1)S(1)}, bf16[1088,128]{1,0:T(8,128)(2,1)S(1)}, u32[]{:S(2)}, u32[]{:S(2)}) collective-permute-start(bf16[1088,128]{1,0:T(8,128)(2,1)S(1)} %pad_maximum_fusion.refs_0_.refs_1_.refs_2_), channel_id=1, source_target_pairs={{0,4},{1,5},{6,2},{7,3},{8,12},{9,13},{14,10},{15,11},{16,20},{17,... | collective-permute-start | bytes 835592 | tf_op jit(solution)/shard_map/ppermute | solution.py:354
  32.8 24.2 %collective-permute-start.1 = (bf16[1088,128]{1,0:T(8,128)(2,1)S(1)}, bf16[1088,128]{1,0:T(8,128)(2,1)S(1)}, u32[]{:S(2)}, u32[]{:S(2)}) collective-permute-start(bf16[1088,128]{1,0:T(8,128)(2,1)S(1)} %pad_maximum_fusion.refs_0_.refs_1_.refs_2_), channel_id=1, source_target_pairs={{0,6},{1,7},{6,0},{7,1},{8,14},{9,15},{14,8},{15,9},{16,22},{17,23... | collective-permute-start | bytes 835592 | tf_op jit(solution)/shard_map/ppermute | solution.py:354
  39.9 34.9 %collective-permute-start.5 = (bf16[256,768]{1,0:T(8,128)(2,1)}, bf16[256,768]{1,0:T(8,128)(2,1)}, u32[]{:S(2)}, u32[]{:S(2)}) collective-permute-start(bf16[256,768]{1,0:T(8,128)(2,1)} %get-tuple-element.100), channel_id=1, source_target_pairs={{0,6},{1,7},{2,0},{3,1},{4,2},{5,3},{6,4},{7,5},{8,14},{9,15},{10,... | collective-permute-start | bytes 1179656 | tf_op jit(solution)/shard_map/ppermute | solution.py:354
  41.3 34.8 %collective-permute-start.3 = (bf16[256,768]{1,0:T(8,128)(2,1)}, bf16[256,768]{1,0:T(8,128)(2,1)}, u32[]{:S(2)}, u32[]{:S(2)}) collective-permute-start(bf16[256,768]{1,0:T(8,128)(2,1)} %get-tuple-element.102), channel_id=1, source_target_pairs={{0,2},{1,3},{2,4},{3,5},{4,6},{5,7},{6,0},{7,1},{8,10},{9,11},{10,... | collective-permute-start | bytes 1179656 | tf_op jit(solution)/shard_map/ppermute | solution.py:354
  41.9 40.0 %collective-permute-start.4 = (bf16[256,768]{1,0:T(8,128)(2,1)}, bf16[256,768]{1,0:T(8,128)(2,1)}, u32[]{:S(2)}, u32[]{:S(2)}) collective-permute-start(bf16[256,768]{1,0:T(8,128)(2,1)} %get-tuple-element.103), channel_id=1, source_target_pairs={{0,4},{1,5},{2,6},{3,7},{4,0},{5,1},{6,2},{7,3},{8,12},{9,13},{10,... | collective-permute-start | bytes 1179656 | tf_op jit(solution)/shard_map/ppermute | solution.py:354
  60.4 38.1 %collective-permute-start.8 = (bf16[1088,128]{1,0:T(8,128)(2,1)S(1)}, bf16[1088,128]{1,0:T(8,128)(2,1)S(1)}, u32[]{:S(2)}, u32[]{:S(2)}) collective-permute-start(bf16[1088,128]{1,0:T(8,128)(2,1)S(1)} %pad_maximum_fusion.refs_0_.refs_1_.refs_2_), channel_id=1, source_target_pairs={{0,2},{1,3},{2,0},{3,1},{4,6},{5,7},{6,4},{7,5},{8,10},{9,11},{10,... | collective-permute-start | bytes 835592 | tf_op jit(solution)/shard_map/ppermute | solution.py:354
  64.2 34.3 %collective-permute-start.7 = (bf16[1088,128]{1,0:T(8,128)(2,1)S(1)}, bf16[1088,128]{1,0:T(8,128)(2,1)S(1)}, u32[]{:S(2)}, u32[]{:S(2)}) collective-permute-start(bf16[1088,128]{1,0:T(8,128)(2,1)S(1)} %pad_maximum_fusion.refs_0_.refs_1_.refs_2_), channel_id=1, source_target_pairs={{2,4},{3,5},{4,2},{5,3},{10,12},{11,13},{12,10},{13,11},{18,20},{1... | collective-permute-start | bytes 835592 | tf_op jit(solution)/shard_map/ppermute | solution.py:354
  64.9 33.6 %all-to-all-start.2 = ((bf16[8,256,512]{2,1,0:T(8,128)(2,1)}), bf16[8,256,512]{2,1,0:T(8,128)(2,1)}, u32[]{:S(2)}, u32[]{:S(2)}) async-start(bf16[8,256,512]{2,1,0:T(8,128)(2,1)} %bitcast.10), calls=%async_computation.2 | async-start | bytes 4194304 | tf_op jit(solution)/shard_map/all_to_all | solution.py:357
  69.2 12.7 %copy-start.5 = (bf16[768,512]{1,0:T(8,128)(2,1)S(1)}, bf16[768,512]{1,0:T(8,128)(2,1)}, u32[]{:S(2)}) copy-start(bf16[768,512]{1,0:T(8,128)(2,1)} %refs_12_.1) | copy-start | bytes 2359300
  69.3 12.7 %copy-start.7 = (f32[3072]{0:T(1024)S(1)}, f32[3072]{0:T(1024)}, u32[]{:S(2)}) copy-start(f32[3072]{0:T(1024)} %refs_7_.1) | copy-start | bytes 36868
  69.3 12.7 %copy-start.8 = (f32[768]{0:T(1024)S(1)}, f32[768]{0:T(1024)}, u32[]{:S(2)}) copy-start(f32[768]{0:T(1024)} %refs_4_.1) | copy-start | bytes 9220
  69.3 12.7 %copy-start.9 = (f32[768]{0:T(1024)S(1)}, f32[768]{0:T(1024)}, u32[]{:S(2)}) copy-start(f32[768]{0:T(1024)} %refs_5_.1) | copy-start | bytes 9220
  69.3 12.7 %copy-start.10 = (f32[768]{0:T(1024)S(1)}, f32[768]{0:T(1024)}, u32[]{:S(2)}) copy-start(f32[768]{0:T(1024)} %refs_9_.1) | copy-start | bytes 9220
  69.3 12.7 %copy-start.11 = (f32[768]{0:T(1024)S(1)}, f32[768]{0:T(1024)}, u32[]{:S(2)}) copy-start(f32[768]{0:T(1024)} %refs_10_.1) | copy-start | bytes 9220
  69.3 12.7 %copy-start.12 = (f32[768]{0:T(1024)S(1)}, f32[768]{0:T(1024)}, u32[]{:S(2)}) copy-start(f32[768]{0:T(1024)} %refs_11_.1) | copy-start | bytes 9220
  74.9 23.6 %collective-permute-start.6 = (bf16[1088,128]{1,0:T(8,128)(2,1)S(1)}, bf16[1088,128]{1,0:T(8,128)(2,1)S(1)}, u32[]{:S(2)}, u32[]{:S(2)}) collective-permute-start(bf16[1088,128]{1,0:T(8,128)(2,1)S(1)} %pad_maximum_fusion.refs_0_.refs_1_.refs_2_), channel_id=1, source_target_pairs={{2,6},{3,7},{4,0},{5,1},{10,14},{11,15},{12,8},{13,9},{18,22},{19,... | collective-permute-start | bytes 835592 | tf_op jit(solution)/shard_map/ppermute | solution.py:354
  76.2 27.7 %collective-permute-start.10 = (bf16[1024,512]{1,0:T(8,128)(2,1)}, bf16[1024,512]{1,0:T(8,128)(2,1)}, u32[]{:S(2)}, u32[]{:S(2)}) collective-permute-start(bf16[1024,512]{1,0:T(8,128)(2,1)} %blend.4), channel_id=1, source_target_pairs={{0,2},{1,3},{6,4},{7,5},{8,10},{9,11},{14,12},{15,13},{16,18},{17,... | collective-permute-start | bytes 3145736 | tf_op jit(solution)/shard_map/ppermute | solution.py:354
  98.5 1.0 copy-start.13
  99.5 35.8 %all-to-all-start.3 = ((bf16[8,256,512]{2,1,0:T(8,128)(2,1)}), bf16[8,256,512]{2,1,0:T(8,128)(2,1)}, u32[]{:S(2)}, u32[]{:S(2)}) async-start(bf16[8,256,512]{2,1,0:T(8,128)(2,1)} %bitcast.18), calls=%async_computation.3 | async-start | bytes 4194304 | tf_op jit(solution)/shard_map/all_to_all | solution.py:357
  106.6 28.6 %collective-permute-start.11 = (bf16[1024,512]{1,0:T(8,128)(2,1)}, bf16[1024,512]{1,0:T(8,128)(2,1)}, u32[]{:S(2)}, u32[]{:S(2)}) collective-permute-start(bf16[1024,512]{1,0:T(8,128)(2,1)} %add.110), channel_id=1, source_target_pairs={{2,4},{3,5},{4,2},{5,3},{10,12},{11,13},{12,10},{13,11},{18,20},{1... | collective-permute-start | bytes 3145736 | tf_op jit(solution)/shard_map/ppermute | solution.py:354
  117.0 28.1 %collective-permute-start.9 = (bf16[1024,512]{1,0:T(8,128)(2,1)S(1)}, bf16[1024,512]{1,0:T(8,128)(2,1)}, u32[]{:S(2)}, u32[]{:S(2)}) collective-permute-start(bf16[1024,512]{1,0:T(8,128)(2,1)S(1)} %blend.5), channel_id=1, source_target_pairs={{0,2},{1,3},{6,4},{7,5},{8,10},{9,11},{14,12},{15,13},{16,18},{17,... | collective-permute-start | bytes 3145736 | tf_op jit(solution)/shard_map/ppermute | solution.py:354
  135.2 38.5 %all-to-all-start.4 = ((bf16[8,256,512]{2,1,0:T(8,128)(2,1)}), bf16[8,256,512]{2,1,0:T(8,128)(2,1)}, u32[]{:S(2)}, u32[]{:S(2)}) async-start(bf16[8,256,512]{2,1,0:T(8,128)(2,1)} %bitcast.20), calls=%async_computation.4 | async-start | bytes 4194304 | tf_op jit(solution)/shard_map/all_to_all | solution.py:357
  146.6 7.9 %collective-permute-start.13 = (bf16[1024,512]{1,0:T(8,128)(2,1)S(1)}, bf16[1024,512]{1,0:T(8,128)(2,1)S(1)}, u32[]{:S(2)}, u32[]{:S(2)}) collective-permute-start(bf16[1024,512]{1,0:T(8,128)(2,1)S(1)} %add.111), channel_id=1, source_target_pairs={{2,4},{3,5},{4,2},{5,3},{10,12},{11,13},{12,10},{13,11},{18,20},{1... | collective-permute-start | bytes 3145736 | tf_op jit(solution)/shard_map/ppermute | solution.py:354
  147.4 26.4 %collective-permute-start.12 = (bf16[1024,512]{1,0:T(8,128)(2,1)S(1)}, bf16[1024,512]{1,0:T(8,128)(2,1)S(1)}, u32[]{:S(2)}, u32[]{:S(2)}) collective-permute-start(bf16[1024,512]{1,0:T(8,128)(2,1)S(1)} %blend.6), channel_id=1, source_target_pairs={{0,2},{1,3},{2,0},{3,1},{4,6},{5,7},{6,4},{7,5},{8,10},{9,11},{10,... | collective-permute-start | bytes 3145736 | tf_op jit(solution)/shard_map/ppermute | solution.py:354
  180.6 13.7 %collective-permute-start.17 = (bf16[1024,512]{1,0:T(8,128)(2,1)}, bf16[1024,512]{1,0:T(8,128)(2,1)S(1)}, u32[]{:S(2)}, u32[]{:S(2)}) collective-permute-start(bf16[1024,512]{1,0:T(8,128)(2,1)} %get-tuple-element.93.refs_0_), channel_id=1, source_target_pairs={{2,4},{3,5},{4,2},{5,3},{10,12},{11,13},{12,10},{13,11},{18,20},{1... | collective-permute-start | bytes 3145736 | tf_op jit(solution)/shard_map/ppermute | solution.py:354
  181.3 25.1 %collective-permute-start.14 = (bf16[1024,512]{1,0:T(8,128)(2,1)}, bf16[1024,512]{1,0:T(8,128)(2,1)}, u32[]{:S(2)}, u32[]{:S(2)}) collective-permute-start(bf16[1024,512]{1,0:T(8,128)(2,1)} %get-tuple-element.93.refs_0_), channel_id=1, source_target_pairs={{0,2},{1,3},{2,0},{3,1},{4,6},{5,7},{6,4},{7,5},{8,10},{9,11},{10,... | collective-permute-start | bytes 3145736 | tf_op jit(solution)/shard_map/ppermute | solution.py:354
  189.1 1.3 copy-start.1
  190.4 30.5 %all-to-all-start.5 = ((bf16[8,256,512]{2,1,0:T(8,128)(2,1)}), bf16[8,256,512]{2,1,0:T(8,128)(2,1)S(1)}, u32[]{:S(2)}, u32[]{:S(2)}) async-start(bf16[8,256,512]{2,1,0:T(8,128)(2,1)} %bitcast.60), calls=%async_computation.5 | async-start | bytes 4194304 | tf_op jit(solution)/shard_map/all_to_all | solution.py:357
  194.3 35.7 %collective-permute-start.18 = (bf16[1024,512]{1,0:T(8,128)(2,1)S(1)}, bf16[1024,512]{1,0:T(8,128)(2,1)}, u32[]{:S(2)}, u32[]{:S(2)}) collective-permute-start(bf16[1024,512]{1,0:T(8,128)(2,1)S(1)} %collective-permute-done.17.refs_0_), channel_id=1, source_target_pairs={{2,0},{3,1},{4,6},{5,7},{10,8},{11,9},{12,14},{13,15},{18,16},{19,... | collective-permute-start | bytes 3145736 | tf_op jit(solution)/shard_map/ppermute | solution.py:354
  206.5 18.8 %collective-permute-start.15 = (bf16[1024,512]{1,0:T(8,128)(2,1)}, bf16[1024,512]{1,0:T(8,128)(2,1)}, u32[]{:S(2)}, u32[]{:S(2)}) collective-permute-start(bf16[1024,512]{1,0:T(8,128)(2,1)} %collective-permute-done.14.refs_0_), channel_id=1, source_target_pairs={{2,4},{3,5},{4,2},{5,3},{10,12},{11,13},{12,10},{13,11},{18,20},{1... | collective-permute-start | bytes 3145736 | tf_op jit(solution)/shard_map/ppermute | solution.py:354
  212.6 1.3 copy-start
  220.9 31.0 %all-to-all-start.6 = ((bf16[8,256,512]{2,1,0:T(8,128)(2,1)}), bf16[8,256,512]{2,1,0:T(8,128)(2,1)}, u32[]{:S(2)}, u32[]{:S(2)}) async-start(bf16[8,256,512]{2,1,0:T(8,128)(2,1)} %bitcast.59), calls=%async_computation.6 | async-start | bytes 4194304 | tf_op jit(solution)/shard_map/all_to_all | solution.py:357
  225.3 31.0 %collective-permute-start.16 = (bf16[1024,512]{1,0:T(8,128)(2,1)}, bf16[1024,512]{1,0:T(8,128)(2,1)}, u32[]{:S(2)}, u32[]{:S(2)}) collective-permute-start(bf16[1024,512]{1,0:T(8,128)(2,1)} %collective-permute-done.15.refs_0_), channel_id=1, source_target_pairs={{2,0},{3,1},{4,6},{5,7},{10,8},{11,9},{12,14},{13,15},{18,16},{19,... | collective-permute-start | bytes 3145736 | tf_op jit(solution)/shard_map/ppermute | solution.py:354
  251.9 31.0 %all-to-all-start.7 = ((bf16[8,256,512]{2,1,0:T(8,128)(2,1)}), bf16[8,256,512]{2,1,0:T(8,128)(2,1)}, u32[]{:S(2)}, u32[]{:S(2)}) async-start(bf16[8,256,512]{2,1,0:T(8,128)(2,1)} %bitcast.69), calls=%async_computation.7 | async-start | bytes 4194304 | tf_op jit(solution)/shard_map/all_to_all | solution.py:357
  282.9 31.0 %all-to-all-start.8 = ((bf16[8,256,512]{2,1,0:T(8,128)(2,1)}), bf16[8,256,512]{2,1,0:T(8,128)(2,1)}, u32[]{:S(2)}, u32[]{:S(2)}) async-start(bf16[8,256,512]{2,1,0:T(8,128)(2,1)} %bitcast.70), calls=%async_computation.8 | async-start | bytes 4194304 | tf_op jit(solution)/shard_map/all_to_all | solution.py:357
  287.6 26.4 %copy-start.4 = (s32[8,256]{1,0:T(8,128)S(1)}, s32[8,256]{1,0:T(8,128)}, u32[]{:S(2)}) copy-start(s32[8,256]{1,0:T(8,128)} %copy-done.3) | copy-start | bytes 24580
where the time goes:
time: 324 us; the launch traced here: 322 us
  Pallas kernels  130 us (40%)
  waiting for transfers between devices  95 us (29%)
  starting transfers between devices  82.1 us (25%)
  other arithmetic  6.98 us (2%)
  local copies, waits for them, and re-layouts  6.67 us (2%)
    all_to_all x8, waiting for transfers between devices, exchange(): lax.all_to_all(x, both, split_axis=0, concat_axis=0, axis_index_groups=gr...  53.9 us
    ppermute x19, starting transfers between devices, move(): return lax.ppermute(x, 'tile', pairs)  41.3 us
    ppermute x19, waiting for transfers between devices, move(): return lax.ppermute(x, 'tile', pairs)  34.6 us
    all_to_all x8, starting transfers between devices, exchange(): lax.all_to_all(x, both, split_axis=0, concat_axis=0, axis_index_groups=gr...  33.9 us
    pallas_call x4, Pallas kernels, gather(): pl.pallas_call(functools.partial(gather_kernel, group, cap), grid=(near /...  29.7 us
    pallas_call x2, Pallas kernels, add_rows(): pl.pallas_call(functools.partial(add_rows_kernel, count), grid=(held // b...  25.2 us
    pallas_call x4, Pallas kernels, blend(): pl.pallas_call(functools.partial(last_blend_kernel if last else blend_ker...  23.3 us
    pallas_call x4, Pallas kernels, terms(): pl.pallas_call(terms_kernel, grid=(slots // block,), in_specs=[pl.BlockSp...  20.2 us
  transfers between devices with their start and end apart: 28, of which 9 were waited for; matrix products, arithmetic and copies ran while one was open for 3% of the time, Pallas kernels for 33%

commit v1 on v0

--- a/solution.py
+++ b/solution.py
@@ -143,7 +143,7 @@
     out_ref[...] = jnp.dot(pick, rows_ref[...], preferred_element_type=F32).astype(BF16)
 
 
-def gather(asked, rows):
+def gather(asked, rows, flops=10**8):
     near, cap = asked.shape
     held, feat = rows.shape
     group = max(1, min(near, 1024 // cap))
@@ -154,7 +154,7 @@
         out_specs=pl.BlockSpec((group * cap, feat), lambda i: (i, 0)),
         out_shape=jax.ShapeDtypeStruct((near * cap, feat), BF16),
         compiler_params=params(),
-        cost_estimate=pl.CostEstimate(flops=10**8, bytes_accessed=10**6, transcendentals=0),
+        cost_estimate=pl.CostEstimate(flops=flops, bytes_accessed=10**6, transcendentals=0),
         name="gather",
     )(asked.T, rows)
 
@@ -304,7 +304,7 @@
         functools.partial(encode_kernel, len(strips)),
         out_shape=jax.ShapeDtypeStruct((len(strips), cells, weights_and_biases[-1].shape[1]), BF16),
         compiler_params=params(),
-        cost_estimate=pl.CostEstimate(flops=10**11, bytes_accessed=10**7, transcendentals=0),
+        cost_estimate=pl.CostEstimate(flops=15 * 10**9, bytes_accessed=10**7, transcendentals=0),
         name="encode",
     )(*strips, *weights_and_biases)
 
@@ -395,10 +395,10 @@
     looked, lists[1] = tie(gather(lists[0], gauss_rows), lists[1])
     rows_1 = exchange(looked)
     looked_2 = gather(lists[1], gauss_rows)
-    looked_2, lists[2] = tie(looked_2, lists[2])
     spread_1 = spread_of(far_to_outer, far_to_inner)
-    looked_3 = gather(lists[2], gauss_rows)
-    looked_2, looked_3, spread_1, rows_1, packed = tie(looked_2, looked_3, spread_1, rows_1, packed)
+    looked_2, spread_1, rows_1, packed, lists[2], *strips[1::2] = tie(
+        looked_2, spread_1, rows_1, packed, lists[2], *strips[1::2]
+    )
 
     rows_2 = exchange(looked_2)
     part_1 = blend(spread_1, rows_1)
@@ -406,17 +406,15 @@
     near_to_outer = move(packed, moves((1, 3), (2, 0)))
     near_to_inner = move(packed, middle)
     from_beside = move(packed, beside)
-    part_1, *strips = tie(part_1, *strips)
-    target = encode(
-        strips, norm_gain, norm_bias, up_weight, up_bias, down_weight, down_bias, final_gain, final_bias, head_weight
-    )
-    looked_3, rows_2, part_1, target, lists[3], near_to_outer, near_to_inner, from_beside = tie(
-        looked_3, rows_2, part_1, target, lists[3], near_to_outer, near_to_inner, from_beside
+    part_1, lists[2], *strips = tie(part_1, lists[2], *strips)
+    looked_3 = gather(lists[2], gauss_rows, 15 * 10**9)
+    spread_2 = spread_of(near_to_outer, near_to_inner)
+    looked_3, rows_2, part_1, lists[3], spread_2, from_beside = tie(
+        looked_3, rows_2, part_1, lists[3], spread_2, from_beside
     )
 
     rows_3 = exchange(looked_3)
     far = move(part_1 + moved_1, middle)
-    spread_2 = spread_of(near_to_outer, near_to_inner)
     part_2 = blend(spread_2, rows_2)
     moved_2 = move(part_2, inwards)
     part_2, lists[3], from_beside = tie(part_2, lists[3], from_beside)
@@ -427,10 +425,15 @@
     rows_4 = exchange(looked_4)
     part_3 = blend(spread_3, rows_3, (far,))
     beside_part = move(part_3, beside)
-    part_2, moved_2, part_3, packed = tie(part_2, moved_2, part_3, packed)
+    part_2, moved_2, part_3, packed, *strips = tie(part_2, moved_2, part_3, packed, *strips)
     middle_part = move(part_2 + moved_2, middle)
     spread_4 = spread_of(packed)
-    color, diff = blend(spread_4, rows_4, (beside_part, middle_part), place, target.reshape(n_tile, -1, feat))
+    target = encode(
+        strips, norm_gain, norm_bias, up_weight, up_bias, down_weight, down_bias, final_gain, final_bias, head_weight
+    )
+    color, diff = blend(
+        spread_4, rows_4, (beside_part, middle_part), place, target.reshape(n_tile, -1, feat)
+    )
     spreads = (spread_1, spread_2, spread_3, spread_4)
 
     diff_beside = move(diff, beside)

time: 324 us -> 331 us (1.022)
  waiting for transfers between devices: 95 us -> 101 us
    ppermute x19, waiting for transfers between devices: 34.6 us -> 46.4 us  [move(): return lax.ppermute(x, 'tile', pairs)]
    all_to_all x8, waiting for transfers between devices: 53.9 us -> 48 us  [exchange(): lax.all_to_all(x, both, split_axis=0, concat_axis=0, axis_index_groups=gr...]
  transfers between devices with their start and end apart: 28 -> 28, of which waited for: 9 -> 14; matrix products, arithmetic and copies ran while one was open for 3% -> 2% of each run, Pallas kernels for 33% -> 32%
where the time goes in v1:
time: 331 us; the launch traced here: 329 us
  Pallas kernels  131 us (40%)
  waiting for transfers between devices  101 us (31%)
  starting transfers between devices  83.5 us (25%)
  local copies, waits for them, and re-layouts  6.74 us (2%)
  other arithmetic  5.9 us (2%)
    all_to_all x8, waiting for transfers between devices, exchange(): lax.all_to_all(x, both, split_axis=0, concat_axis=0, axis_index_groups=gr...  48 us
    ppermute x19, waiting for transfers between devices, move(): return lax.ppermute(x, 'tile', pairs)  46.4 us
    ppermute x19, starting transfers between devices, move(): return lax.ppermute(x, 'tile', pairs)  42.8 us
    all_to_all x8, starting transfers between devices, exchange(): lax.all_to_all(x, both, split_axis=0, concat_axis=0, axis_index_groups=gr...  33.8 us
    pallas_call x4, Pallas kernels, gather(): pl.pallas_call(functools.partial(gather_kernel, group, cap), grid=(near /...  29.7 us
    pallas_call x2, Pallas kernels, add_rows(): pl.pallas_call(functools.partial(add_rows_kernel, count), grid=(held // b...  25.2 us
    pallas_call x4, Pallas kernels, blend(): pl.pallas_call(functools.partial(last_blend_kernel if last else blend_ker...  23.5 us
    pallas_call x4, Pallas kernels, terms(): pl.pallas_call(terms_kernel, grid=(slots // block,), in_specs=[pl.BlockSp...  20.5 us
  transfers between devices with their start and end apart: 28, of which 14 were waited for; matrix products, arithmetic and copies ran while one was open for 2% of the time, Pallas kernels for 32%

profile of v1, /device:TPU:0, one launch (start us, length us, event | category | flops | bytes accessed | tf_op | source)
XLA Modules:
  0.0 329.2 jit_solution(17503745018091018009)
XLA Ops:
  1.4 1.3 index.1
  2.8 1.0 dynamic-slice_bitcast_fusion
  4.9 7.0 %all-to-all-start = ((s32[32,1,256]{2,1,0:T(1,128)}), s32[32,1,256]{2,1,0:T(1,128)S(1)}, u32[]{:S(2)}, u32[]{:S(2)}) async-start(s32[32,1,256]{2,1,0:T(1,128)} %copy.31), calls=%async_computation | async-start | bytes 65536 | tf_op jit(solution)/shard_map/all_to_all | solution.py:366
  12.6 6.5 %all-to-all-done = s32[32,1,256]{2,1,0:T(1,128)S(1)} async-done(((s32[32,1,256]{2,1,0:T(1,128)}), s32[32,1,256]{2,1,0:T(1,128)S(1)}, u32[]{:S(2)}, u32[]{:S(2)}) %all-to-all-start) | async-done | bytes 32800 | tf_op jit(solution)/shard_map/all_to_all | solution.py:366
  19.3 7.4 %gather.4 = bf16[2048,512]{1,0:T(8,128)(2,1)} custom-call(s32[256,8]{1,0:T(8,128)S(1)} %copy.33.asked_ref, bf16[2048,512]{1,0:T(8,128)(2,1)} %rows_ref.7), custom_call_target="tpu_custom_call" | custom-call | flops 100000000 | bytes 1000000 | tf_op jit(solution)/shard_map/gather/pallas_call | solution.py:150
  26.7 3.6 %all-to-all-start.1 = ((bf16[8,256,512]{2,1,0:T(8,128)(2,1)}), bf16[8,256,512]{2,1,0:T(8,128)(2,1)S(1)}, u32[]{:S(2)}, u32[]{:S(2)}) async-start(bf16[8,256,512]{2,1,0:T(8,128)(2,1)} %bitcast.7), calls=%async_computation.1 | async-start | bytes 4194304 | tf_op jit(solution)/shard_map/all_to_all | solution.py:357
  30.4 2.4 fusion.1
  33.3 3.3 %collective-permute-start.4 = (bf16[256,768]{1,0:T(8,128)(2,1)}, bf16[256,768]{1,0:T(8,128)(2,1)}, u32[]{:S(2)}, u32[]{:S(2)}) collective-permute-start(bf16[256,768]{1,0:T(8,128)(2,1)} %get-tuple-element.108), channel_id=1, source_target_pairs={{0,6},{1,7},{2,0},{3,1},{4,2},{5,3},{6,4},{7,5},{8,14},{9,15},{10,... | collective-permute-start | bytes 1179656 | tf_op jit(solution)/shard_map/ppermute | solution.py:354
  36.7 1.3 collective-permute-start.2
  38.0 3.6 %collective-permute-start.1 = (bf16[1088,128]{1,0:T(8,128)(2,1)S(1)}, bf16[1088,128]{1,0:T(8,128)(2,1)S(1)}, u32[]{:S(2)}, u32[]{:S(2)}) collective-permute-start(bf16[1088,128]{1,0:T(8,128)(2,1)S(1)} %pad_maximum_fusion.refs_0_.refs_1_.refs_2_), channel_id=1, source_target_pairs={{0,6},{1,7},{6,0},{7,1},{8,14},{9,15},{14,8},{15,9},{16,22},{17,23... | collective-permute-start | bytes 835592 | tf_op jit(solution)/shard_map/ppermute | solution.py:354
  41.9 7.5 %gather.5 = bf16[2048,512]{1,0:T(8,128)(2,1)} custom-call(s32[256,8]{1,0:T(8,128)S(1)} %copy.35.asked_ref, bf16[2048,512]{1,0:T(8,128)(2,1)} %rows_ref.7), custom_call_target="tpu_custom_call" | custom-call | flops 100000000 | bytes 1000000 | tf_op jit(solution)/shard_map/gather/pallas_call | solution.py:150
  49.4 8.0 %collective-permute-done.2.refs_3_.refs_4_.refs_5_ = bf16[1088,128]{1,0:T(8,128)(2,1)S(1)} collective-permute-done((bf16[1088,128]{1,0:T(8,128)(2,1)S(1)}, bf16[1088,128]{1,0:T(8,128)(2,1)S(1)}, u32[]{:S(2)}, u32[]{:S(2)}) %collective-permute-start.2) | collective-permute-done | bytes 278560 | tf_op jit(solution)/shard_map/ppermute | solution.py:354
  57.4 9.2 %collective-permute-done.1.refs_0_.refs_1_.refs_2_ = bf16[1088,128]{1,0:T(8,128)(2,1)S(1)} collective-permute-done((bf16[1088,128]{1,0:T(8,128)(2,1)S(1)}, bf16[1088,128]{1,0:T(8,128)(2,1)S(1)}, u32[]{:S(2)}, u32[]{:S(2)}) %collective-permute-start.1) | collective-permute-done | bytes 278560 | tf_op jit(solution)/shard_map/ppermute | solution.py:354
  66.6 3.4 %spread.4.weight_ref = bf16[1024,2048]{1,0:T(8,128)(2,1)} custom-call(s32[8]{0:T(128)S(1)} %add.99.base_ref, bf16[1088,128]{1,0:T(8,128)(2,1)S(1)} %collective-permute-done.1.refs_0_.refs_1_.refs_2_, bf16[1088,128]{1,0:T(8,128)(2,1)S(1)} %collective-permute-done.1.refs_0_.refs_1_.refs_2_, ...), custom_call_target="tpu_custom_call" | custom-call | flops 100000000 | bytes 1000000 | tf_op jit(solution)/shard_map/spread/pallas_call | solution.py:120
  70.0 4.4 %all-to-all-start.2 = ((bf16[8,256,512]{2,1,0:T(8,128)(2,1)}), bf16[8,256,512]{2,1,0:T(8,128)(2,1)}, u32[]{:S(2)}, u32[]{:S(2)}) async-start(bf16[8,256,512]{2,1,0:T(8,128)(2,1)} %bitcast.15), calls=%async_computation.2 | async-start | bytes 4194304 | tf_op jit(solution)/shard_map/all_to_all | solution.py:357
  74.5 1.0 collective-permute-start.8
  76.2 1.3 collective-permute-start.6
  77.5 5.5 %blend.4 = bf16[1024,512]{1,0:T(8,128)(2,1)} custom-call(bf16[1024,2048]{1,0:T(8,128)(2,1)} %spread.4.weight_ref, bf16[2048,512]{1,0:T(8,128)(2,1)S(1)} %bitcast.57), custom_call_target="tpu_custom_call" | custom-call | flops 4000000000 | bytes 10000000 | tf_op jit(solution)/shard_map/blend/pallas_call | solution.py:197
  83.0 7.4 %collective-permute-start.10 = (bf16[1024,512]{1,0:T(8,128)(2,1)}, bf16[1024,512]{1,0:T(8,128)(2,1)}, u32[]{:S(2)}, u32[]{:S(2)}) collective-permute-start(bf16[1024,512]{1,0:T(8,128)(2,1)} %blend.4), channel_id=1, source_target_pairs={{0,2},{1,3},{6,4},{7,5},{8,10},{9,11},{14,12},{15,13},{16,18},{17,... | collective-permute-start | bytes 3145736 | tf_op jit(solution)/shard_map/ppermute | solution.py:354
  90.4 2.9 collective-permute-done.5.refs_2_
  93.5 7.4 %gather.6 = bf16[2048,512]{1,0:T(8,128)(2,1)} custom-call(s32[256,8]{1,0:T(8,128)S(1)} %copy.37.asked_ref, bf16[2048,512]{1,0:T(8,128)(2,1)} %rows_ref.7), custom_call_target="tpu_custom_call" | custom-call | flops 15000000512 | bytes 1000000 | tf_op jit(solution)/shard_map/gather/pallas_call | solution.py:150
  100.9 4.2 %collective-permute-done.6.refs_0_.refs_1_.refs_2_ = bf16[1088,128]{1,0:T(8,128)(2,1)S(1)} collective-permute-done((bf16[1088,128]{1,0:T(8,128)(2,1)S(1)}, bf16[1088,128]{1,0:T(8,128)(2,1)S(1)}, u32[]{:S(2)}, u32[]{:S(2)}) %collective-permute-start.6) | collective-permute-done | bytes 278560 | tf_op jit(solution)/shard_map/ppermute | solution.py:354
  105.1 3.4 %spread.5.weight_ref = bf16[1024,2048]{1,0:T(8,128)(2,1)} custom-call(s32[8]{0:T(128)S(1)} %add.99.base_ref, bf16[1088,128]{1,0:T(8,128)(2,1)S(1)} %collective-permute-done.6.refs_0_.refs_1_.refs_2_, bf16[1088,128]{1,0:T(8,128)(2,1)S(1)} %collective-permute-done.6.refs_0_.refs_1_.refs_2_, ...), custom_call_target="tpu_custom_call" | custom-call | flops 100000000 | bytes 1000000 | tf_op jit(solution)/shard_map/spread/pallas_call | solution.py:120
  108.5 4.4 %all-to-all-start.3 = ((bf16[8,256,512]{2,1,0:T(8,128)(2,1)}), bf16[8,256,512]{2,1,0:T(8,128)(2,1)}, u32[]{:S(2)}, u32[]{:S(2)}) async-start(bf16[8,256,512]{2,1,0:T(8,128)(2,1)} %bitcast.18), calls=%async_computation.3 | async-start | bytes 4194304 | tf_op jit(solution)/shard_map/all_to_all | solution.py:357
  112.9 1.8 add.110
  114.7 1.6 collective-permute-start.11
  116.3 5.4 %blend.5 = bf16[1024,512]{1,0:T(8,128)(2,1)S(1)} custom-call(bf16[1024,2048]{1,0:T(8,128)(2,1)} %spread.5.weight_ref, bf16[2048,512]{1,0:T(8,128)(2,1)} %bitcast.16.rows_ref), custom_call_target="tpu_custom_call" | custom-call | flops 4000000000 | bytes 10000000 | tf_op jit(solution)/shard_map/blend/pallas_call | solution.py:197
  121.7 5.2 %collective-permute-start.9 = (bf16[1024,512]{1,0:T(8,128)(2,1)S(1)}, bf16[1024,512]{1,0:T(8,128)(2,1)}, u32[]{:S(2)}, u32[]{:S(2)}) collective-permute-start(bf16[1024,512]{1,0:T(8,128)(2,1)S(1)} %blend.5), channel_id=1, source_target_pairs={{0,2},{1,3},{6,4},{7,5},{8,10},{9,11},{14,12},{15,13},{16,18},{17,... | collective-permute-start | bytes 3145736 | tf_op jit(solution)/shard_map/ppermute | solution.py:354
  127.0 7.4 %gather.7 = bf16[2048,512]{1,0:T(8,128)(2,1)} custom-call(s32[256,8]{1,0:T(8,128)S(1)} %copy.39.asked_ref, bf16[2048,512]{1,0:T(8,128)(2,1)} %rows_ref.7), custom_call_target="tpu_custom_call" | custom-call | flops 100000000 | bytes 1000000 | tf_op jit(solution)/shard_map/gather/pallas_call | solution.py:150
  134.4 3.4 %spread.6.weight_ref = bf16[1024,2048]{1,0:T(8,128)(2,1)} custom-call(s32[8]{0:T(128)S(1)} %add.99.base_ref, bf16[1088,128]{1,0:T(8,128)(2,1)S(1)} %collective-permute-done.8.refs_0_.refs_1_.refs_2_, bf16[1088,128]{1,0:T(8,128)(2,1)S(1)} %collective-permute-done.8.refs_0_.refs_1_.refs_2_, bf16[1088,128]{1,0:T(8,128)(2,1)S(1)} %collective-permute-done.8.refs_0_.refs_1_.refs_2_), custom_call_target="tpu_custom_call" | custom-call | flops 100000000 | bytes 1000000 | tf_op jit(solution)/shard_map/spread/pallas_call | solution.py:120
  137.9 1.6 all-to-all-done.3
  139.5 4.3 %all-to-all-start.4 = ((bf16[8,256,512]{2,1,0:T(8,128)(2,1)}), bf16[8,256,512]{2,1,0:T(8,128)(2,1)}, u32[]{:S(2)}, u32[]{:S(2)}) async-start(bf16[8,256,512]{2,1,0:T(8,128)(2,1)} %bitcast.20), calls=%async_computation.4 | async-start | bytes 4194304 | tf_op jit(solution)/shard_map/all_to_all | solution.py:357
  143.9 5.5 %blend.6 = bf16[1024,512]{1,0:T(8,128)(2,1)S(1)} custom-call(bf16[1024,2048]{1,0:T(8,128)(2,1)} %spread.6.weight_ref, bf16[2048,512]{1,0:T(8,128)(2,1)} %bitcast.19.rows_ref, bf16[1024,512]{1,0:T(8,128)(2,1)} %collective-permute-done.11.rest_0_), custom_call_target="tpu_custom_call" | custom-call | flops 4000000000 | bytes 10000000 | tf_op jit(solution)/shard_map/blend/pallas_call | solution.py:197
  149.4 3.5 %collective-permute-start.12 = (bf16[1024,512]{1,0:T(8,128)(2,1)S(1)}, bf16[1024,512]{1,0:T(8,128)(2,1)S(1)}, u32[]{:S(2)}, u32[]{:S(2)}) collective-permute-start(bf16[1024,512]{1,0:T(8,128)(2,1)S(1)} %blend.6), channel_id=1, source_target_pairs={{0,2},{1,3},{2,0},{3,1},{4,6},{5,7},{6,4},{7,5},{8,10},{9,11},{10,... | collective-permute-start | bytes 3145736 | tf_op jit(solution)/shard_map/ppermute | solution.py:354
  153.0 1.5 add.111
  154.6 0.9 collective-permute-start.13
  155.5 3.4 %spread.7.weight_ref = bf16[1024,2048]{1,0:T(8,128)(2,1)} custom-call(s32[8]{0:T(128)S(1)} %add.99.base_ref, bf16[1088,128]{1,0:T(8,128)(2,1)S(1)} %pad_maximum_fusion.refs_0_.refs_1_.refs_2_, bf16[1088,128]{1,0:T(8,128)(2,1)S(1)} %pad_maximum_fusion.refs_0_.refs_1_.refs_2_, bf16[1088,128]{1,0:T(8,128)(2,1)S(1)} %pad_maximum_fusion.refs_0_.refs_1_.refs_2_), custom_call_target="tpu_custom_call" | custom-call | flops 100000000 | bytes 1000000 | tf_op jit(solution)/shard_map/spread/pallas_call | solution.py:120
  158.9 16.5 %encode.1 = bf16[4,256,512]{2,1,0:T(8,128)(2,1)S(1)} custom-call(bf16[256,768]{1,0:T(8,128)(2,1)S(1)} %copy-done.3, bf16[256,768]{1,0:T(8,128)(2,1)} %collective-permute-done.3.refs_1_, bf16[256,768]{1,0:T(8,128)(2,1)} %collective-permute-done.5.refs_2_, bf16[256,768]{1,0:T(8,128)(2,1)} %collective-permute-done.4.refs_3_, f32[768]{0:T(1024)S(1)} %copy-done.11, ...), custom_call_target="tpu_custom_call" | custom-call | flops 15000000512 | bytes 10000000 | tf_op jit(solution)/shard_map/encode/pallas_call | solution.py:303
  175.4 1.0 copy-done.16
  176.6 7.1 %blend.7 = (bf16[1024,512]{1,0:T(8,128)(2,1)}, bf16[1024,512]{1,0:T(8,128)(2,1)}) custom-call(s32[8]{0:T(128)S(1)} %fusion.8.place_ref, bf16[1024,2048]{1,0:T(8,128)(2,1)} %spread.7.weight_ref, bf16[2048,512]{1,0:T(8,128)(2,1)} %bitcast.21.rows_ref, bf16[1024,512]{1,0:T(8,128)(2,1)S(1)} %collective-permute-done.12.rest_0_, ...), custom_call_target="tpu_custom_call" | custom-call | flops 4000000000 | bytes 10000000 | tf_op jit(solution)/shard_map/blend/pallas_call | solution.py:197
  183.7 1.6 collective-permute-start.17
  185.4 6.0 %collective-permute-start.14 = (bf16[1024,512]{1,0:T(8,128)(2,1)}, bf16[1024,512]{1,0:T(8,128)(2,1)}, u32[]{:S(2)}, u32[]{:S(2)}) collective-permute-start(bf16[1024,512]{1,0:T(8,128)(2,1)} %get-tuple-element.99.refs_0_), channel_id=1, source_target_pairs={{0,2},{1,3},{2,0},{3,1},{4,6},{5,7},{6,4},{7,5},{8,10},{9,11},{10,... | collective-permute-start | bytes 3145736 | tf_op jit(solution)/shard_map/ppermute | solution.py:354
  191.4 4.5 %terms.7 = bf16[2048,512]{1,0:T(8,128)(2,1)S(1)} custom-call(bf16[1024,2048]{1,0:T(8,128)(2,1)} %spread.7.weight_ref, bf16[1024,512]{1,0:T(8,128)(2,1)} %get-tuple-element.99.refs_0_), custom_call_target="tpu_custom_call" | custom-call | flops 99999997952 | bytes 10000000 | tf_op jit(solution)/shard_map/terms/pallas_call | solution.py:220
  195.9 1.3 copy-done.1
  197.2 3.9 %all-to-all-start.5 = ((bf16[8,256,512]{2,1,0:T(8,128)(2,1)}), bf16[8,256,512]{2,1,0:T(8,128)(2,1)S(1)}, u32[]{:S(2)}, u32[]{:S(2)}) async-start(bf16[8,256,512]{2,1,0:T(8,128)(2,1)} %bitcast.60), calls=%async_computation.5 | async-start | bytes 4194304 | tf_op jit(solution)/shard_map/all_to_all | solution.py:357
  201.1 1.3 collective-permute-start.18
  202.4 11.9 %collective-permute-done.14.refs_0_ = bf16[1024,512]{1,0:T(8,128)(2,1)} collective-permute-done((bf16[1024,512]{1,0:T(8,128)(2,1)}, bf16[1024,512]{1,0:T(8,128)(2,1)}, u32[]{:S(2)}, u32[]{:S(2)}) %collective-permute-start.14) | collective-permute-done | bytes 1048608 | tf_op jit(solution)/shard_map/ppermute | solution.py:354
  214.3 1.7 collective-permute-start.15
  216.0 4.5 %terms.6 = bf16[2048,512]{1,0:T(8,128)(2,1)S(1)} custom-call(bf16[1024,2048]{1,0:T(8,128)(2,1)} %spread.6.weight_ref, bf16[1024,512]{1,0:T(8,128)(2,1)} %collective-permute-done.14.refs_0_), custom_call_target="tpu_custom_call" | custom-call | flops 99999997952 | bytes 10000000 | tf_op jit(solution)/shard_map/terms/pallas_call | solution.py:220
  220.5 1.3 copy-done
  221.7 6.0 %all-to-all-done.5 = bf16[8,256,512]{2,1,0:T(8,128)(2,1)S(1)} async-done(((bf16[8,256,512]{2,1,0:T(8,128)(2,1)}), bf16[8,256,512]{2,1,0:T(8,128)(2,1)S(1)}, u32[]{:S(2)}, u32[]{:S(2)}) %all-to-all-start.5) | async-done | bytes 2097184 | tf_op jit(solution)/shard_map/all_to_all | solution.py:357
  227.7 4.4 %all-to-all-start.6 = ((bf16[8,256,512]{2,1,0:T(8,128)(2,1)}), bf16[8,256,512]{2,1,0:T(8,128)(2,1)}, u32[]{:S(2)}, u32[]{:S(2)}) async-start(bf16[8,256,512]{2,1,0:T(8,128)(2,1)} %bitcast.59), calls=%async_computation.6 | async-start | bytes 4194304 | tf_op jit(solution)/shard_map/all_to_all | solution.py:357
  232.1 1.3 collective-permute-start.16
  233.4 6.1 %collective-permute-done.18.refs_1_ = bf16[1024,512]{1,0:T(8,128)(2,1)} collective-permute-done((bf16[1024,512]{1,0:T(8,128)(2,1)}, bf16[1024,512]{1,0:T(8,128)(2,1)}, u32[]{:S(2)}, u32[]{:S(2)}) %collective-permute-start.18) | collective-permute-done | bytes 1048608 | tf_op jit(solution)/shard_map/ppermute | solution.py:354
  239.5 5.8 %terms.5 = bf16[2048,512]{1,0:T(8,128)(2,1)} custom-call(bf16[1024,2048]{1,0:T(8,128)(2,1)} %spread.5.weight_ref, bf16[1024,512]{1,0:T(8,128)(2,1)} %collective-permute-done.17.refs_0_, bf16[1024,512]{1,0:T(8,128)(2,1)} %collective-permute-done.18.refs_1_), custom_call_target="tpu_custom_call" | custom-call | flops 99999997952 | bytes 10000000 | tf_op jit(solution)/shard_map/terms/pallas_call | solution.py:220
  245.3 13.4 %all-to-all-done.6 = bf16[8,256,512]{2,1,0:T(8,128)(2,1)} async-done(((bf16[8,256,512]{2,1,0:T(8,128)(2,1)}), bf16[8,256,512]{2,1,0:T(8,128)(2,1)}, u32[]{:S(2)}, u32[]{:S(2)}) %all-to-all-start.6) | async-done | bytes 2097184 | tf_op jit(solution)/shard_map/all_to_all | solution.py:357
  258.7 4.3 %all-to-all-start.7 = ((bf16[8,256,512]{2,1,0:T(8,128)(2,1)}), bf16[8,256,512]{2,1,0:T(8,128)(2,1)}, u32[]{:S(2)}, u32[]{:S(2)}) async-start(bf16[8,256,512]{2,1,0:T(8,128)(2,1)} %bitcast.69), calls=%async_computation.7 | async-start | bytes 4194304 | tf_op jit(solution)/shard_map/all_to_all | solution.py:357
  263.1 3.7 %collective-permute-done.16.refs_1_ = bf16[1024,512]{1,0:T(8,128)(2,1)} collective-permute-done((bf16[1024,512]{1,0:T(8,128)(2,1)}, bf16[1024,512]{1,0:T(8,128)(2,1)}, u32[]{:S(2)}, u32[]{:S(2)}) %collective-permute-start.16) | collective-permute-done | bytes 1048608 | tf_op jit(solution)/shard_map/ppermute | solution.py:354
  266.8 5.7 %terms.4 = bf16[2048,512]{1,0:T(8,128)(2,1)} custom-call(bf16[1024,2048]{1,0:T(8,128)(2,1)} %spread.4.weight_ref, bf16[1024,512]{1,0:T(8,128)(2,1)} %collective-permute-done.15.refs_0_, bf16[1024,512]{1,0:T(8,128)(2,1)} %collective-permute-done.16.refs_1_), custom_call_target="tpu_custom_call" | custom-call | flops 99999997952 | bytes 10000000 | tf_op jit(solution)/shard_map/terms/pallas_call | solution.py:220
  272.5 17.2 %all-to-all-done.7 = bf16[8,256,512]{2,1,0:T(8,128)(2,1)} async-done(((bf16[8,256,512]{2,1,0:T(8,128)(2,1)}), bf16[8,256,512]{2,1,0:T(8,128)(2,1)}, u32[]{:S(2)}, u32[]{:S(2)}) %all-to-all-start.7) | async-done | bytes 2097184 | tf_op jit(solution)/shard_map/all_to_all | solution.py:357
  289.7 4.5 %all-to-all-start.8 = ((bf16[8,256,512]{2,1,0:T(8,128)(2,1)}), bf16[8,256,512]{2,1,0:T(8,128)(2,1)}, u32[]{:S(2)}, u32[]{:S(2)}) async-start(bf16[8,256,512]{2,1,0:T(8,128)(2,1)} %bitcast.70), calls=%async_computation.8 | async-start | bytes 4194304 | tf_op jit(solution)/shard_map/all_to_all | solution.py:357
  294.3 16.9 %add_rows.2.refs_2_ = f32[2048,512]{1,0:T(8,128)} custom-call(s32[8,256]{1,0:T(8,128)S(1)} %reshape.74.refs_0_, s32[8,256]{1,0:T(8,128)S(1)} %reshape.73.refs_1_, s32[8,256]{1,0:T(8,128)S(1)} %copy-done.7, bf16[2048,512]{1,0:T(8,128)(2,1)S(1)} %bitcast.58, bf16[2048,512]{1,0:T(8,128)(2,1)} %bitcast.27.refs_4_, bf16[2048,512]{1,0:T(8,128)(2,1)} %bitcast.29.refs_5_), custom_call_target="tpu_custom_call" | custom-call | flops 15000000512 | bytes 10000000 | tf_op jit(solution)/shard_map/add_rows/pallas_call | solution.py:259
  311.1 9.8 %all-to-all-done.8 = bf16[8,256,512]{2,1,0:T(8,128)(2,1)} async-done(((bf16[8,256,512]{2,1,0:T(8,128)(2,1)}), bf16[8,256,512]{2,1,0:T(8,128)(2,1)}, u32[]{:S(2)}, u32[]{:S(2)}) %all-to-all-start.8) | async-done | bytes 2097184 | tf_op jit(solution)/shard_map/all_to_all | solution.py:357
  320.9 8.3 %add_rows.3 = f32[2048,512]{1,0:T(8,128)} custom-call(s32[8,256]{1,0:T(8,128)S(1)} %copy-done.5, bf16[2048,512]{1,0:T(8,128)(2,1)} %bitcast.31.refs_1_, f32[2048,512]{1,0:T(8,128)} %add_rows.2.refs_2_), custom_call_target="tpu_custom_call" | custom-call | flops 5000000000 | bytes 10000000 | tf_op jit(solution)/shard_map/add_rows/pallas_call | solution.py:259
  (72 shorter events, 5.0 us)
Async XLA Ops:
  0.6 0.7 copy-start.9
  1.4 1.4 copy-start.17
  2.7 9.1 %copy-start.2 = (f32[8,4,32,128]{3,2,1,0:T(8,128)S(1)}, f32[8,4,32,128]{3,2,1,0:T(8,128)}, u32[]{:S(2)}) copy-start(f32[8,4,32,128]{3,2,1,0:T(8,128)} %param.25) | copy-start | bytes 1572868
  3.8 15.3 %collective-permute-start = (bf16[4,128,768]{2,1,0:T(8,128)(2,1)}, bf16[4,128,768]{2,1,0:T(8,128)(2,1)S(1)}, u32[]{:S(2)}, u32[]{:S(2)}) collective-permute-start(bf16[4,128,768]{2,1,0:T(8,128)(2,1)} %get-tuple-element.111), channel_id=1, source_target_pairs={{0,1},{1,0},{2,3},{3,2},{4,5},{5,4},{6,7},{7,6},{8,9},{9,8},{10,11... | collective-permute-start | bytes 2359304 | tf_op jit(solution)/shard_map/ppermute | solution.py:354
  4.9 14.2 %all-to-all-start = ((s32[32,1,256]{2,1,0:T(1,128)}), s32[32,1,256]{2,1,0:T(1,128)S(1)}, u32[]{:S(2)}, u32[]{:S(2)}) async-start(s32[32,1,256]{2,1,0:T(1,128)} %copy.31), calls=%async_computation | async-start | bytes 65536 | tf_op jit(solution)/shard_map/all_to_all | solution.py:366
  19.1 7.7 %copy-start.18 = (bf16[4,128,768]{2,1,0:T(8,128)(2,1)}, bf16[4,128,768]{2,1,0:T(8,128)(2,1)S(1)}, u32[]{:S(2)}) copy-start(bf16[4,128,768]{2,1,0:T(8,128)(2,1)S(1)} %collective-permute-done) | copy-start | bytes 2359300
  19.2 7.6 %copy-start.4 = (s32[8,256]{1,0:T(8,128)}, s32[8,256]{1,0:T(8,128)S(1)}, u32[]{:S(2)}) copy-start(s32[8,256]{1,0:T(8,128)S(1)} %reshape.71.refs_0_) | copy-start | bytes 24580
  19.2 22.6 %copy-start.6 = (s32[8,256]{1,0:T(8,128)}, s32[8,256]{1,0:T(8,128)S(1)}, u32[]{:S(2)}) copy-start(s32[8,256]{1,0:T(8,128)S(1)} %reshape.72.refs_2_) | copy-start | bytes 24580
  26.7 43.3 %all-to-all-start.1 = ((bf16[8,256,512]{2,1,0:T(8,128)(2,1)}), bf16[8,256,512]{2,1,0:T(8,128)(2,1)S(1)}, u32[]{:S(2)}, u32[]{:S(2)}) async-start(bf16[8,256,512]{2,1,0:T(8,128)(2,1)} %bitcast.7), calls=%async_computation.1 | async-start | bytes 4194304 | tf_op jit(solution)/shard_map/all_to_all | solution.py:357
  32.8 37.2 %collective-permute-start.3 = (bf16[256,768]{1,0:T(8,128)(2,1)}, bf16[256,768]{1,0:T(8,128)(2,1)}, u32[]{:S(2)}, u32[]{:S(2)}) collective-permute-start(bf16[256,768]{1,0:T(8,128)(2,1)} %get-tuple-element.107), channel_id=1, source_target_pairs={{0,2},{1,3},{2,4},{3,5},{4,6},{5,7},{6,0},{7,1},{8,10},{9,11},{10,... | collective-permute-start | bytes 1179656 | tf_op jit(solution)/shard_map/ppermute | solution.py:354
  33.3 36.7 %collective-permute-start.4 = (bf16[256,768]{1,0:T(8,128)(2,1)}, bf16[256,768]{1,0:T(8,128)(2,1)}, u32[]{:S(2)}, u32[]{:S(2)}) collective-permute-start(bf16[256,768]{1,0:T(8,128)(2,1)} %get-tuple-element.108), channel_id=1, source_target_pairs={{0,6},{1,7},{2,0},{3,1},{4,2},{5,3},{6,4},{7,5},{8,14},{9,15},{10,... | collective-permute-start | bytes 1179656 | tf_op jit(solution)/shard_map/ppermute | solution.py:354
  36.7 20.7 %collective-permute-start.2 = (bf16[1088,128]{1,0:T(8,128)(2,1)S(1)}, bf16[1088,128]{1,0:T(8,128)(2,1)S(1)}, u32[]{:S(2)}, u32[]{:S(2)}) collective-permute-start(bf16[1088,128]{1,0:T(8,128)(2,1)S(1)} %pad_maximum_fusion.refs_0_.refs_1_.refs_2_), channel_id=1, source_target_pairs={{0,4},{1,5},{6,2},{7,3},{8,12},{9,13},{14,10},{15,11},{16,20},{17,... | collective-permute-start | bytes 835592 | tf_op jit(solution)/shard_map/ppermute | solution.py:354
  38.0 28.7 %collective-permute-start.1 = (bf16[1088,128]{1,0:T(8,128)(2,1)S(1)}, bf16[1088,128]{1,0:T(8,128)(2,1)S(1)}, u32[]{:S(2)}, u32[]{:S(2)}) collective-permute-start(bf16[1088,128]{1,0:T(8,128)(2,1)S(1)} %pad_maximum_fusion.refs_0_.refs_1_.refs_2_), channel_id=1, source_target_pairs={{0,6},{1,7},{6,0},{7,1},{8,14},{9,15},{14,8},{15,9},{16,22},{17,23... | collective-permute-start | bytes 835592 | tf_op jit(solution)/shard_map/ppermute | solution.py:354
  70.0 38.5 %all-to-all-start.2 = ((bf16[8,256,512]{2,1,0:T(8,128)(2,1)}), bf16[8,256,512]{2,1,0:T(8,128)(2,1)}, u32[]{:S(2)}, u32[]{:S(2)}) async-start(bf16[8,256,512]{2,1,0:T(8,128)(2,1)} %bitcast.15), calls=%async_computation.2 | async-start | bytes 4194304 | tf_op jit(solution)/shard_map/all_to_all | solution.py:357
  74.4 18.9 %collective-permute-start.5 = (bf16[256,768]{1,0:T(8,128)(2,1)}, bf16[256,768]{1,0:T(8,128)(2,1)}, u32[]{:S(2)}, u32[]{:S(2)}) collective-permute-start(bf16[256,768]{1,0:T(8,128)(2,1)} %get-tuple-element.106), channel_id=1, source_target_pairs={{0,4},{1,5},{2,6},{3,7},{4,0},{5,1},{6,2},{7,3},{8,12},{9,13},{10,... | collective-permute-start | bytes 1179656 | tf_op jit(solution)/shard_map/ppermute | solution.py:354
  74.5 34.0 %collective-permute-start.8 = (bf16[1088,128]{1,0:T(8,128)(2,1)S(1)}, bf16[1088,128]{1,0:T(8,128)(2,1)S(1)}, u32[]{:S(2)}, u32[]{:S(2)}) collective-permute-start(bf16[1088,128]{1,0:T(8,128)(2,1)S(1)} %pad_maximum_fusion.refs_0_.refs_1_.refs_2_), channel_id=1, source_target_pairs={{0,2},{1,3},{2,0},{3,1},{4,6},{5,7},{6,4},{7,5},{8,10},{9,11},{10,... | collective-permute-start | bytes 835592 | tf_op jit(solution)/shard_map/ppermute | solution.py:354
  75.5 25.4 %collective-permute-start.7 = (bf16[1088,128]{1,0:T(8,128)(2,1)S(1)}, bf16[1088,128]{1,0:T(8,128)(2,1)S(1)}, u32[]{:S(2)}, u32[]{:S(2)}) collective-permute-start(bf16[1088,128]{1,0:T(8,128)(2,1)S(1)} %pad_maximum_fusion.refs_0_.refs_1_.refs_2_), channel_id=1, source_target_pairs={{2,4},{3,5},{4,2},{5,3},{10,12},{11,13},{12,10},{13,11},{18,20},{1... | collective-permute-start | bytes 835592 | tf_op jit(solution)/shard_map/ppermute | solution.py:354
  76.2 28.9 %collective-permute-start.6 = (bf16[1088,128]{1,0:T(8,128)(2,1)S(1)}, bf16[1088,128]{1,0:T(8,128)(2,1)S(1)}, u32[]{:S(2)}, u32[]{:S(2)}) collective-permute-start(bf16[1088,128]{1,0:T(8,128)(2,1)S(1)} %pad_maximum_fusion.refs_0_.refs_1_.refs_2_), channel_id=1, source_target_pairs={{2,6},{3,7},{4,0},{5,1},{10,14},{11,15},{12,8},{13,9},{18,22},{19,... | collective-permute-start | bytes 835592 | tf_op jit(solution)/shard_map/ppermute | solution.py:354
  83.0 29.9 %collective-permute-start.10 = (bf16[1024,512]{1,0:T(8,128)(2,1)}, bf16[1024,512]{1,0:T(8,128)(2,1)}, u32[]{:S(2)}, u32[]{:S(2)}) collective-permute-start(bf16[1024,512]{1,0:T(8,128)(2,1)} %blend.4), channel_id=1, source_target_pairs={{0,2},{1,3},{6,4},{7,5},{8,10},{9,11},{14,12},{15,13},{16,18},{17,... | collective-permute-start | bytes 3145736 | tf_op jit(solution)/shard_map/ppermute | solution.py:354
  108.5 31.0 %all-to-all-start.3 = ((bf16[8,256,512]{2,1,0:T(8,128)(2,1)}), bf16[8,256,512]{2,1,0:T(8,128)(2,1)}, u32[]{:S(2)}, u32[]{:S(2)}) async-start(bf16[8,256,512]{2,1,0:T(8,128)(2,1)} %bitcast.18), calls=%async_computation.3 | async-start | bytes 4194304 | tf_op jit(solution)/shard_map/all_to_all | solution.py:357
  114.7 23.2 %collective-permute-start.11 = (bf16[1024,512]{1,0:T(8,128)(2,1)S(1)}, bf16[1024,512]{1,0:T(8,128)(2,1)}, u32[]{:S(2)}, u32[]{:S(2)}) collective-permute-start(bf16[1024,512]{1,0:T(8,128)(2,1)S(1)} %add.110), channel_id=1, source_target_pairs={{2,4},{3,5},{4,2},{5,3},{10,12},{11,13},{12,10},{13,11},{18,20},{1... | collective-permute-start | bytes 3145736 | tf_op jit(solution)/shard_map/ppermute | solution.py:354
  121.7 31.2 %collective-permute-start.9 = (bf16[1024,512]{1,0:T(8,128)(2,1)S(1)}, bf16[1024,512]{1,0:T(8,128)(2,1)}, u32[]{:S(2)}, u32[]{:S(2)}) collective-permute-start(bf16[1024,512]{1,0:T(8,128)(2,1)S(1)} %blend.5), channel_id=1, source_target_pairs={{0,2},{1,3},{6,4},{7,5},{8,10},{9,11},{14,12},{15,13},{16,18},{17,... | collective-permute-start | bytes 3145736 | tf_op jit(solution)/shard_map/ppermute | solution.py:354
  139.5 37.1 %all-to-all-start.4 = ((bf16[8,256,512]{2,1,0:T(8,128)(2,1)}), bf16[8,256,512]{2,1,0:T(8,128)(2,1)}, u32[]{:S(2)}, u32[]{:S(2)}) async-start(bf16[8,256,512]{2,1,0:T(8,128)(2,1)} %bitcast.20), calls=%async_computation.4 | async-start | bytes 4194304 | tf_op jit(solution)/shard_map/all_to_all | solution.py:357
  149.4 27.2 %collective-permute-start.12 = (bf16[1024,512]{1,0:T(8,128)(2,1)S(1)}, bf16[1024,512]{1,0:T(8,128)(2,1)S(1)}, u32[]{:S(2)}, u32[]{:S(2)}) collective-permute-start(bf16[1024,512]{1,0:T(8,128)(2,1)S(1)} %blend.6), channel_id=1, source_target_pairs={{0,2},{1,3},{2,0},{3,1},{4,6},{5,7},{6,4},{7,5},{8,10},{9,11},{10,... | collective-permute-start | bytes 3145736 | tf_op jit(solution)/shard_map/ppermute | solution.py:354
  154.5 4.3 %copy-start.3 = (bf16[256,768]{1,0:T(8,128)(2,1)S(1)}, bf16[256,768]{1,0:T(8,128)(2,1)}, u32[]{:S(2)}) copy-start(bf16[256,768]{1,0:T(8,128)(2,1)} %get-tuple-element.94.refs_0_) | copy-start | bytes 1179652
  154.5 4.3 %copy-start.8 = (bf16[768,512]{1,0:T(8,128)(2,1)S(1)}, bf16[768,512]{1,0:T(8,128)(2,1)}, u32[]{:S(2)}) copy-start(bf16[768,512]{1,0:T(8,128)(2,1)} %refs_12_.1) | copy-start | bytes 2359300
  154.5 4.3 %copy-start.10 = (f32[3072]{0:T(1024)S(1)}, f32[3072]{0:T(1024)}, u32[]{:S(2)}) copy-start(f32[3072]{0:T(1024)} %refs_7_.1) | copy-start | bytes 36868
  154.5 4.3 %copy-start.11 = (f32[768]{0:T(1024)S(1)}, f32[768]{0:T(1024)}, u32[]{:S(2)}) copy-start(f32[768]{0:T(1024)} %refs_4_.1) | copy-start | bytes 9220
  154.5 4.3 %copy-start.12 = (f32[768]{0:T(1024)S(1)}, f32[768]{0:T(1024)}, u32[]{:S(2)}) copy-start(f32[768]{0:T(1024)} %refs_5_.1) | copy-start | bytes 9220
  154.6 4.3 %copy-start.13 = (f32[768]{0:T(1024)S(1)}, f32[768]{0:T(1024)}, u32[]{:S(2)}) copy-start(f32[768]{0:T(1024)} %refs_9_.1) | copy-start | bytes 9220
  154.6 4.3 %copy-start.14 = (f32[768]{0:T(1024)S(1)}, f32[768]{0:T(1024)}, u32[]{:S(2)}) copy-start(f32[768]{0:T(1024)} %refs_10_.1) | copy-start | bytes 9220
  154.6 4.3 %copy-start.15 = (f32[768]{0:T(1024)S(1)}, f32[768]{0:T(1024)}, u32[]{:S(2)}) copy-start(f32[768]{0:T(1024)} %refs_11_.1) | copy-start | bytes 9220
  154.6 21.8 %collective-permute-start.13 = (bf16[1024,512]{1,0:T(8,128)(2,1)S(1)}, bf16[1024,512]{1,0:T(8,128)(2,1)S(1)}, u32[]{:S(2)}, u32[]{:S(2)}) collective-permute-start(bf16[1024,512]{1,0:T(8,128)(2,1)S(1)} %add.111), channel_id=1, source_target_pairs={{2,4},{3,5},{4,2},{5,3},{10,12},{11,13},{12,10},{13,11},{18,20},{1... | collective-permute-start | bytes 3145736 | tf_op jit(solution)/shard_map/ppermute | solution.py:354
  175.4 1.0 copy-start.16
  183.7 17.3 %collective-permute-start.17 = (bf16[1024,512]{1,0:T(8,128)(2,1)}, bf16[1024,512]{1,0:T(8,128)(2,1)}, u32[]{:S(2)}, u32[]{:S(2)}) collective-permute-start(bf16[1024,512]{1,0:T(8,128)(2,1)} %get-tuple-element.99.refs_0_), channel_id=1, source_target_pairs={{2,4},{3,5},{4,2},{5,3},{10,12},{11,13},{12,10},{13,11},{18,20},{1... | collective-permute-start | bytes 3145736 | tf_op jit(solution)/shard_map/ppermute | solution.py:354
  185.4 29.0 %collective-permute-start.14 = (bf16[1024,512]{1,0:T(8,128)(2,1)}, bf16[1024,512]{1,0:T(8,128)(2,1)}, u32[]{:S(2)}, u32[]{:S(2)}) collective-permute-start(bf16[1024,512]{1,0:T(8,128)(2,1)} %get-tuple-element.99.refs_0_), channel_id=1, source_target_pairs={{0,2},{1,3},{2,0},{3,1},{4,6},{5,7},{6,4},{7,5},{8,10},{9,11},{10,... | collective-permute-start | bytes 3145736 | tf_op jit(solution)/shard_map/ppermute | solution.py:354
  195.9 1.3 copy-start.1
  197.2 30.5 %all-to-all-start.5 = ((bf16[8,256,512]{2,1,0:T(8,128)(2,1)}), bf16[8,256,512]{2,1,0:T(8,128)(2,1)S(1)}, u32[]{:S(2)}, u32[]{:S(2)}) async-start(bf16[8,256,512]{2,1,0:T(8,128)(2,1)} %bitcast.60), calls=%async_computation.5 | async-start | bytes 4194304 | tf_op jit(solution)/shard_map/all_to_all | solution.py:357
  201.1 38.4 %collective-permute-start.18 = (bf16[1024,512]{1,0:T(8,128)(2,1)}, bf16[1024,512]{1,0:T(8,128)(2,1)}, u32[]{:S(2)}, u32[]{:S(2)}) collective-permute-start(bf16[1024,512]{1,0:T(8,128)(2,1)} %collective-permute-done.17.refs_0_), channel_id=1, source_target_pairs={{2,0},{3,1},{4,6},{5,7},{10,8},{11,9},{12,14},{13,15},{18,16},{19,... | collective-permute-start | bytes 3145736 | tf_op jit(solution)/shard_map/ppermute | solution.py:354
  214.3 17.8 %collective-permute-start.15 = (bf16[1024,512]{1,0:T(8,128)(2,1)}, bf16[1024,512]{1,0:T(8,128)(2,1)}, u32[]{:S(2)}, u32[]{:S(2)}) collective-permute-start(bf16[1024,512]{1,0:T(8,128)(2,1)} %collective-permute-done.14.refs_0_), channel_id=1, source_target_pairs={{2,4},{3,5},{4,2},{5,3},{10,12},{11,13},{12,10},{13,11},{18,20},{1... | collective-permute-start | bytes 3145736 | tf_op jit(solution)/shard_map/ppermute | solution.py:354
  220.4 1.3 copy-start
  227.7 31.0 %all-to-all-start.6 = ((bf16[8,256,512]{2,1,0:T(8,128)(2,1)}), bf16[8,256,512]{2,1,0:T(8,128)(2,1)}, u32[]{:S(2)}, u32[]{:S(2)}) async-start(bf16[8,256,512]{2,1,0:T(8,128)(2,1)} %bitcast.59), calls=%async_computation.6 | async-start | bytes 4194304 | tf_op jit(solution)/shard_map/all_to_all | solution.py:357
  232.1 34.7 %collective-permute-start.16 = (bf16[1024,512]{1,0:T(8,128)(2,1)}, bf16[1024,512]{1,0:T(8,128)(2,1)}, u32[]{:S(2)}, u32[]{:S(2)}) collective-permute-start(bf16[1024,512]{1,0:T(8,128)(2,1)} %collective-permute-done.15.refs_0_), channel_id=1, source_target_pairs={{2,0},{3,1},{4,6},{5,7},{10,8},{11,9},{12,14},{13,15},{18,16},{19,... | collective-permute-start | bytes 3145736 | tf_op jit(solution)/shard_map/ppermute | solution.py:354
  258.7 31.0 %all-to-all-start.7 = ((bf16[8,256,512]{2,1,0:T(8,128)(2,1)}), bf16[8,256,512]{2,1,0:T(8,128)(2,1)}, u32[]{:S(2)}, u32[]{:S(2)}) async-start(bf16[8,256,512]{2,1,0:T(8,128)(2,1)} %bitcast.69), calls=%async_computation.7 | async-start | bytes 4194304 | tf_op jit(solution)/shard_map/all_to_all | solution.py:357
  289.7 4.5 %copy-start.7 = (s32[8,256]{1,0:T(8,128)S(1)}, s32[8,256]{1,0:T(8,128)}, u32[]{:S(2)}) copy-start(s32[8,256]{1,0:T(8,128)} %copy-done.6) | copy-start | bytes 24580
  289.7 31.2 %all-to-all-start.8 = ((bf16[8,256,512]{2,1,0:T(8,128)(2,1)}), bf16[8,256,512]{2,1,0:T(8,128)(2,1)}, u32[]{:S(2)}, u32[]{:S(2)}) async-start(bf16[8,256,512]{2,1,0:T(8,128)(2,1)} %bitcast.70), calls=%async_computation.8 | async-start | bytes 4194304 | tf_op jit(solution)/shard_map/all_to_all | solution.py:357
  294.3 26.6 %copy-start.5 = (s32[8,256]{1,0:T(8,128)S(1)}, s32[8,256]{1,0:T(8,128)}, u32[]{:S(2)}) copy-start(s32[8,256]{1,0:T(8,128)} %copy-done.4) | copy-start | bytes 24580

commit v2 on v1

--- a/solution.py
+++ b/solution.py
@@ -374,10 +374,11 @@
     far_to_outer = move(packed, moves((0, 3), (3, 0)))
     far_to_inner = move(packed, moves((0, 2), (3, 1)))
     pairs = jnp.concatenate([lax.dynamic_index_in_dim(patches, core, 1, keepdims=False), others], 1)
-    strips = []
-    for n in range(chips):
+
+    def strip(pairs, n):
         pair = lax.dynamic_index_in_dim(pairs, lax.rem(chip + n, chips), 0, keepdims=False)
-        strips.append(move(pair, [(a, (a + 2 * n) % n_tile) for a in range(n_tile)]) if n else pair)
+        return move(pair, [(a, (a + 2 * n) % n_tile) for a in range(n_tile)]) if n else pair
+
     view = jnp.arange(n_tile, dtype=I32)
     place = lax.rem(chip + chips - view // 2, chips) * 2 + (view % 2 != core).astype(I32)
     asked = asked.reshape(n_img, 4, wide_layer, cap)
@@ -395,29 +396,30 @@
     looked, lists[1] = tie(gather(lists[0], gauss_rows), lists[1])
     rows_1 = exchange(looked)
     looked_2 = gather(lists[1], gauss_rows)
+    far_to_outer, far_to_inner, pairs, looked_2 = tie(far_to_outer, far_to_inner, pairs, looked_2)
+    strips = [strip(pairs, n) for n in range(2)]
     spread_1 = spread_of(far_to_outer, far_to_inner)
-    looked_2, spread_1, rows_1, packed, lists[2], *strips[1::2] = tie(
-        looked_2, spread_1, rows_1, packed, lists[2], *strips[1::2]
-    )
+    looked_2, spread_1, rows_1, *strips = tie(looked_2, spread_1, rows_1, *strips)
 
     rows_2 = exchange(looked_2)
     part_1 = blend(spread_1, rows_1)
     moved_1 = move(part_1, inwards)
+    part_1, lists[2], packed, pairs = tie(part_1, lists[2], packed, pairs)
     near_to_outer = move(packed, moves((1, 3), (2, 0)))
     near_to_inner = move(packed, middle)
-    from_beside = move(packed, beside)
-    part_1, lists[2], *strips = tie(part_1, lists[2], *strips)
+    strips += [strip(pairs, n) for n in range(2, chips)]
     looked_3 = gather(lists[2], gauss_rows, 15 * 10**9)
     spread_2 = spread_of(near_to_outer, near_to_inner)
-    looked_3, rows_2, part_1, lists[3], spread_2, from_beside = tie(
-        looked_3, rows_2, part_1, lists[3], spread_2, from_beside
+    looked_3, rows_2, part_1, lists[3], spread_2, packed, *strips = tie(
+        looked_3, rows_2, part_1, lists[3], spread_2, packed, *strips
     )
 
     rows_3 = exchange(looked_3)
+    from_beside = move(packed, beside)
     far = move(part_1 + moved_1, middle)
     part_2 = blend(spread_2, rows_2)
     moved_2 = move(part_2, inwards)
-    part_2, lists[3], from_beside = tie(part_2, lists[3], from_beside)
+    part_2, lists[3] = tie(part_2, lists[3])
     looked_4 = gather(lists[3], gauss_rows)
     spread_3 = spread_of(from_beside)
     looked_4, rows_3, far, spread_3, packed = tie(looked_4, rows_3, far, spread_3, packed)

time: 331 us -> 362 us (1.094)
  waiting for transfers between devices: 101 us -> 130 us
  local copies, waits for them, and re-layouts: 6.74 us -> 10.4 us
    ppermute x19, waiting for transfers between devices: 46.4 us -> 74 us  [move(): return lax.ppermute(x, 'tile', pairs)]
  transfers between devices with their start and end apart: 28 -> 28, of which waited for: 14 -> 14; matrix products, arithmetic and copies ran while one was open for 2% -> 2% of each run, Pallas kernels for 32% -> 29%
where the time goes in v2:
time: 362 us; the launch traced here: 360 us
  waiting for transfers between devices  130 us (36%)
  Pallas kernels  129 us (36%)
  starting transfers between devices  84.6 us (23%)
  local copies, waits for them, and re-layouts  10.4 us (3%)
  other arithmetic  4.22 us (1%)
    ppermute x19, waiting for transfers between devices, move(): return lax.ppermute(x, 'tile', pairs)  74 us
    all_to_all x8, waiting for transfers between devices, exchange(): lax.all_to_all(x, both, split_axis=0, concat_axis=0, axis_index_groups=gr...  49.7 us
    ppermute x19, starting transfers between devices, move(): return lax.ppermute(x, 'tile', pairs)  43.9 us
    all_to_all x8, starting transfers between devices, exchange(): lax.all_to_all(x, both, split_axis=0, concat_axis=0, axis_index_groups=gr...  33.7 us
    pallas_call x4, Pallas kernels, gather(): pl.pallas_call(functools.partial(gather_kernel, group, cap), grid=(near /...  29.7 us
    pallas_call x2, Pallas kernels, add_rows(): pl.pallas_call(functools.partial(add_rows_kernel, count), grid=(held // b...  25.2 us
    pallas_call x4, Pallas kernels, blend(): pl.pallas_call(functools.partial(last_blend_kernel if last else blend_ker...  22.5 us
    pallas_call x4, Pallas kernels, terms(): pl.pallas_call(terms_kernel, grid=(slots // block,), in_specs=[pl.BlockSp...  20.1 us
  transfers between devices with their start and end apart: 28, of which 14 were waited for; matrix products, arithmetic and copies ran while one was open for 2% of the time, Pallas kernels for 29%

profile of v2, /device:TPU:0, one launch (start us, length us, event | category | flops | bytes accessed | tf_op | source)
XLA Modules:
  0.0 360.0 jit_solution(5279528940809430593)
XLA Ops:
  1.4 1.3 index.1
  2.8 1.0 dynamic-slice_bitcast_fusion
  4.9 7.0 %all-to-all-start = ((s32[32,1,256]{2,1,0:T(1,128)}), s32[32,1,256]{2,1,0:T(1,128)S(1)}, u32[]{:S(2)}, u32[]{:S(2)}) async-start(s32[32,1,256]{2,1,0:T(1,128)} %copy.31), calls=%async_computation | async-start | bytes 65536 | tf_op jit(solution)/shard_map/all_to_all | solution.py:366
  12.6 6.5 %all-to-all-done = s32[32,1,256]{2,1,0:T(1,128)S(1)} async-done(((s32[32,1,256]{2,1,0:T(1,128)}), s32[32,1,256]{2,1,0:T(1,128)S(1)}, u32[]{:S(2)}, u32[]{:S(2)}) %all-to-all-start) | async-done | bytes 32800 | tf_op jit(solution)/shard_map/all_to_all | solution.py:366
  19.3 7.4 %gather.4 = bf16[2048,512]{1,0:T(8,128)(2,1)} custom-call(s32[256,8]{1,0:T(8,128)S(1)} %copy.33.asked_ref, bf16[2048,512]{1,0:T(8,128)(2,1)} %rows_ref.7), custom_call_target="tpu_custom_call" | custom-call | flops 100000000 | bytes 1000000 | tf_op jit(solution)/shard_map/gather/pallas_call | solution.py:150
  26.7 3.6 %all-to-all-start.1 = ((bf16[8,256,512]{2,1,0:T(8,128)(2,1)}), bf16[8,256,512]{2,1,0:T(8,128)(2,1)S(1)}, u32[]{:S(2)}, u32[]{:S(2)}) async-start(bf16[8,256,512]{2,1,0:T(8,128)(2,1)} %bitcast.8), calls=%async_computation.1 | async-start | bytes 4194304 | tf_op jit(solution)/shard_map/all_to_all | solution.py:357
  30.3 2.4 collective-permute-start.2
  32.8 4.3 %collective-permute-start.1 = (bf16[1088,128]{1,0:T(8,128)(2,1)S(1)}, bf16[1088,128]{1,0:T(8,128)(2,1)S(1)}, u32[]{:S(2)}, u32[]{:S(2)}) collective-permute-start(bf16[1088,128]{1,0:T(8,128)(2,1)S(1)} %pad_maximum_fusion.1.refs_0_.refs_1_.refs_2_), channel_id=1, source_target_pairs={{0,6},{1,7},{6,0},{7,1},{8,14},{9,15},{14,8},{15,9},{16,22},{17,23... | collective-permute-start | bytes 835592 | tf_op jit(solution)/shard_map/ppermute | solution.py:354
  37.3 7.5 %gather.5 = bf16[2048,512]{1,0:T(8,128)(2,1)} custom-call(s32[256,8]{1,0:T(8,128)S(1)} %copy.35.asked_ref, bf16[2048,512]{1,0:T(8,128)(2,1)} %rows_ref.7), custom_call_target="tpu_custom_call" | custom-call | flops 100000000 | bytes 1000000 | tf_op jit(solution)/shard_map/gather/pallas_call | solution.py:150
  44.9 3.1 collective-permute-done.1.refs_0_.refs_1_.refs_2_
  48.0 0.9 dynamic-slice_bitcast_fusion.4
  49.1 3.4 spread.4.weight_ref
  52.5 9.0 %collective-permute-done.3.refs_1_ = bf16[256,768]{1,0:T(8,128)(2,1)S(1)} collective-permute-done((bf16[256,768]{1,0:T(8,128)(2,1)}, bf16[256,768]{1,0:T(8,128)(2,1)S(1)}, u32[]{:S(2)}, u32[]{:S(2)}) %collective-permute-start.3) | collective-permute-done | bytes 393248 | tf_op jit(solution)/shard_map/ppermute | solution.py:354
  61.5 0.8 copy-done.9
  62.3 4.4 %all-to-all-start.2 = ((bf16[8,256,512]{2,1,0:T(8,128)(2,1)}), bf16[8,256,512]{2,1,0:T(8,128)(2,1)}, u32[]{:S(2)}, u32[]{:S(2)}) async-start(bf16[8,256,512]{2,1,0:T(8,128)(2,1)} %bitcast.13), calls=%async_computation.2 | async-start | bytes 4194304 | tf_op jit(solution)/shard_map/all_to_all | solution.py:357
  66.7 4.7 %blend.4 = bf16[1024,512]{1,0:T(8,128)(2,1)S(1)} custom-call(bf16[1024,2048]{1,0:T(8,128)(2,1)} %spread.4.weight_ref, bf16[2048,512]{1,0:T(8,128)(2,1)S(1)} %bitcast.57), custom_call_target="tpu_custom_call" | custom-call | flops 4000000000 | bytes 10000000 | tf_op jit(solution)/shard_map/blend/pallas_call | solution.py:197
  72.0 1.3 collective-permute-start.4
  73.3 3.8 %collective-permute-start.9 = (bf16[1024,512]{1,0:T(8,128)(2,1)S(1)}, bf16[1024,512]{1,0:T(8,128)(2,1)}, u32[]{:S(2)}, u32[]{:S(2)}) collective-permute-start(bf16[1024,512]{1,0:T(8,128)(2,1)S(1)} %blend.4), channel_id=1, source_target_pairs={{0,2},{1,3},{6,4},{7,5},{8,10},{9,11},{14,12},{15,13},{16,18},{17,... | collective-permute-start | bytes 3145736 | tf_op jit(solution)/shard_map/ppermute | solution.py:354
  77.2 1.2 dynamic-slice_bitcast_fusion.2
  78.4 4.2 %collective-permute-start.7 = (bf16[256,768]{1,0:T(8,128)(2,1)S(1)}, bf16[256,768]{1,0:T(8,128)(2,1)S(1)}, u32[]{:S(2)}, u32[]{:S(2)}) collective-permute-start(bf16[256,768]{1,0:T(8,128)(2,1)S(1)} %get-tuple-element.112), channel_id=1, source_target_pairs={{0,6},{1,7},{2,0},{3,1},{4,2},{5,3},{6,4},{7,5},{8,14},{9,15},{10,... | collective-permute-start | bytes 1179656 | tf_op jit(solution)/shard_map/ppermute | solution.py:354
  82.6 7.4 %gather.6 = bf16[2048,512]{1,0:T(8,128)(2,1)} custom-call(s32[256,8]{1,0:T(8,128)S(1)} %copy.37.asked_ref, bf16[2048,512]{1,0:T(8,128)(2,1)} %rows_ref.7), custom_call_target="tpu_custom_call" | custom-call | flops 15000000512 | bytes 1000000 | tf_op jit(solution)/shard_map/gather/pallas_call | solution.py:150
  90.0 3.4 spread.5.weight_ref
  93.4 14.6 %collective-permute-done.7.refs_3_ = bf16[256,768]{1,0:T(8,128)(2,1)S(1)} collective-permute-done((bf16[256,768]{1,0:T(8,128)(2,1)S(1)}, bf16[256,768]{1,0:T(8,128)(2,1)S(1)}, u32[]{:S(2)}, u32[]{:S(2)}) %collective-permute-start.7) | collective-permute-done | bytes 393248 | tf_op jit(solution)/shard_map/ppermute | solution.py:354
  108.1 7.5 %collective-permute-done.6.refs_2_ = bf16[256,768]{1,0:T(8,128)(2,1)S(1)} collective-permute-done((bf16[256,768]{1,0:T(8,128)(2,1)S(1)}, bf16[256,768]{1,0:T(8,128)(2,1)S(1)}, u32[]{:S(2)}, u32[]{:S(2)}) %collective-permute-start.6) | collective-permute-done | bytes 393248 | tf_op jit(solution)/shard_map/ppermute | solution.py:354
  115.6 0.7 copy-done.13
  116.4 4.4 %all-to-all-start.3 = ((bf16[8,256,512]{2,1,0:T(8,128)(2,1)}), bf16[8,256,512]{2,1,0:T(8,128)(2,1)}, u32[]{:S(2)}, u32[]{:S(2)}) async-start(bf16[8,256,512]{2,1,0:T(8,128)(2,1)} %bitcast.18), calls=%async_computation.3 | async-start | bytes 4194304 | tf_op jit(solution)/shard_map/all_to_all | solution.py:357
  120.7 2.5 add.110
  124.0 5.4 %blend.5 = bf16[1024,512]{1,0:T(8,128)(2,1)S(1)} custom-call(bf16[1024,2048]{1,0:T(8,128)(2,1)} %spread.5.weight_ref, bf16[2048,512]{1,0:T(8,128)(2,1)} %bitcast.14.rows_ref), custom_call_target="tpu_custom_call" | custom-call | flops 4000000000 | bytes 10000000 | tf_op jit(solution)/shard_map/blend/pallas_call | solution.py:197
  129.4 9.3 %collective-permute-start.8 = (bf16[1024,512]{1,0:T(8,128)(2,1)S(1)}, bf16[1024,512]{1,0:T(8,128)(2,1)}, u32[]{:S(2)}, u32[]{:S(2)}) collective-permute-start(bf16[1024,512]{1,0:T(8,128)(2,1)S(1)} %blend.5), channel_id=1, source_target_pairs={{0,2},{1,3},{6,4},{7,5},{8,10},{9,11},{14,12},{15,13},{16,18},{17,... | collective-permute-start | bytes 3145736 | tf_op jit(solution)/shard_map/ppermute | solution.py:354
  138.8 7.4 %gather.7 = bf16[2048,512]{1,0:T(8,128)(2,1)} custom-call(s32[256,8]{1,0:T(8,128)S(1)} %copy.39.asked_ref, bf16[2048,512]{1,0:T(8,128)(2,1)} %rows_ref.7), custom_call_target="tpu_custom_call" | custom-call | flops 100000000 | bytes 1000000 | tf_op jit(solution)/shard_map/gather/pallas_call | solution.py:150
  146.2 20.3 %collective-permute-done.11.refs_0_.refs_1_.refs_2_ = bf16[1088,128]{1,0:T(8,128)(2,1)S(1)} collective-permute-done((bf16[1088,128]{1,0:T(8,128)(2,1)S(1)}, bf16[1088,128]{1,0:T(8,128)(2,1)S(1)}, u32[]{:S(2)}, u32[]{:S(2)}) %collective-permute-start.11) | collective-permute-done | bytes 278560 | tf_op jit(solution)/shard_map/ppermute | solution.py:354
  166.5 3.4 spread.6.weight_ref
  170.0 4.3 %all-to-all-start.4 = ((bf16[8,256,512]{2,1,0:T(8,128)(2,1)}), bf16[8,256,512]{2,1,0:T(8,128)(2,1)}, u32[]{:S(2)}, u32[]{:S(2)}) async-start(bf16[8,256,512]{2,1,0:T(8,128)(2,1)} %bitcast.20), calls=%async_computation.4 | async-start | bytes 4194304 | tf_op jit(solution)/shard_map/all_to_all | solution.py:357
  174.4 5.4 %blend.6 = bf16[1024,512]{1,0:T(8,128)(2,1)S(1)} custom-call(bf16[1024,2048]{1,0:T(8,128)(2,1)} %spread.6.weight_ref, bf16[2048,512]{1,0:T(8,128)(2,1)} %bitcast.19.rows_ref, bf16[1024,512]{1,0:T(8,128)(2,1)S(1)} %collective-permute-done.10.rest_0_), custom_call_target="tpu_custom_call" | custom-call | flops 4000000000 | bytes 10000000 | tf_op jit(solution)/shard_map/blend/pallas_call | solution.py:197
  179.8 2.6 collective-permute-start.12
  182.3 1.5 add.111
  184.0 0.9 collective-permute-start.13
  184.8 3.4 spread.7.weight_ref
  188.3 16.1 %encode.1 = bf16[4,256,512]{2,1,0:T(8,128)(2,1)S(1)} custom-call(bf16[256,768]{1,0:T(8,128)(2,1)S(1)} %copy-done.3, bf16[256,768]{1,0:T(8,128)(2,1)S(1)} %copy-done.10, bf16[256,768]{1,0:T(8,128)(2,1)S(1)} %copy-done.14, bf16[256,768]{1,0:T(8,128)(2,1)S(1)} %copy-done.12, f32[768]{0:T(1024)S(1)} %copy-done.17, f32[768]{0:T(1024)S(1)} %copy-done.18, ...), custom_call_target="tpu_custom_call" | custom-call | flops 15000000512 | bytes 10000000 | tf_op jit(solution)/shard_map/encode/pallas_call | solution.py:303
  204.4 1.0 copy-done.22
  206.0 7.1 %blend.7 = (bf16[1024,512]{1,0:T(8,128)(2,1)}, bf16[1024,512]{1,0:T(8,128)(2,1)}) custom-call(s32[8]{0:T(128)S(1)} %fusion.place_ref, bf16[1024,2048]{1,0:T(8,128)(2,1)} %spread.7.weight_ref, bf16[2048,512]{1,0:T(8,128)(2,1)} %bitcast.21.rows_ref, bf16[1024,512]{1,0:T(8,128)(2,1)S(1)} %collective-permute-done.12.rest_0_, ...), custom_call_target="tpu_custom_call" | custom-call | flops 4000000000 | bytes 10000000 | tf_op jit(solution)/shard_map/blend/pallas_call | solution.py:197
  213.8 8.4 %collective-permute-start.14 = (bf16[1024,512]{1,0:T(8,128)(2,1)}, bf16[1024,512]{1,0:T(8,128)(2,1)}, u32[]{:S(2)}, u32[]{:S(2)}) collective-permute-start(bf16[1024,512]{1,0:T(8,128)(2,1)} %get-tuple-element.105.refs_0_), channel_id=1, source_target_pairs={{0,2},{1,3},{2,0},{3,1},{4,6},{5,7},{6,4},{7,5},{8,10},{9,11},{10,... | collective-permute-start | bytes 3145736 | tf_op jit(solution)/shard_map/ppermute | solution.py:354
  222.2 4.5 %terms.7 = bf16[2048,512]{1,0:T(8,128)(2,1)S(1)} custom-call(bf16[1024,2048]{1,0:T(8,128)(2,1)} %spread.7.weight_ref, bf16[1024,512]{1,0:T(8,128)(2,1)} %get-tuple-element.105.refs_0_), custom_call_target="tpu_custom_call" | custom-call | flops 99999997952 | bytes 10000000 | tf_op jit(solution)/shard_map/terms/pallas_call | solution.py:220
  226.7 1.3 copy-done.1
  228.0 3.9 %all-to-all-start.5 = ((bf16[8,256,512]{2,1,0:T(8,128)(2,1)}), bf16[8,256,512]{2,1,0:T(8,128)(2,1)S(1)}, u32[]{:S(2)}, u32[]{:S(2)}) async-start(bf16[8,256,512]{2,1,0:T(8,128)(2,1)} %bitcast.60), calls=%async_computation.5 | async-start | bytes 4194304 | tf_op jit(solution)/shard_map/all_to_all | solution.py:357
  231.9 1.3 collective-permute-start.18
  233.2 12.0 %collective-permute-done.14.refs_0_ = bf16[1024,512]{1,0:T(8,128)(2,1)} collective-permute-done((bf16[1024,512]{1,0:T(8,128)(2,1)}, bf16[1024,512]{1,0:T(8,128)(2,1)}, u32[]{:S(2)}, u32[]{:S(2)}) %collective-permute-start.14) | collective-permute-done | bytes 1048608 | tf_op jit(solution)/shard_map/ppermute | solution.py:354
  245.1 1.6 collective-permute-start.15
  246.8 4.5 %terms.6 = bf16[2048,512]{1,0:T(8,128)(2,1)S(1)} custom-call(bf16[1024,2048]{1,0:T(8,128)(2,1)} %spread.6.weight_ref, bf16[1024,512]{1,0:T(8,128)(2,1)} %collective-permute-done.14.refs_0_), custom_call_target="tpu_custom_call" | custom-call | flops 99999997952 | bytes 10000000 | tf_op jit(solution)/shard_map/terms/pallas_call | solution.py:220
  251.2 1.3 copy-done
  252.5 6.0 %all-to-all-done.5 = bf16[8,256,512]{2,1,0:T(8,128)(2,1)S(1)} async-done(((bf16[8,256,512]{2,1,0:T(8,128)(2,1)}), bf16[8,256,512]{2,1,0:T(8,128)(2,1)S(1)}, u32[]{:S(2)}, u32[]{:S(2)}) %all-to-all-start.5) | async-done | bytes 2097184 | tf_op jit(solution)/shard_map/all_to_all | solution.py:357
  258.5 4.3 %all-to-all-start.6 = ((bf16[8,256,512]{2,1,0:T(8,128)(2,1)}), bf16[8,256,512]{2,1,0:T(8,128)(2,1)}, u32[]{:S(2)}, u32[]{:S(2)}) async-start(bf16[8,256,512]{2,1,0:T(8,128)(2,1)} %bitcast.59), calls=%async_computation.6 | async-start | bytes 4194304 | tf_op jit(solution)/shard_map/all_to_all | solution.py:357
  262.9 1.3 collective-permute-start.16
  264.2 4.5 %collective-permute-done.18.refs_1_ = bf16[1024,512]{1,0:T(8,128)(2,1)} collective-permute-done((bf16[1024,512]{1,0:T(8,128)(2,1)S(1)}, bf16[1024,512]{1,0:T(8,128)(2,1)}, u32[]{:S(2)}, u32[]{:S(2)}) %collective-permute-start.18) | collective-permute-done | bytes 1048608 | tf_op jit(solution)/shard_map/ppermute | solution.py:354
  268.7 5.5 %terms.5 = bf16[2048,512]{1,0:T(8,128)(2,1)} custom-call(bf16[1024,2048]{1,0:T(8,128)(2,1)} %spread.5.weight_ref, bf16[1024,512]{1,0:T(8,128)(2,1)S(1)} %collective-permute-done.17.refs_0_, bf16[1024,512]{1,0:T(8,128)(2,1)} %collective-permute-done.18.refs_1_), custom_call_target="tpu_custom_call" | custom-call | flops 99999997952 | bytes 10000000 | tf_op jit(solution)/shard_map/terms/pallas_call | solution.py:220
  274.2 15.4 %all-to-all-done.6 = bf16[8,256,512]{2,1,0:T(8,128)(2,1)} async-done(((bf16[8,256,512]{2,1,0:T(8,128)(2,1)}), bf16[8,256,512]{2,1,0:T(8,128)(2,1)}, u32[]{:S(2)}, u32[]{:S(2)}) %all-to-all-start.6) | async-done | bytes 2097184 | tf_op jit(solution)/shard_map/all_to_all | solution.py:357
  289.5 4.4 %all-to-all-start.7 = ((bf16[8,256,512]{2,1,0:T(8,128)(2,1)}), bf16[8,256,512]{2,1,0:T(8,128)(2,1)}, u32[]{:S(2)}, u32[]{:S(2)}) async-start(bf16[8,256,512]{2,1,0:T(8,128)(2,1)} %bitcast.69), calls=%async_computation.7 | async-start | bytes 4194304 | tf_op jit(solution)/shard_map/all_to_all | solution.py:357
  293.9 2.4 collective-permute-done.16.refs_1_
  296.2 5.8 %terms.4 = bf16[2048,512]{1,0:T(8,128)(2,1)} custom-call(bf16[1024,2048]{1,0:T(8,128)(2,1)} %spread.4.weight_ref, bf16[1024,512]{1,0:T(8,128)(2,1)} %collective-permute-done.15.refs_0_, bf16[1024,512]{1,0:T(8,128)(2,1)} %collective-permute-done.16.refs_1_), custom_call_target="tpu_custom_call" | custom-call | flops 99999997952 | bytes 10000000 | tf_op jit(solution)/shard_map/terms/pallas_call | solution.py:220
  302.0 18.5 %all-to-all-done.7 = bf16[8,256,512]{2,1,0:T(8,128)(2,1)} async-done(((bf16[8,256,512]{2,1,0:T(8,128)(2,1)}), bf16[8,256,512]{2,1,0:T(8,128)(2,1)}, u32[]{:S(2)}, u32[]{:S(2)}) %all-to-all-start.7) | async-done | bytes 2097184 | tf_op jit(solution)/shard_map/all_to_all | solution.py:357
  320.5 4.5 %all-to-all-start.8 = ((bf16[8,256,512]{2,1,0:T(8,128)(2,1)}), bf16[8,256,512]{2,1,0:T(8,128)(2,1)}, u32[]{:S(2)}, u32[]{:S(2)}) async-start(bf16[8,256,512]{2,1,0:T(8,128)(2,1)} %bitcast.70), calls=%async_computation.8 | async-start | bytes 4194304 | tf_op jit(solution)/shard_map/all_to_all | solution.py:357
  325.0 16.9 %add_rows.2.refs_2_ = f32[2048,512]{1,0:T(8,128)} custom-call(s32[8,256]{1,0:T(8,128)S(1)} %reshape.74.refs_0_, s32[8,256]{1,0:T(8,128)S(1)} %reshape.73.refs_1_, s32[8,256]{1,0:T(8,128)S(1)} %copy-done.7, bf16[2048,512]{1,0:T(8,128)(2,1)S(1)} %bitcast.58, bf16[2048,512]{1,0:T(8,128)(2,1)} %bitcast.27.refs_4_, bf16[2048,512]{1,0:T(8,128)(2,1)} %bitcast.29.refs_5_), custom_call_target="tpu_custom_call" | custom-call | flops 15000000512 | bytes 10000000 | tf_op jit(solution)/shard_map/add_rows/pallas_call | solution.py:259
  341.9 9.8 %all-to-all-done.8 = bf16[8,256,512]{2,1,0:T(8,128)(2,1)} async-done(((bf16[8,256,512]{2,1,0:T(8,128)(2,1)}), bf16[8,256,512]{2,1,0:T(8,128)(2,1)}, u32[]{:S(2)}, u32[]{:S(2)}) %all-to-all-start.8) | async-done | bytes 2097184 | tf_op jit(solution)/shard_map/all_to_all | solution.py:357
  351.7 8.3 %add_rows.3 = f32[2048,512]{1,0:T(8,128)} custom-call(s32[8,256]{1,0:T(8,128)S(1)} %copy-done.5, bf16[2048,512]{1,0:T(8,128)(2,1)} %bitcast.31.refs_1_, f32[2048,512]{1,0:T(8,128)} %add_rows.2.refs_2_), custom_call_target="tpu_custom_call" | custom-call | flops 5000000000 | bytes 10000000 | tf_op jit(solution)/shard_map/add_rows/pallas_call | solution.py:259
  (92 shorter events, 6.2 us)
Async XLA Ops:
  0.6 0.7 copy-start.15
  1.4 1.4 copy-start.25
  2.7 9.1 %copy-start.2 = (f32[8,4,32,128]{3,2,1,0:T(8,128)S(1)}, f32[8,4,32,128]{3,2,1,0:T(8,128)}, u32[]{:S(2)}) copy-start(f32[8,4,32,128]{3,2,1,0:T(8,128)} %param.25) | copy-start | bytes 1572868
  3.8 15.3 %collective-permute-start = (bf16[4,128,768]{2,1,0:T(8,128)(2,1)S(1)}, bf16[4,128,768]{2,1,0:T(8,128)(2,1)S(1)}, u32[]{:S(2)}, u32[]{:S(2)}) collective-permute-start(bf16[4,128,768]{2,1,0:T(8,128)(2,1)S(1)} %get-tuple-element.117), channel_id=1, source_target_pairs={{0,1},{1,0},{2,3},{3,2},{4,5},{5,4},{6,7},{7,6},{8,9},{9,8},{10,11... | collective-permute-start | bytes 2359304 | tf_op jit(solution)/shard_map/ppermute | solution.py:354
  4.9 14.2 %all-to-all-start = ((s32[32,1,256]{2,1,0:T(1,128)}), s32[32,1,256]{2,1,0:T(1,128)S(1)}, u32[]{:S(2)}, u32[]{:S(2)}) async-start(s32[32,1,256]{2,1,0:T(1,128)} %copy.31), calls=%async_computation | async-start | bytes 65536 | tf_op jit(solution)/shard_map/all_to_all | solution.py:366
  19.1 7.7 %copy-start.26 = (bf16[4,128,768]{2,1,0:T(8,128)(2,1)}, bf16[4,128,768]{2,1,0:T(8,128)(2,1)S(1)}, u32[]{:S(2)}) copy-start(bf16[4,128,768]{2,1,0:T(8,128)(2,1)S(1)} %collective-permute-done) | copy-start | bytes 2359300
  19.2 7.6 %copy-start.4 = (s32[8,256]{1,0:T(8,128)}, s32[8,256]{1,0:T(8,128)S(1)}, u32[]{:S(2)}) copy-start(s32[8,256]{1,0:T(8,128)S(1)} %reshape.71.refs_0_) | copy-start | bytes 24580
  19.2 17.9 %copy-start.6 = (s32[8,256]{1,0:T(8,128)}, s32[8,256]{1,0:T(8,128)S(1)}, u32[]{:S(2)}) copy-start(s32[8,256]{1,0:T(8,128)S(1)} %reshape.72.refs_2_) | copy-start | bytes 24580
  26.7 34.8 %all-to-all-start.1 = ((bf16[8,256,512]{2,1,0:T(8,128)(2,1)}), bf16[8,256,512]{2,1,0:T(8,128)(2,1)S(1)}, u32[]{:S(2)}, u32[]{:S(2)}) async-start(bf16[8,256,512]{2,1,0:T(8,128)(2,1)} %bitcast.8), calls=%async_computation.1 | async-start | bytes 4194304 | tf_op jit(solution)/shard_map/all_to_all | solution.py:357
  30.3 14.6 %collective-permute-start.2 = (bf16[1088,128]{1,0:T(8,128)(2,1)S(1)}, bf16[1088,128]{1,0:T(8,128)(2,1)S(1)}, u32[]{:S(2)}, u32[]{:S(2)}) collective-permute-start(bf16[1088,128]{1,0:T(8,128)(2,1)S(1)} %pad_maximum_fusion.1.refs_0_.refs_1_.refs_2_), channel_id=1, source_target_pairs={{0,4},{1,5},{6,2},{7,3},{8,12},{9,13},{14,10},{15,11},{16,20},{17,... | collective-permute-start | bytes 835592 | tf_op jit(solution)/shard_map/ppermute | solution.py:354
  32.8 15.2 %collective-permute-start.1 = (bf16[1088,128]{1,0:T(8,128)(2,1)S(1)}, bf16[1088,128]{1,0:T(8,128)(2,1)S(1)}, u32[]{:S(2)}, u32[]{:S(2)}) collective-permute-start(bf16[1088,128]{1,0:T(8,128)(2,1)S(1)} %pad_maximum_fusion.1.refs_0_.refs_1_.refs_2_), channel_id=1, source_target_pairs={{0,6},{1,7},{6,0},{7,1},{8,14},{9,15},{14,8},{15,9},{16,22},{17,23... | collective-permute-start | bytes 835592 | tf_op jit(solution)/shard_map/ppermute | solution.py:354
  37.3 7.5 %copy-start.24 = (bf16[4,128,768]{2,1,0:T(8,128)(2,1)S(1)}, bf16[4,128,768]{2,1,0:T(8,128)(2,1)}, u32[]{:S(2)}) copy-start(bf16[4,128,768]{2,1,0:T(8,128)(2,1)} %get-tuple-element.116) | copy-start | bytes 2359300
  37.3 7.5 %copy-start.27 = (bf16[4,128,768]{2,1,0:T(8,128)(2,1)S(1)}, bf16[4,128,768]{2,1,0:T(8,128)(2,1)}, u32[]{:S(2)}) copy-start(bf16[4,128,768]{2,1,0:T(8,128)(2,1)} %copy-done.26) | copy-start | bytes 2359300
  44.9 4.0 %copy-start.23 = (bf16[4,256,768]{2,1,0:T(8,128)(2,1)}, bf16[4,256,768]{2,1,0:T(8,128)(2,1)S(1)}, u32[]{:S(2)}) copy-start(bf16[4,256,768]{2,1,0:T(8,128)(2,1)S(1)} %pad_maximum_fusion) | copy-start | bytes 4718596
  48.9 12.6 %collective-permute-start.3 = (bf16[256,768]{1,0:T(8,128)(2,1)}, bf16[256,768]{1,0:T(8,128)(2,1)S(1)}, u32[]{:S(2)}, u32[]{:S(2)}) collective-permute-start(bf16[256,768]{1,0:T(8,128)(2,1)} %get-tuple-element.114), channel_id=1, source_target_pairs={{0,2},{1,3},{2,4},{3,5},{4,6},{5,7},{6,0},{7,1},{8,10},{9,11},{10,... | collective-permute-start | bytes 1179656 | tf_op jit(solution)/shard_map/ppermute | solution.py:354
  61.5 0.8 copy-start.9
  62.3 53.3 %all-to-all-start.2 = ((bf16[8,256,512]{2,1,0:T(8,128)(2,1)}), bf16[8,256,512]{2,1,0:T(8,128)(2,1)}, u32[]{:S(2)}, u32[]{:S(2)}) async-start(bf16[8,256,512]{2,1,0:T(8,128)(2,1)} %bitcast.13), calls=%async_computation.2 | async-start | bytes 4194304 | tf_op jit(solution)/shard_map/all_to_all | solution.py:357
  71.4 18.6 %collective-permute-start.5 = (bf16[1088,128]{1,0:T(8,128)(2,1)S(1)}, bf16[1088,128]{1,0:T(8,128)(2,1)S(1)}, u32[]{:S(2)}, u32[]{:S(2)}) collective-permute-start(bf16[1088,128]{1,0:T(8,128)(2,1)S(1)} %pad_maximum_fusion.1.refs_0_.refs_1_.refs_2_), channel_id=1, source_target_pairs={{2,4},{3,5},{4,2},{5,3},{10,12},{11,13},{12,10},{13,11},{18,20},{1... | collective-permute-start | bytes 835592 | tf_op jit(solution)/shard_map/ppermute | solution.py:354
  72.0 18.0 %collective-permute-start.4 = (bf16[1088,128]{1,0:T(8,128)(2,1)S(1)}, bf16[1088,128]{1,0:T(8,128)(2,1)S(1)}, u32[]{:S(2)}, u32[]{:S(2)}) collective-permute-start(bf16[1088,128]{1,0:T(8,128)(2,1)S(1)} %pad_maximum_fusion.1.refs_0_.refs_1_.refs_2_), channel_id=1, source_target_pairs={{2,6},{3,7},{4,0},{5,1},{10,14},{11,15},{12,8},{13,9},{18,22},{19,... | collective-permute-start | bytes 835592 | tf_op jit(solution)/shard_map/ppermute | solution.py:354
  73.3 47.4 %collective-permute-start.9 = (bf16[1024,512]{1,0:T(8,128)(2,1)S(1)}, bf16[1024,512]{1,0:T(8,128)(2,1)}, u32[]{:S(2)}, u32[]{:S(2)}) collective-permute-start(bf16[1024,512]{1,0:T(8,128)(2,1)S(1)} %blend.4), channel_id=1, source_target_pairs={{0,2},{1,3},{6,4},{7,5},{8,10},{9,11},{14,12},{15,13},{16,18},{17,... | collective-permute-start | bytes 3145736 | tf_op jit(solution)/shard_map/ppermute | solution.py:354
  78.4 29.7 %collective-permute-start.7 = (bf16[256,768]{1,0:T(8,128)(2,1)S(1)}, bf16[256,768]{1,0:T(8,128)(2,1)S(1)}, u32[]{:S(2)}, u32[]{:S(2)}) collective-permute-start(bf16[256,768]{1,0:T(8,128)(2,1)S(1)} %get-tuple-element.112), channel_id=1, source_target_pairs={{0,6},{1,7},{2,0},{3,1},{4,2},{5,3},{6,4},{7,5},{8,14},{9,15},{10,... | collective-permute-start | bytes 1179656 | tf_op jit(solution)/shard_map/ppermute | solution.py:354
  82.6 33.0 %collective-permute-start.6 = (bf16[256,768]{1,0:T(8,128)(2,1)S(1)}, bf16[256,768]{1,0:T(8,128)(2,1)S(1)}, u32[]{:S(2)}, u32[]{:S(2)}) collective-permute-start(bf16[256,768]{1,0:T(8,128)(2,1)S(1)} %get-tuple-element.113), channel_id=1, source_target_pairs={{0,4},{1,5},{2,6},{3,7},{4,0},{5,1},{6,2},{7,3},{8,12},{9,13},{10,... | collective-permute-start | bytes 1179656 | tf_op jit(solution)/shard_map/ppermute | solution.py:354
  108.1 7.6 %copy-start.11 = (bf16[256,768]{1,0:T(8,128)(2,1)}, bf16[256,768]{1,0:T(8,128)(2,1)S(1)}, u32[]{:S(2)}) copy-start(bf16[256,768]{1,0:T(8,128)(2,1)S(1)} %collective-permute-done.7.refs_3_) | copy-start | bytes 1179652
  115.6 0.7 copy-start.13
  116.4 53.6 %all-to-all-start.3 = ((bf16[8,256,512]{2,1,0:T(8,128)(2,1)}), bf16[8,256,512]{2,1,0:T(8,128)(2,1)}, u32[]{:S(2)}, u32[]{:S(2)}) async-start(bf16[8,256,512]{2,1,0:T(8,128)(2,1)} %bitcast.18), calls=%async_computation.3 | async-start | bytes 4194304 | tf_op jit(solution)/shard_map/all_to_all | solution.py:357
  123.2 46.7 %collective-permute-start.10 = (bf16[1024,512]{1,0:T(8,128)(2,1)}, bf16[1024,512]{1,0:T(8,128)(2,1)S(1)}, u32[]{:S(2)}, u32[]{:S(2)}) collective-permute-start(bf16[1024,512]{1,0:T(8,128)(2,1)} %add.110), channel_id=1, source_target_pairs={{2,4},{3,5},{4,2},{5,3},{10,12},{11,13},{12,10},{13,11},{18,20},{1... | collective-permute-start | bytes 3145736 | tf_op jit(solution)/shard_map/ppermute | solution.py:354
  129.4 53.0 %collective-permute-start.8 = (bf16[1024,512]{1,0:T(8,128)(2,1)S(1)}, bf16[1024,512]{1,0:T(8,128)(2,1)}, u32[]{:S(2)}, u32[]{:S(2)}) collective-permute-start(bf16[1024,512]{1,0:T(8,128)(2,1)S(1)} %blend.5), channel_id=1, source_target_pairs={{0,2},{1,3},{6,4},{7,5},{8,10},{9,11},{14,12},{15,13},{16,18},{17,... | collective-permute-start | bytes 3145736 | tf_op jit(solution)/shard_map/ppermute | solution.py:354
  138.6 27.9 %collective-permute-start.11 = (bf16[1088,128]{1,0:T(8,128)(2,1)S(1)}, bf16[1088,128]{1,0:T(8,128)(2,1)S(1)}, u32[]{:S(2)}, u32[]{:S(2)}) collective-permute-start(bf16[1088,128]{1,0:T(8,128)(2,1)S(1)} %pad_maximum_fusion.1.refs_0_.refs_1_.refs_2_), channel_id=1, source_target_pairs={{0,2},{1,3},{2,0},{3,1},{4,6},{5,7},{6,4},{7,5},{8,10},{9,11},{10,... | collective-permute-start | bytes 835592 | tf_op jit(solution)/shard_map/ppermute | solution.py:354
  170.0 36.0 %all-to-all-start.4 = ((bf16[8,256,512]{2,1,0:T(8,128)(2,1)}), bf16[8,256,512]{2,1,0:T(8,128)(2,1)}, u32[]{:S(2)}, u32[]{:S(2)}) async-start(bf16[8,256,512]{2,1,0:T(8,128)(2,1)} %bitcast.20), calls=%async_computation.4 | async-start | bytes 4194304 | tf_op jit(solution)/shard_map/all_to_all | solution.py:357
  179.8 26.2 %collective-permute-start.12 = (bf16[1024,512]{1,0:T(8,128)(2,1)S(1)}, bf16[1024,512]{1,0:T(8,128)(2,1)S(1)}, u32[]{:S(2)}, u32[]{:S(2)}) collective-permute-start(bf16[1024,512]{1,0:T(8,128)(2,1)S(1)} %blend.6), channel_id=1, source_target_pairs={{0,2},{1,3},{2,0},{3,1},{4,6},{5,7},{6,4},{7,5},{8,10},{9,11},{10,... | collective-permute-start | bytes 3145736 | tf_op jit(solution)/shard_map/ppermute | solution.py:354
  183.8 4.3 %copy-start.3 = (bf16[256,768]{1,0:T(8,128)(2,1)S(1)}, bf16[256,768]{1,0:T(8,128)(2,1)}, u32[]{:S(2)}) copy-start(bf16[256,768]{1,0:T(8,128)(2,1)} %get-tuple-element.100.refs_0_) | copy-start | bytes 1179652
  183.9 4.3 %copy-start.8 = (bf16[768,512]{1,0:T(8,128)(2,1)S(1)}, bf16[768,512]{1,0:T(8,128)(2,1)}, u32[]{:S(2)}) copy-start(bf16[768,512]{1,0:T(8,128)(2,1)} %refs_12_.1) | copy-start | bytes 2359300
  183.9 4.3 %copy-start.10 = (bf16[256,768]{1,0:T(8,128)(2,1)S(1)}, bf16[256,768]{1,0:T(8,128)(2,1)}, u32[]{:S(2)}) copy-start(bf16[256,768]{1,0:T(8,128)(2,1)} %copy-done.9) | copy-start | bytes 1179652
  183.9 4.3 %copy-start.12 = (bf16[256,768]{1,0:T(8,128)(2,1)S(1)}, bf16[256,768]{1,0:T(8,128)(2,1)}, u32[]{:S(2)}) copy-start(bf16[256,768]{1,0:T(8,128)(2,1)} %copy-done.11) | copy-start | bytes 1179652
  183.9 4.3 %copy-start.14 = (bf16[256,768]{1,0:T(8,128)(2,1)S(1)}, bf16[256,768]{1,0:T(8,128)(2,1)}, u32[]{:S(2)}) copy-start(bf16[256,768]{1,0:T(8,128)(2,1)} %copy-done.13) | copy-start | bytes 1179652
  183.9 4.3 %copy-start.16 = (f32[3072]{0:T(1024)S(1)}, f32[3072]{0:T(1024)}, u32[]{:S(2)}) copy-start(f32[3072]{0:T(1024)} %refs_7_.1) | copy-start | bytes 36868
  183.9 4.3 %copy-start.17 = (f32[768]{0:T(1024)S(1)}, f32[768]{0:T(1024)}, u32[]{:S(2)}) copy-start(f32[768]{0:T(1024)} %refs_4_.1) | copy-start | bytes 9220
  183.9 4.3 %copy-start.18 = (f32[768]{0:T(1024)S(1)}, f32[768]{0:T(1024)}, u32[]{:S(2)}) copy-start(f32[768]{0:T(1024)} %refs_5_.1) | copy-start | bytes 9220
  183.9 4.3 %copy-start.19 = (f32[768]{0:T(1024)S(1)}, f32[768]{0:T(1024)}, u32[]{:S(2)}) copy-start(f32[768]{0:T(1024)} %refs_9_.1) | copy-start | bytes 9220
  183.9 4.3 %copy-start.20 = (f32[768]{0:T(1024)S(1)}, f32[768]{0:T(1024)}, u32[]{:S(2)}) copy-start(f32[768]{0:T(1024)} %refs_10_.1) | copy-start | bytes 9220
  184.0 4.3 %copy-start.21 = (f32[768]{0:T(1024)S(1)}, f32[768]{0:T(1024)}, u32[]{:S(2)}) copy-start(f32[768]{0:T(1024)} %refs_11_.1) | copy-start | bytes 9220
  184.0 21.5 %collective-permute-start.13 = (bf16[1024,512]{1,0:T(8,128)(2,1)S(1)}, bf16[1024,512]{1,0:T(8,128)(2,1)S(1)}, u32[]{:S(2)}, u32[]{:S(2)}) collective-permute-start(bf16[1024,512]{1,0:T(8,128)(2,1)S(1)} %add.111), channel_id=1, source_target_pairs={{2,4},{3,5},{4,2},{5,3},{10,12},{11,13},{12,10},{13,11},{18,20},{1... | collective-permute-start | bytes 3145736 | tf_op jit(solution)/shard_map/ppermute | solution.py:354
  204.4 1.0 copy-start.22
  213.1 18.8 %collective-permute-start.17 = (bf16[1024,512]{1,0:T(8,128)(2,1)}, bf16[1024,512]{1,0:T(8,128)(2,1)S(1)}, u32[]{:S(2)}, u32[]{:S(2)}) collective-permute-start(bf16[1024,512]{1,0:T(8,128)(2,1)} %get-tuple-element.105.refs_0_), channel_id=1, source_target_pairs={{2,4},{3,5},{4,2},{5,3},{10,12},{11,13},{12,10},{13,11},{18,20},{1... | collective-permute-start | bytes 3145736 | tf_op jit(solution)/shard_map/ppermute | solution.py:354
  213.8 31.3 %collective-permute-start.14 = (bf16[1024,512]{1,0:T(8,128)(2,1)}, bf16[1024,512]{1,0:T(8,128)(2,1)}, u32[]{:S(2)}, u32[]{:S(2)}) collective-permute-start(bf16[1024,512]{1,0:T(8,128)(2,1)} %get-tuple-element.105.refs_0_), channel_id=1, source_target_pairs={{0,2},{1,3},{2,0},{3,1},{4,6},{5,7},{6,4},{7,5},{8,10},{9,11},{10,... | collective-permute-start | bytes 3145736 | tf_op jit(solution)/shard_map/ppermute | solution.py:354
  226.7 1.3 copy-start.1
  228.0 30.5 %all-to-all-start.5 = ((bf16[8,256,512]{2,1,0:T(8,128)(2,1)}), bf16[8,256,512]{2,1,0:T(8,128)(2,1)S(1)}, u32[]{:S(2)}, u32[]{:S(2)}) async-start(bf16[8,256,512]{2,1,0:T(8,128)(2,1)} %bitcast.60), calls=%async_computation.5 | async-start | bytes 4194304 | tf_op jit(solution)/shard_map/all_to_all | solution.py:357
  231.9 36.8 %collective-permute-start.18 = (bf16[1024,512]{1,0:T(8,128)(2,1)S(1)}, bf16[1024,512]{1,0:T(8,128)(2,1)}, u32[]{:S(2)}, u32[]{:S(2)}) collective-permute-start(bf16[1024,512]{1,0:T(8,128)(2,1)S(1)} %collective-permute-done.17.refs_0_), channel_id=1, source_target_pairs={{2,0},{3,1},{4,6},{5,7},{10,8},{11,9},{12,14},{13,15},{18,16},{19,... | collective-permute-start | bytes 3145736 | tf_op jit(solution)/shard_map/ppermute | solution.py:354
  245.1 17.7 %collective-permute-start.15 = (bf16[1024,512]{1,0:T(8,128)(2,1)}, bf16[1024,512]{1,0:T(8,128)(2,1)}, u32[]{:S(2)}, u32[]{:S(2)}) collective-permute-start(bf16[1024,512]{1,0:T(8,128)(2,1)} %collective-permute-done.14.refs_0_), channel_id=1, source_target_pairs={{2,4},{3,5},{4,2},{5,3},{10,12},{11,13},{12,10},{13,11},{18,20},{1... | collective-permute-start | bytes 3145736 | tf_op jit(solution)/shard_map/ppermute | solution.py:354
  251.2 1.3 copy-start
  258.5 31.0 %all-to-all-start.6 = ((bf16[8,256,512]{2,1,0:T(8,128)(2,1)}), bf16[8,256,512]{2,1,0:T(8,128)(2,1)}, u32[]{:S(2)}, u32[]{:S(2)}) async-start(bf16[8,256,512]{2,1,0:T(8,128)(2,1)} %bitcast.59), calls=%async_computation.6 | async-start | bytes 4194304 | tf_op jit(solution)/shard_map/all_to_all | solution.py:357
  262.9 33.4 %collective-permute-start.16 = (bf16[1024,512]{1,0:T(8,128)(2,1)}, bf16[1024,512]{1,0:T(8,128)(2,1)}, u32[]{:S(2)}, u32[]{:S(2)}) collective-permute-start(bf16[1024,512]{1,0:T(8,128)(2,1)} %collective-permute-done.15.refs_0_), channel_id=1, source_target_pairs={{2,0},{3,1},{4,6},{5,7},{10,8},{11,9},{12,14},{13,15},{18,16},{19,... | collective-permute-start | bytes 3145736 | tf_op jit(solution)/shard_map/ppermute | solution.py:354
  289.5 31.0 %all-to-all-start.7 = ((bf16[8,256,512]{2,1,0:T(8,128)(2,1)}), bf16[8,256,512]{2,1,0:T(8,128)(2,1)}, u32[]{:S(2)}, u32[]{:S(2)}) async-start(bf16[8,256,512]{2,1,0:T(8,128)(2,1)} %bitcast.69), calls=%async_computation.7 | async-start | bytes 4194304 | tf_op jit(solution)/shard_map/all_to_all | solution.py:357
  320.5 4.5 %copy-start.7 = (s32[8,256]{1,0:T(8,128)S(1)}, s32[8,256]{1,0:T(8,128)}, u32[]{:S(2)}) copy-start(s32[8,256]{1,0:T(8,128)} %copy-done.6) | copy-start | bytes 24580
  320.5 31.1 %all-to-all-start.8 = ((bf16[8,256,512]{2,1,0:T(8,128)(2,1)}), bf16[8,256,512]{2,1,0:T(8,128)(2,1)}, u32[]{:S(2)}, u32[]{:S(2)}) async-start(bf16[8,256,512]{2,1,0:T(8,128)(2,1)} %bitcast.70), calls=%async_computation.8 | async-start | bytes 4194304 | tf_op jit(solution)/shard_map/all_to_all | solution.py:357
  325.0 26.6 %copy-start.5 = (s32[8,256]{1,0:T(8,128)S(1)}, s32[8,256]{1,0:T(8,128)}, u32[]{:S(2)}) copy-start(s32[8,256]{1,0:T(8,128)} %copy-done.4) | copy-start | bytes 24580

commit v3 on v0

--- a/solution.py
+++ b/solution.py
@@ -415,8 +415,9 @@
     )
 
     rows_3 = exchange(looked_3)
+    spread_2 = spread_of(near_to_outer, near_to_inner)
+    part_1, moved_1, spread_2 = tie(part_1, moved_1, spread_2)
     far = move(part_1 + moved_1, middle)
-    spread_2 = spread_of(near_to_outer, near_to_inner)
     part_2 = blend(spread_2, rows_2)
     moved_2 = move(part_2, inwards)
     part_2, lists[3], from_beside = tie(part_2, lists[3], from_beside)

time: 324 us -> 325 us (level)
    ppermute x19, waiting for transfers between devices: 34.6 us -> 40.9 us  [move(): return lax.ppermute(x, 'tile', pairs)]
    all_to_all x8, waiting for transfers between devices: 53.9 us -> 49 us  [exchange(): lax.all_to_all(x, both, split_axis=0, concat_axis=0, axis_index_groups=gr...]
  transfers between devices with their start and end apart: 28 -> 28, of which waited for: 9 -> 11; matrix products, arithmetic and copies ran while one was open for 3% -> 2% of each run, Pallas kernels for 33% -> 33%
where the time goes in v3:
time: 325 us; the launch traced here: 323 us
  Pallas kernels  130 us (40%)
  waiting for transfers between devices  96.4 us (30%)
  starting transfers between devices  81.7 us (25%)
  other arithmetic  6.93 us (2%)
  local copies, waits for them, and re-layouts  6.67 us (2%)
    all_to_all x8, waiting for transfers between devices, exchange(): lax.all_to_all(x, both, split_axis=0, concat_axis=0, axis_index_groups=gr...  49 us
    ppermute x19, waiting for transfers between devices, move(): return lax.ppermute(x, 'tile', pairs)  40.9 us
    ppermute x19, starting transfers between devices, move(): return lax.ppermute(x, 'tile', pairs)  40.7 us
    all_to_all x8, starting transfers between devices, exchange(): lax.all_to_all(x, both, split_axis=0, concat_axis=0, axis_index_groups=gr...  34.1 us
    pallas_call x4, Pallas kernels, gather(): pl.pallas_call(functools.partial(gather_kernel, group, cap), grid=(near /...  29.7 us
    pallas_call x2, Pallas kernels, add_rows(): pl.pallas_call(functools.partial(add_rows_kernel, count), grid=(held // b...  25.2 us
    pallas_call x4, Pallas kernels, blend(): pl.pallas_call(functools.partial(last_blend_kernel if last else blend_ker...  23.3 us
    pallas_call x4, Pallas kernels, terms(): pl.pallas_call(terms_kernel, grid=(slots // block,), in_specs=[pl.BlockSp...  20.2 us
  transfers between devices with their start and end apart: 28, of which 11 were waited for; matrix products, arithmetic and copies ran while one was open for 2% of the time, Pallas kernels for 33%

profile of v3, /device:TPU:0, one launch (start us, length us, event | category | flops | bytes accessed | tf_op | source)
XLA Modules:
  0.0 323.3 jit_solution(2482422385663591694)
XLA Ops:
  0.7 0.7 copy-done.6
  1.4 1.3 index.1
  2.8 1.0 dynamic-slice_bitcast_fusion
  4.9 7.0 %all-to-all-start = ((s32[32,1,256]{2,1,0:T(1,128)}), s32[32,1,256]{2,1,0:T(1,128)S(1)}, u32[]{:S(2)}, u32[]{:S(2)}) async-start(s32[32,1,256]{2,1,0:T(1,128)} %copy.31), calls=%async_computation | async-start | bytes 65536 | tf_op jit(solution)/shard_map/all_to_all | solution.py:366
  11.8 0.7 weights.1
  12.6 6.5 %all-to-all-done = s32[32,1,256]{2,1,0:T(1,128)S(1)} async-done(((s32[32,1,256]{2,1,0:T(1,128)}), s32[32,1,256]{2,1,0:T(1,128)S(1)}, u32[]{:S(2)}, u32[]{:S(2)}) %all-to-all-start) | async-done | bytes 32800 | tf_op jit(solution)/shard_map/all_to_all | solution.py:366
  19.3 7.5 %gather.4 = bf16[2048,512]{1,0:T(8,128)(2,1)} custom-call(s32[256,8]{1,0:T(8,128)S(1)} %copy.33.asked_ref, bf16[2048,512]{1,0:T(8,128)(2,1)} %rows_ref.7), custom_call_target="tpu_custom_call" | custom-call | flops 100000000 | bytes 1000000 | tf_op jit(solution)/shard_map/gather/pallas_call | solution.py:150
  26.8 3.6 %all-to-all-start.1 = ((bf16[8,256,512]{2,1,0:T(8,128)(2,1)}), bf16[8,256,512]{2,1,0:T(8,128)(2,1)S(1)}, u32[]{:S(2)}, u32[]{:S(2)}) async-start(bf16[8,256,512]{2,1,0:T(8,128)(2,1)} %bitcast.8), calls=%async_computation.1 | async-start | bytes 4194304 | tf_op jit(solution)/shard_map/all_to_all | solution.py:357
  30.4 2.4 collective-permute-start.2
  32.8 4.3 %collective-permute-start.1 = (bf16[1088,128]{1,0:T(8,128)(2,1)S(1)}, bf16[1088,128]{1,0:T(8,128)(2,1)S(1)}, u32[]{:S(2)}, u32[]{:S(2)}) collective-permute-start(bf16[1088,128]{1,0:T(8,128)(2,1)S(1)} %pad_maximum_fusion.refs_0_.refs_1_.refs_2_), channel_id=1, source_target_pairs={{0,6},{1,7},{6,0},{7,1},{8,14},{9,15},{14,8},{15,9},{16,22},{17,23... | collective-permute-start | bytes 835592 | tf_op jit(solution)/shard_map/ppermute | solution.py:354
  37.3 2.5 fusion.1
  39.9 1.4 collective-permute-start.5
  42.0 7.4 %gather.5 = bf16[2048,512]{1,0:T(8,128)(2,1)} custom-call(s32[256,8]{1,0:T(8,128)S(1)} %copy.35.asked_ref, bf16[2048,512]{1,0:T(8,128)(2,1)} %rows_ref.7), custom_call_target="tpu_custom_call" | custom-call | flops 100000000 | bytes 1000000 | tf_op jit(solution)/shard_map/gather/pallas_call | solution.py:150
  49.6 7.4 %gather.6 = bf16[2048,512]{1,0:T(8,128)(2,1)} custom-call(s32[256,8]{1,0:T(8,128)S(1)} %copy.37.asked_ref, bf16[2048,512]{1,0:T(8,128)(2,1)} %rows_ref.7), custom_call_target="tpu_custom_call" | custom-call | flops 100000000 | bytes 1000000 | tf_op jit(solution)/shard_map/gather/pallas_call | solution.py:150
  57.0 3.4 %spread.4.weight_ref = bf16[1024,2048]{1,0:T(8,128)(2,1)} custom-call(s32[8]{0:T(128)S(1)} %add.99.base_ref, bf16[1088,128]{1,0:T(8,128)(2,1)S(1)} %collective-permute-done.1.refs_0_.refs_1_.refs_2_, bf16[1088,128]{1,0:T(8,128)(2,1)S(1)} %collective-permute-done.1.refs_0_.refs_1_.refs_2_, ...), custom_call_target="tpu_custom_call" | custom-call | flops 100000000 | bytes 1000000 | tf_op jit(solution)/shard_map/spread/pallas_call | solution.py:120
  60.4 3.7 %collective-permute-start.8 = (bf16[1088,128]{1,0:T(8,128)(2,1)S(1)}, bf16[1088,128]{1,0:T(8,128)(2,1)S(1)}, u32[]{:S(2)}, u32[]{:S(2)}) collective-permute-start(bf16[1088,128]{1,0:T(8,128)(2,1)S(1)} %pad_maximum_fusion.refs_0_.refs_1_.refs_2_), channel_id=1, source_target_pairs={{0,2},{1,3},{2,0},{3,1},{4,6},{5,7},{6,4},{7,5},{8,10},{9,11},{10,... | collective-permute-start | bytes 835592 | tf_op jit(solution)/shard_map/ppermute | solution.py:354
  64.1 0.7 collective-permute-start.7
  64.8 4.4 %all-to-all-start.2 = ((bf16[8,256,512]{2,1,0:T(8,128)(2,1)}), bf16[8,256,512]{2,1,0:T(8,128)(2,1)}, u32[]{:S(2)}, u32[]{:S(2)}) async-start(bf16[8,256,512]{2,1,0:T(8,128)(2,1)} %bitcast.10), calls=%async_computation.2 | async-start | bytes 4194304 | tf_op jit(solution)/shard_map/all_to_all | solution.py:357
  69.3 5.5 %blend.4 = bf16[1024,512]{1,0:T(8,128)(2,1)} custom-call(bf16[1024,2048]{1,0:T(8,128)(2,1)} %spread.4.weight_ref, bf16[2048,512]{1,0:T(8,128)(2,1)S(1)} %bitcast.57), custom_call_target="tpu_custom_call" | custom-call | flops 4000000000 | bytes 10000000 | tf_op jit(solution)/shard_map/blend/pallas_call | solution.py:197
  74.8 1.3 collective-permute-start.6
  76.1 4.7 %collective-permute-start.9 = (bf16[1024,512]{1,0:T(8,128)(2,1)}, bf16[1024,512]{1,0:T(8,128)(2,1)}, u32[]{:S(2)}, u32[]{:S(2)}) collective-permute-start(bf16[1024,512]{1,0:T(8,128)(2,1)} %blend.4), channel_id=1, source_target_pairs={{0,2},{1,3},{6,4},{7,5},{8,10},{9,11},{14,12},{15,13},{16,18},{17,... | collective-permute-start | bytes 3145736 | tf_op jit(solution)/shard_map/ppermute | solution.py:354
  80.8 1.1 collective-permute-done.4.refs_2_
  82.0 16.5 %encode.1 = bf16[4,256,512]{2,1,0:T(8,128)(2,1)S(1)} custom-call(bf16[256,768]{1,0:T(8,128)(2,1)S(1)} %get-tuple-element.71.refs_0_, bf16[256,768]{1,0:T(8,128)(2,1)} %collective-permute-done.3.refs_1_, bf16[256,768]{1,0:T(8,128)(2,1)} %collective-permute-done.4.refs_2_, bf16[256,768]{1,0:T(8,128)(2,1)} %collective-permute-done.5.refs_3_, ...), custom_call_target="tpu_custom_call" | custom-call | flops 99999997952 | bytes 10000000 | tf_op jit(solution)/shard_map/encode/pallas_call | solution.py:303
  98.5 0.9 copy-done.13
  99.5 4.6 %all-to-all-start.3 = ((bf16[8,256,512]{2,1,0:T(8,128)(2,1)}), bf16[8,256,512]{2,1,0:T(8,128)(2,1)}, u32[]{:S(2)}, u32[]{:S(2)}) async-start(bf16[8,256,512]{2,1,0:T(8,128)(2,1)} %bitcast.18), calls=%async_computation.3 | async-start | bytes 4194304 | tf_op jit(solution)/shard_map/all_to_all | solution.py:357
  104.0 3.4 %spread.5.weight_ref = bf16[1024,2048]{1,0:T(8,128)(2,1)} custom-call(s32[8]{0:T(128)S(1)} %add.99.base_ref, bf16[1088,128]{1,0:T(8,128)(2,1)S(1)} %collective-permute-done.6.refs_0_.refs_1_.refs_2_, bf16[1088,128]{1,0:T(8,128)(2,1)S(1)} %collective-permute-done.6.refs_0_.refs_1_.refs_2_, ...), custom_call_target="tpu_custom_call" | custom-call | flops 100000000 | bytes 1000000 | tf_op jit(solution)/shard_map/spread/pallas_call | solution.py:120
  107.5 2.8 add.110
  110.2 1.6 collective-permute-start.11
  111.9 5.4 %blend.5 = bf16[1024,512]{1,0:T(8,128)(2,1)S(1)} custom-call(bf16[1024,2048]{1,0:T(8,128)(2,1)} %spread.5.weight_ref, bf16[2048,512]{1,0:T(8,128)(2,1)} %bitcast.11.rows_ref), custom_call_target="tpu_custom_call" | custom-call | flops 4000000000 | bytes 10000000 | tf_op jit(solution)/shard_map/blend/pallas_call | solution.py:197
  117.3 3.3 %collective-permute-start.10 = (bf16[1024,512]{1,0:T(8,128)(2,1)S(1)}, bf16[1024,512]{1,0:T(8,128)(2,1)}, u32[]{:S(2)}, u32[]{:S(2)}) collective-permute-start(bf16[1024,512]{1,0:T(8,128)(2,1)S(1)} %blend.5), channel_id=1, source_target_pairs={{0,2},{1,3},{6,4},{7,5},{8,10},{9,11},{14,12},{15,13},{16,18},{17,... | collective-permute-start | bytes 3145736 | tf_op jit(solution)/shard_map/ppermute | solution.py:354
  120.7 7.4 %gather.7 = bf16[2048,512]{1,0:T(8,128)(2,1)} custom-call(s32[256,8]{1,0:T(8,128)S(1)} %copy.39.asked_ref, bf16[2048,512]{1,0:T(8,128)(2,1)} %rows_ref.7), custom_call_target="tpu_custom_call" | custom-call | flops 100000000 | bytes 1000000 | tf_op jit(solution)/shard_map/gather/pallas_call | solution.py:150
  128.1 3.4 %spread.6.weight_ref = bf16[1024,2048]{1,0:T(8,128)(2,1)} custom-call(s32[8]{0:T(128)S(1)} %add.99.base_ref, bf16[1088,128]{1,0:T(8,128)(2,1)S(1)} %collective-permute-done.8.refs_0_.refs_1_.refs_2_, bf16[1088,128]{1,0:T(8,128)(2,1)S(1)} %collective-permute-done.8.refs_0_.refs_1_.refs_2_, bf16[1088,128]{1,0:T(8,128)(2,1)S(1)} %collective-permute-done.8.refs_0_.refs_1_.refs_2_), custom_call_target="tpu_custom_call" | custom-call | flops 100000000 | bytes 1000000 | tf_op jit(solution)/shard_map/spread/pallas_call | solution.py:120
  131.5 4.4 %all-to-all-start.4 = ((bf16[8,256,512]{2,1,0:T(8,128)(2,1)}), bf16[8,256,512]{2,1,0:T(8,128)(2,1)}, u32[]{:S(2)}, u32[]{:S(2)}) async-start(bf16[8,256,512]{2,1,0:T(8,128)(2,1)} %bitcast.20), calls=%async_computation.4 | async-start | bytes 4194304 | tf_op jit(solution)/shard_map/all_to_all | solution.py:357
  135.9 5.5 %blend.6 = bf16[1024,512]{1,0:T(8,128)(2,1)S(1)} custom-call(bf16[1024,2048]{1,0:T(8,128)(2,1)} %spread.6.weight_ref, bf16[2048,512]{1,0:T(8,128)(2,1)} %bitcast.19.rows_ref, bf16[1024,512]{1,0:T(8,128)(2,1)} %collective-permute-done.11.rest_0_), custom_call_target="tpu_custom_call" | custom-call | flops 4000000000 | bytes 10000000 | tf_op jit(solution)/shard_map/blend/pallas_call | solution.py:197
  142.0 1.5 add.111
  143.5 0.7 collective-permute-start.13
  144.2 7.0 %collective-permute-start.12 = (bf16[1024,512]{1,0:T(8,128)(2,1)S(1)}, bf16[1024,512]{1,0:T(8,128)(2,1)S(1)}, u32[]{:S(2)}, u32[]{:S(2)}) collective-permute-start(bf16[1024,512]{1,0:T(8,128)(2,1)S(1)} %blend.6), channel_id=1, source_target_pairs={{0,2},{1,3},{2,0},{3,1},{4,6},{5,7},{6,4},{7,5},{8,10},{9,11},{10,... | collective-permute-start | bytes 3145736 | tf_op jit(solution)/shard_map/ppermute | solution.py:354
  151.2 3.3 %spread.7.weight_ref = bf16[1024,2048]{1,0:T(8,128)(2,1)} custom-call(s32[8]{0:T(128)S(1)} %add.99.base_ref, bf16[1088,128]{1,0:T(8,128)(2,1)S(1)} %pad_maximum_fusion.refs_0_.refs_1_.refs_2_, bf16[1088,128]{1,0:T(8,128)(2,1)S(1)} %pad_maximum_fusion.refs_0_.refs_1_.refs_2_, bf16[1088,128]{1,0:T(8,128)(2,1)S(1)} %pad_maximum_fusion.refs_0_.refs_1_.refs_2_), custom_call_target="tpu_custom_call" | custom-call | flops 100000000 | bytes 1000000 | tf_op jit(solution)/shard_map/spread/pallas_call | solution.py:120
  154.6 20.0 %collective-permute-done.12.rest_0_ = bf16[1024,512]{1,0:T(8,128)(2,1)S(1)} collective-permute-done((bf16[1024,512]{1,0:T(8,128)(2,1)S(1)}, bf16[1024,512]{1,0:T(8,128)(2,1)S(1)}, u32[]{:S(2)}, u32[]{:S(2)}) %collective-permute-start.12) | collective-permute-done | bytes 1048608 | tf_op jit(solution)/shard_map/ppermute | solution.py:354
  174.6 6.8 %blend.7 = (bf16[1024,512]{1,0:T(8,128)(2,1)}, bf16[1024,512]{1,0:T(8,128)(2,1)}) custom-call(s32[8]{0:T(128)S(1)} %fusion.8.place_ref, bf16[1024,2048]{1,0:T(8,128)(2,1)} %spread.7.weight_ref, bf16[2048,512]{1,0:T(8,128)(2,1)} %bitcast.21.rows_ref, bf16[1024,512]{1,0:T(8,128)(2,1)S(1)} %collective-permute-done.12.rest_0_, ...), custom_call_target="tpu_custom_call" | custom-call | flops 4000000000 | bytes 10000000 | tf_op jit(solution)/shard_map/blend/pallas_call | solution.py:197
  181.4 0.7 collective-permute-start.17
  182.1 3.5 %collective-permute-start.14 = (bf16[1024,512]{1,0:T(8,128)(2,1)}, bf16[1024,512]{1,0:T(8,128)(2,1)}, u32[]{:S(2)}, u32[]{:S(2)}) collective-permute-start(bf16[1024,512]{1,0:T(8,128)(2,1)} %get-tuple-element.99.refs_0_), channel_id=1, source_target_pairs={{0,2},{1,3},{2,0},{3,1},{4,6},{5,7},{6,4},{7,5},{8,10},{9,11},{10,... | collective-permute-start | bytes 3145736 | tf_op jit(solution)/shard_map/ppermute | solution.py:354
  185.7 4.5 %terms.7 = bf16[2048,512]{1,0:T(8,128)(2,1)S(1)} custom-call(bf16[1024,2048]{1,0:T(8,128)(2,1)} %spread.7.weight_ref, bf16[1024,512]{1,0:T(8,128)(2,1)} %get-tuple-element.99.refs_0_), custom_call_target="tpu_custom_call" | custom-call | flops 99999997952 | bytes 10000000 | tf_op jit(solution)/shard_map/terms/pallas_call | solution.py:220
  190.1 1.3 copy-done.1
  191.4 3.9 %all-to-all-start.5 = ((bf16[8,256,512]{2,1,0:T(8,128)(2,1)}), bf16[8,256,512]{2,1,0:T(8,128)(2,1)S(1)}, u32[]{:S(2)}, u32[]{:S(2)}) async-start(bf16[8,256,512]{2,1,0:T(8,128)(2,1)} %bitcast.60), calls=%async_computation.5 | async-start | bytes 4194304 | tf_op jit(solution)/shard_map/all_to_all | solution.py:357
  195.3 1.3 collective-permute-start.18
  196.6 11.6 %collective-permute-done.14.refs_0_ = bf16[1024,512]{1,0:T(8,128)(2,1)} collective-permute-done((bf16[1024,512]{1,0:T(8,128)(2,1)}, bf16[1024,512]{1,0:T(8,128)(2,1)}, u32[]{:S(2)}, u32[]{:S(2)}) %collective-permute-start.14) | collective-permute-done | bytes 1048608 | tf_op jit(solution)/shard_map/ppermute | solution.py:354
  208.2 1.7 collective-permute-start.15
  209.9 4.5 %terms.6 = bf16[2048,512]{1,0:T(8,128)(2,1)S(1)} custom-call(bf16[1024,2048]{1,0:T(8,128)(2,1)} %spread.6.weight_ref, bf16[1024,512]{1,0:T(8,128)(2,1)} %collective-permute-done.14.refs_0_), custom_call_target="tpu_custom_call" | custom-call | flops 99999997952 | bytes 10000000 | tf_op jit(solution)/shard_map/terms/pallas_call | solution.py:220
  214.4 1.3 copy-done
  215.7 6.3 %all-to-all-done.5 = bf16[8,256,512]{2,1,0:T(8,128)(2,1)S(1)} async-done(((bf16[8,256,512]{2,1,0:T(8,128)(2,1)}), bf16[8,256,512]{2,1,0:T(8,128)(2,1)S(1)}, u32[]{:S(2)}, u32[]{:S(2)}) %all-to-all-start.5) | async-done | bytes 2097184 | tf_op jit(solution)/shard_map/all_to_all | solution.py:357
  222.0 4.3 %all-to-all-start.6 = ((bf16[8,256,512]{2,1,0:T(8,128)(2,1)}), bf16[8,256,512]{2,1,0:T(8,128)(2,1)}, u32[]{:S(2)}, u32[]{:S(2)}) async-start(bf16[8,256,512]{2,1,0:T(8,128)(2,1)} %bitcast.59), calls=%async_computation.6 | async-start | bytes 4194304 | tf_op jit(solution)/shard_map/all_to_all | solution.py:357
  226.3 1.3 collective-permute-start.16
  227.6 5.0 %collective-permute-done.18.refs_1_ = bf16[1024,512]{1,0:T(8,128)(2,1)} collective-permute-done((bf16[1024,512]{1,0:T(8,128)(2,1)S(1)}, bf16[1024,512]{1,0:T(8,128)(2,1)}, u32[]{:S(2)}, u32[]{:S(2)}) %collective-permute-start.18) | collective-permute-done | bytes 1048608 | tf_op jit(solution)/shard_map/ppermute | solution.py:354
  232.6 5.5 %terms.5 = bf16[2048,512]{1,0:T(8,128)(2,1)} custom-call(bf16[1024,2048]{1,0:T(8,128)(2,1)} %spread.5.weight_ref, bf16[1024,512]{1,0:T(8,128)(2,1)S(1)} %collective-permute-done.17.refs_0_, bf16[1024,512]{1,0:T(8,128)(2,1)} %collective-permute-done.18.refs_1_), custom_call_target="tpu_custom_call" | custom-call | flops 99999997952 | bytes 10000000 | tf_op jit(solution)/shard_map/terms/pallas_call | solution.py:220
  238.2 14.8 %all-to-all-done.6 = bf16[8,256,512]{2,1,0:T(8,128)(2,1)} async-done(((bf16[8,256,512]{2,1,0:T(8,128)(2,1)}), bf16[8,256,512]{2,1,0:T(8,128)(2,1)}, u32[]{:S(2)}, u32[]{:S(2)}) %all-to-all-start.6) | async-done | bytes 2097184 | tf_op jit(solution)/shard_map/all_to_all | solution.py:357
  253.0 4.3 %all-to-all-start.7 = ((bf16[8,256,512]{2,1,0:T(8,128)(2,1)}), bf16[8,256,512]{2,1,0:T(8,128)(2,1)}, u32[]{:S(2)}, u32[]{:S(2)}) async-start(bf16[8,256,512]{2,1,0:T(8,128)(2,1)} %bitcast.69), calls=%async_computation.7 | async-start | bytes 4194304 | tf_op jit(solution)/shard_map/all_to_all | solution.py:357
  257.3 2.6 collective-permute-done.16.refs_1_
  259.9 5.7 %terms.4 = bf16[2048,512]{1,0:T(8,128)(2,1)} custom-call(bf16[1024,2048]{1,0:T(8,128)(2,1)} %spread.4.weight_ref, bf16[1024,512]{1,0:T(8,128)(2,1)} %collective-permute-done.15.refs_0_, bf16[1024,512]{1,0:T(8,128)(2,1)} %collective-permute-done.16.refs_1_), custom_call_target="tpu_custom_call" | custom-call | flops 99999997952 | bytes 10000000 | tf_op jit(solution)/shard_map/terms/pallas_call | solution.py:220
  265.6 18.4 %all-to-all-done.7 = bf16[8,256,512]{2,1,0:T(8,128)(2,1)} async-done(((bf16[8,256,512]{2,1,0:T(8,128)(2,1)}), bf16[8,256,512]{2,1,0:T(8,128)(2,1)}, u32[]{:S(2)}, u32[]{:S(2)}) %all-to-all-start.7) | async-done | bytes 2097184 | tf_op jit(solution)/shard_map/all_to_all | solution.py:357
  284.0 4.6 %all-to-all-start.8 = ((bf16[8,256,512]{2,1,0:T(8,128)(2,1)}), bf16[8,256,512]{2,1,0:T(8,128)(2,1)}, u32[]{:S(2)}, u32[]{:S(2)}) async-start(bf16[8,256,512]{2,1,0:T(8,128)(2,1)} %bitcast.70), calls=%async_computation.8 | async-start | bytes 4194304 | tf_op jit(solution)/shard_map/all_to_all | solution.py:357
  288.6 16.9 %add_rows.2.refs_2_ = f32[2048,512]{1,0:T(8,128)} custom-call(s32[8,256]{1,0:T(8,128)S(1)} %reshape.74.refs_0_, s32[8,256]{1,0:T(8,128)S(1)} %reshape.73.refs_1_, s32[8,256]{1,0:T(8,128)S(1)} %reshape.72.refs_2_, bf16[2048,512]{1,0:T(8,128)(2,1)S(1)} %bitcast.58, bf16[2048,512]{1,0:T(8,128)(2,1)} %bitcast.27.refs_4_, bf16[2048,512]{1,0:T(8,128)(2,1)} %bitcast.29.refs_5_), custom_call_target="tpu_custom_call" | custom-call | flops 15000000512 | bytes 10000000 | tf_op jit(solution)/shard_map/add_rows/pallas_call | solution.py:259
  305.5 9.5 %all-to-all-done.8 = bf16[8,256,512]{2,1,0:T(8,128)(2,1)} async-done(((bf16[8,256,512]{2,1,0:T(8,128)(2,1)}), bf16[8,256,512]{2,1,0:T(8,128)(2,1)}, u32[]{:S(2)}, u32[]{:S(2)}) %all-to-all-start.8) | async-done | bytes 2097184 | tf_op jit(solution)/shard_map/all_to_all | solution.py:357
  315.0 8.3 %add_rows.3 = f32[2048,512]{1,0:T(8,128)} custom-call(s32[8,256]{1,0:T(8,128)S(1)} %copy-done.4, bf16[2048,512]{1,0:T(8,128)(2,1)} %bitcast.31.refs_1_, f32[2048,512]{1,0:T(8,128)} %add_rows.2.refs_2_), custom_call_target="tpu_custom_call" | custom-call | flops 5000000000 | bytes 10000000 | tf_op jit(solution)/shard_map/add_rows/pallas_call | solution.py:259
  (66 shorter events, 3.2 us)
Async XLA Ops:
  0.6 0.7 copy-start.6
  1.4 1.4 copy-start.14
  2.7 9.1 %copy-start.2 = (f32[8,4,32,128]{3,2,1,0:T(8,128)S(1)}, f32[8,4,32,128]{3,2,1,0:T(8,128)}, u32[]{:S(2)}) copy-start(f32[8,4,32,128]{3,2,1,0:T(8,128)} %param.25) | copy-start | bytes 1572868
  3.8 15.3 %collective-permute-start = (bf16[4,128,768]{2,1,0:T(8,128)(2,1)S(1)}, bf16[4,128,768]{2,1,0:T(8,128)(2,1)S(1)}, u32[]{:S(2)}, u32[]{:S(2)}) collective-permute-start(bf16[4,128,768]{2,1,0:T(8,128)(2,1)S(1)} %get-tuple-element.111), channel_id=1, source_target_pairs={{0,1},{1,0},{2,3},{3,2},{4,5},{5,4},{6,7},{7,6},{8,9},{9,8},{10,11... | collective-permute-start | bytes 2359304 | tf_op jit(solution)/shard_map/ppermute | solution.py:354
  4.9 14.2 %all-to-all-start = ((s32[32,1,256]{2,1,0:T(1,128)}), s32[32,1,256]{2,1,0:T(1,128)S(1)}, u32[]{:S(2)}, u32[]{:S(2)}) async-start(s32[32,1,256]{2,1,0:T(1,128)} %copy.31), calls=%async_computation | async-start | bytes 65536 | tf_op jit(solution)/shard_map/all_to_all | solution.py:366
  19.1 7.7 %copy-start.15 = (bf16[4,128,768]{2,1,0:T(8,128)(2,1)}, bf16[4,128,768]{2,1,0:T(8,128)(2,1)S(1)}, u32[]{:S(2)}) copy-start(bf16[4,128,768]{2,1,0:T(8,128)(2,1)S(1)} %collective-permute-done) | copy-start | bytes 2359300
  19.2 7.7 %copy-start.3 = (s32[8,256]{1,0:T(8,128)}, s32[8,256]{1,0:T(8,128)S(1)}, u32[]{:S(2)}) copy-start(s32[8,256]{1,0:T(8,128)S(1)} %reshape.71.refs_0_) | copy-start | bytes 24580
  26.8 33.6 %all-to-all-start.1 = ((bf16[8,256,512]{2,1,0:T(8,128)(2,1)}), bf16[8,256,512]{2,1,0:T(8,128)(2,1)S(1)}, u32[]{:S(2)}, u32[]{:S(2)}) async-start(bf16[8,256,512]{2,1,0:T(8,128)(2,1)} %bitcast.8), calls=%async_computation.1 | async-start | bytes 4194304 | tf_op jit(solution)/shard_map/all_to_all | solution.py:357
  30.4 26.6 %collective-permute-start.2 = (bf16[1088,128]{1,0:T(8,128)(2,1)S(1)}, bf16[1088,128]{1,0:T(8,128)(2,1)S(1)}, u32[]{:S(2)}, u32[]{:S(2)}) collective-permute-start(bf16[1088,128]{1,0:T(8,128)(2,1)S(1)} %pad_maximum_fusion.refs_0_.refs_1_.refs_2_), channel_id=1, source_target_pairs={{0,4},{1,5},{6,2},{7,3},{8,12},{9,13},{14,10},{15,11},{16,20},{17,... | collective-permute-start | bytes 835592 | tf_op jit(solution)/shard_map/ppermute | solution.py:354
  32.8 24.2 %collective-permute-start.1 = (bf16[1088,128]{1,0:T(8,128)(2,1)S(1)}, bf16[1088,128]{1,0:T(8,128)(2,1)S(1)}, u32[]{:S(2)}, u32[]{:S(2)}) collective-permute-start(bf16[1088,128]{1,0:T(8,128)(2,1)S(1)} %pad_maximum_fusion.refs_0_.refs_1_.refs_2_), channel_id=1, source_target_pairs={{0,6},{1,7},{6,0},{7,1},{8,14},{9,15},{14,8},{15,9},{16,22},{17,23... | collective-permute-start | bytes 835592 | tf_op jit(solution)/shard_map/ppermute | solution.py:354
  39.9 34.9 %collective-permute-start.5 = (bf16[256,768]{1,0:T(8,128)(2,1)}, bf16[256,768]{1,0:T(8,128)(2,1)}, u32[]{:S(2)}, u32[]{:S(2)}) collective-permute-start(bf16[256,768]{1,0:T(8,128)(2,1)} %get-tuple-element.106), channel_id=1, source_target_pairs={{0,6},{1,7},{2,0},{3,1},{4,2},{5,3},{6,4},{7,5},{8,14},{9,15},{10,... | collective-permute-start | bytes 1179656 | tf_op jit(solution)/shard_map/ppermute | solution.py:354
  41.3 34.8 %collective-permute-start.3 = (bf16[256,768]{1,0:T(8,128)(2,1)}, bf16[256,768]{1,0:T(8,128)(2,1)}, u32[]{:S(2)}, u32[]{:S(2)}) collective-permute-start(bf16[256,768]{1,0:T(8,128)(2,1)} %get-tuple-element.108), channel_id=1, source_target_pairs={{0,2},{1,3},{2,4},{3,5},{4,6},{5,7},{6,0},{7,1},{8,10},{9,11},{10,... | collective-permute-start | bytes 1179656 | tf_op jit(solution)/shard_map/ppermute | solution.py:354
  41.9 40.1 %collective-permute-start.4 = (bf16[256,768]{1,0:T(8,128)(2,1)}, bf16[256,768]{1,0:T(8,128)(2,1)}, u32[]{:S(2)}, u32[]{:S(2)}) collective-permute-start(bf16[256,768]{1,0:T(8,128)(2,1)} %get-tuple-element.109), channel_id=1, source_target_pairs={{0,4},{1,5},{2,6},{3,7},{4,0},{5,1},{6,2},{7,3},{8,12},{9,13},{10,... | collective-permute-start | bytes 1179656 | tf_op jit(solution)/shard_map/ppermute | solution.py:354
  60.4 38.1 %collective-permute-start.8 = (bf16[1088,128]{1,0:T(8,128)(2,1)S(1)}, bf16[1088,128]{1,0:T(8,128)(2,1)S(1)}, u32[]{:S(2)}, u32[]{:S(2)}) collective-permute-start(bf16[1088,128]{1,0:T(8,128)(2,1)S(1)} %pad_maximum_fusion.refs_0_.refs_1_.refs_2_), channel_id=1, source_target_pairs={{0,2},{1,3},{2,0},{3,1},{4,6},{5,7},{6,4},{7,5},{8,10},{9,11},{10,... | collective-permute-start | bytes 835592 | tf_op jit(solution)/shard_map/ppermute | solution.py:354
  64.1 34.4 %collective-permute-start.7 = (bf16[1088,128]{1,0:T(8,128)(2,1)S(1)}, bf16[1088,128]{1,0:T(8,128)(2,1)S(1)}, u32[]{:S(2)}, u32[]{:S(2)}) collective-permute-start(bf16[1088,128]{1,0:T(8,128)(2,1)S(1)} %pad_maximum_fusion.refs_0_.refs_1_.refs_2_), channel_id=1, source_target_pairs={{2,4},{3,5},{4,2},{5,3},{10,12},{11,13},{12,10},{13,11},{18,20},{1... | collective-permute-start | bytes 835592 | tf_op jit(solution)/shard_map/ppermute | solution.py:354
  64.8 33.7 %all-to-all-start.2 = ((bf16[8,256,512]{2,1,0:T(8,128)(2,1)}), bf16[8,256,512]{2,1,0:T(8,128)(2,1)}, u32[]{:S(2)}, u32[]{:S(2)}) async-start(bf16[8,256,512]{2,1,0:T(8,128)(2,1)} %bitcast.10), calls=%async_computation.2 | async-start | bytes 4194304 | tf_op jit(solution)/shard_map/all_to_all | solution.py:357
  69.2 12.8 %copy-start.5 = (bf16[768,512]{1,0:T(8,128)(2,1)S(1)}, bf16[768,512]{1,0:T(8,128)(2,1)}, u32[]{:S(2)}) copy-start(bf16[768,512]{1,0:T(8,128)(2,1)} %refs_12_.1) | copy-start | bytes 2359300
  69.2 12.8 %copy-start.7 = (f32[3072]{0:T(1024)S(1)}, f32[3072]{0:T(1024)}, u32[]{:S(2)}) copy-start(f32[3072]{0:T(1024)} %refs_7_.1) | copy-start | bytes 36868
  69.2 12.7 %copy-start.8 = (f32[768]{0:T(1024)S(1)}, f32[768]{0:T(1024)}, u32[]{:S(2)}) copy-start(f32[768]{0:T(1024)} %refs_4_.1) | copy-start | bytes 9220
  69.2 12.7 %copy-start.9 = (f32[768]{0:T(1024)S(1)}, f32[768]{0:T(1024)}, u32[]{:S(2)}) copy-start(f32[768]{0:T(1024)} %refs_5_.1) | copy-start | bytes 9220
  69.2 12.7 %copy-start.10 = (f32[768]{0:T(1024)S(1)}, f32[768]{0:T(1024)}, u32[]{:S(2)}) copy-start(f32[768]{0:T(1024)} %refs_9_.1) | copy-start | bytes 9220
  69.2 12.7 %copy-start.11 = (f32[768]{0:T(1024)S(1)}, f32[768]{0:T(1024)}, u32[]{:S(2)}) copy-start(f32[768]{0:T(1024)} %refs_10_.1) | copy-start | bytes 9220
  69.3 12.7 %copy-start.12 = (f32[768]{0:T(1024)S(1)}, f32[768]{0:T(1024)}, u32[]{:S(2)}) copy-start(f32[768]{0:T(1024)} %refs_11_.1) | copy-start | bytes 9220
  74.8 23.7 %collective-permute-start.6 = (bf16[1088,128]{1,0:T(8,128)(2,1)S(1)}, bf16[1088,128]{1,0:T(8,128)(2,1)S(1)}, u32[]{:S(2)}, u32[]{:S(2)}) collective-permute-start(bf16[1088,128]{1,0:T(8,128)(2,1)S(1)} %pad_maximum_fusion.refs_0_.refs_1_.refs_2_), channel_id=1, source_target_pairs={{2,6},{3,7},{4,0},{5,1},{10,14},{11,15},{12,8},{13,9},{18,22},{19,... | collective-permute-start | bytes 835592 | tf_op jit(solution)/shard_map/ppermute | solution.py:354
  76.1 31.4 %collective-permute-start.9 = (bf16[1024,512]{1,0:T(8,128)(2,1)}, bf16[1024,512]{1,0:T(8,128)(2,1)}, u32[]{:S(2)}, u32[]{:S(2)}) collective-permute-start(bf16[1024,512]{1,0:T(8,128)(2,1)} %blend.4), channel_id=1, source_target_pairs={{0,2},{1,3},{6,4},{7,5},{8,10},{9,11},{14,12},{15,13},{16,18},{17,... | collective-permute-start | bytes 3145736 | tf_op jit(solution)/shard_map/ppermute | solution.py:354
  98.5 1.0 copy-start.13
  99.5 32.1 %all-to-all-start.3 = ((bf16[8,256,512]{2,1,0:T(8,128)(2,1)}), bf16[8,256,512]{2,1,0:T(8,128)(2,1)}, u32[]{:S(2)}, u32[]{:S(2)}) async-start(bf16[8,256,512]{2,1,0:T(8,128)(2,1)} %bitcast.18), calls=%async_computation.3 | async-start | bytes 4194304 | tf_op jit(solution)/shard_map/all_to_all | solution.py:357
  110.2 21.3 %collective-permute-start.11 = (bf16[1024,512]{1,0:T(8,128)(2,1)}, bf16[1024,512]{1,0:T(8,128)(2,1)}, u32[]{:S(2)}, u32[]{:S(2)}) collective-permute-start(bf16[1024,512]{1,0:T(8,128)(2,1)} %add.110), channel_id=1, source_target_pairs={{2,4},{3,5},{4,2},{5,3},{10,12},{11,13},{12,10},{13,11},{18,20},{1... | collective-permute-start | bytes 3145736 | tf_op jit(solution)/shard_map/ppermute | solution.py:354
  117.3 24.7 %collective-permute-start.10 = (bf16[1024,512]{1,0:T(8,128)(2,1)S(1)}, bf16[1024,512]{1,0:T(8,128)(2,1)}, u32[]{:S(2)}, u32[]{:S(2)}) collective-permute-start(bf16[1024,512]{1,0:T(8,128)(2,1)S(1)} %blend.5), channel_id=1, source_target_pairs={{0,2},{1,3},{6,4},{7,5},{8,10},{9,11},{14,12},{15,13},{16,18},{17,... | collective-permute-start | bytes 3145736 | tf_op jit(solution)/shard_map/ppermute | solution.py:354
  131.5 43.1 %all-to-all-start.4 = ((bf16[8,256,512]{2,1,0:T(8,128)(2,1)}), bf16[8,256,512]{2,1,0:T(8,128)(2,1)}, u32[]{:S(2)}, u32[]{:S(2)}) async-start(bf16[8,256,512]{2,1,0:T(8,128)(2,1)} %bitcast.20), calls=%async_computation.4 | async-start | bytes 4194304 | tf_op jit(solution)/shard_map/all_to_all | solution.py:357
  143.5 11.0 %collective-permute-start.13 = (bf16[1024,512]{1,0:T(8,128)(2,1)S(1)}, bf16[1024,512]{1,0:T(8,128)(2,1)S(1)}, u32[]{:S(2)}, u32[]{:S(2)}) collective-permute-start(bf16[1024,512]{1,0:T(8,128)(2,1)S(1)} %add.111), channel_id=1, source_target_pairs={{2,4},{3,5},{4,2},{5,3},{10,12},{11,13},{12,10},{13,11},{18,20},{1... | collective-permute-start | bytes 3145736 | tf_op jit(solution)/shard_map/ppermute | solution.py:354
  144.2 30.3 %collective-permute-start.12 = (bf16[1024,512]{1,0:T(8,128)(2,1)S(1)}, bf16[1024,512]{1,0:T(8,128)(2,1)S(1)}, u32[]{:S(2)}, u32[]{:S(2)}) collective-permute-start(bf16[1024,512]{1,0:T(8,128)(2,1)S(1)} %blend.6), channel_id=1, source_target_pairs={{0,2},{1,3},{2,0},{3,1},{4,6},{5,7},{6,4},{7,5},{8,10},{9,11},{10,... | collective-permute-start | bytes 3145736 | tf_op jit(solution)/shard_map/ppermute | solution.py:354
  181.4 13.9 %collective-permute-start.17 = (bf16[1024,512]{1,0:T(8,128)(2,1)}, bf16[1024,512]{1,0:T(8,128)(2,1)S(1)}, u32[]{:S(2)}, u32[]{:S(2)}) collective-permute-start(bf16[1024,512]{1,0:T(8,128)(2,1)} %get-tuple-element.99.refs_0_), channel_id=1, source_target_pairs={{2,4},{3,5},{4,2},{5,3},{10,12},{11,13},{12,10},{13,11},{18,20},{1... | collective-permute-start | bytes 3145736 | tf_op jit(solution)/shard_map/ppermute | solution.py:354
  182.1 26.1 %collective-permute-start.14 = (bf16[1024,512]{1,0:T(8,128)(2,1)}, bf16[1024,512]{1,0:T(8,128)(2,1)}, u32[]{:S(2)}, u32[]{:S(2)}) collective-permute-start(bf16[1024,512]{1,0:T(8,128)(2,1)} %get-tuple-element.99.refs_0_), channel_id=1, source_target_pairs={{0,2},{1,3},{2,0},{3,1},{4,6},{5,7},{6,4},{7,5},{8,10},{9,11},{10,... | collective-permute-start | bytes 3145736 | tf_op jit(solution)/shard_map/ppermute | solution.py:354
  190.1 1.3 copy-start.1
  191.4 30.5 %all-to-all-start.5 = ((bf16[8,256,512]{2,1,0:T(8,128)(2,1)}), bf16[8,256,512]{2,1,0:T(8,128)(2,1)S(1)}, u32[]{:S(2)}, u32[]{:S(2)}) async-start(bf16[8,256,512]{2,1,0:T(8,128)(2,1)} %bitcast.60), calls=%async_computation.5 | async-start | bytes 4194304 | tf_op jit(solution)/shard_map/all_to_all | solution.py:357
  195.3 37.3 %collective-permute-start.18 = (bf16[1024,512]{1,0:T(8,128)(2,1)S(1)}, bf16[1024,512]{1,0:T(8,128)(2,1)}, u32[]{:S(2)}, u32[]{:S(2)}) collective-permute-start(bf16[1024,512]{1,0:T(8,128)(2,1)S(1)} %collective-permute-done.17.refs_0_), channel_id=1, source_target_pairs={{2,0},{3,1},{4,6},{5,7},{10,8},{11,9},{12,14},{13,15},{18,16},{19,... | collective-permute-start | bytes 3145736 | tf_op jit(solution)/shard_map/ppermute | solution.py:354
  208.2 18.1 %collective-permute-start.15 = (bf16[1024,512]{1,0:T(8,128)(2,1)}, bf16[1024,512]{1,0:T(8,128)(2,1)}, u32[]{:S(2)}, u32[]{:S(2)}) collective-permute-start(bf16[1024,512]{1,0:T(8,128)(2,1)} %collective-permute-done.14.refs_0_), channel_id=1, source_target_pairs={{2,4},{3,5},{4,2},{5,3},{10,12},{11,13},{12,10},{13,11},{18,20},{1... | collective-permute-start | bytes 3145736 | tf_op jit(solution)/shard_map/ppermute | solution.py:354
  214.4 1.3 copy-start
  222.0 31.0 %all-to-all-start.6 = ((bf16[8,256,512]{2,1,0:T(8,128)(2,1)}), bf16[8,256,512]{2,1,0:T(8,128)(2,1)}, u32[]{:S(2)}, u32[]{:S(2)}) async-start(bf16[8,256,512]{2,1,0:T(8,128)(2,1)} %bitcast.59), calls=%async_computation.6 | async-start | bytes 4194304 | tf_op jit(solution)/shard_map/all_to_all | solution.py:357
  226.3 33.5 %collective-permute-start.16 = (bf16[1024,512]{1,0:T(8,128)(2,1)}, bf16[1024,512]{1,0:T(8,128)(2,1)}, u32[]{:S(2)}, u32[]{:S(2)}) collective-permute-start(bf16[1024,512]{1,0:T(8,128)(2,1)} %collective-permute-done.15.refs_0_), channel_id=1, source_target_pairs={{2,0},{3,1},{4,6},{5,7},{10,8},{11,9},{12,14},{13,15},{18,16},{19,... | collective-permute-start | bytes 3145736 | tf_op jit(solution)/shard_map/ppermute | solution.py:354
  253.0 31.0 %all-to-all-start.7 = ((bf16[8,256,512]{2,1,0:T(8,128)(2,1)}), bf16[8,256,512]{2,1,0:T(8,128)(2,1)}, u32[]{:S(2)}, u32[]{:S(2)}) async-start(bf16[8,256,512]{2,1,0:T(8,128)(2,1)} %bitcast.69), calls=%async_computation.7 | async-start | bytes 4194304 | tf_op jit(solution)/shard_map/all_to_all | solution.py:357
  284.0 31.0 %all-to-all-start.8 = ((bf16[8,256,512]{2,1,0:T(8,128)(2,1)}), bf16[8,256,512]{2,1,0:T(8,128)(2,1)}, u32[]{:S(2)}, u32[]{:S(2)}) async-start(bf16[8,256,512]{2,1,0:T(8,128)(2,1)} %bitcast.70), calls=%async_computation.8 | async-start | bytes 4194304 | tf_op jit(solution)/shard_map/all_to_all | solution.py:357
  288.6 26.4 %copy-start.4 = (s32[8,256]{1,0:T(8,128)S(1)}, s32[8,256]{1,0:T(8,128)}, u32[]{:S(2)}) copy-start(s32[8,256]{1,0:T(8,128)} %copy-done.3) | copy-start | bytes 24580

commit v4 on v0

--- a/solution.py
+++ b/solution.py
@@ -27,10 +27,10 @@
     every = jnp.ones((length, length), BF16)
     peer_id = lax.broadcasted_iota(I32, (peers, length), 0)
     slot_id = lax.broadcasted_iota(I32, (cap, length), 0)
-    hots = []
+    hots, owners, ranks = [], [], []
     for t in range(tiles):
         owner = ids_ref[t : t + 1, :] // rows_held
-        own_ref[t : t + 1, :] = owner.astype(F32).astype(BF16)
+        owners.append(owner.astype(F32))
         hots.append((jnp.broadcast_to(owner, (peers, length)) == peer_id).astype(F32))
     stack = jnp.concatenate(hots, 0).astype(BF16)
     within = jnp.dot(stack, upper, preferred_element_type=F32)
@@ -41,7 +41,7 @@
         own_rows = slice(t * peers, (t + 1) * peers)
         rank = jnp.sum(hots[t] * (within[own_rows] + offset), axis=0, keepdims=True).astype(I32)
         offset = offset + totals[own_rows]
-        rank_ref[t : t + 1, :] = rank.astype(F32).astype(BF16)
+        ranks.append(rank.astype(F32))
         ids = ids_ref[t : t + 1, :]
         row = ids - (ids // rows_held) * rows_held + 1
         high = (row >> 6).astype(F32)
@@ -49,6 +49,8 @@
         digits = jnp.concatenate([hots[t] * high, hots[t] * low], 0).astype(BF16)
         slots = (jnp.broadcast_to(rank, (cap, length)) == slot_id).astype(F32).astype(BF16)
         found = found + lax.dot_general(digits, slots, LANES, preferred_element_type=F32)
+    own_ref[...] = jnp.concatenate(owners, 0).astype(BF16)
+    rank_ref[...] = jnp.concatenate(ranks, 0).astype(BF16)
     req_ref[...] = (found[:peers] * 64.0 + found[peers:]).astype(I32) - 1
 
 

time: 324 us -> 324 us (level)
  no operation moved by 1% of the time
where the time goes in v4:
time: 324 us; the launch traced here: 322 us
  Pallas kernels  130 us (40%)
  waiting for transfers between devices  95 us (29%)
  starting transfers between devices  82.1 us (25%)
  other arithmetic  6.98 us (2%)
  local copies, waits for them, and re-layouts  6.74 us (2%)
    all_to_all x8, waiting for transfers between devices, exchange(): lax.all_to_all(x, both, split_axis=0, concat_axis=0, axis_index_groups=gr...  53.9 us
    ppermute x19, starting transfers between devices, move(): return lax.ppermute(x, 'tile', pairs)  41.3 us
    ppermute x19, waiting for transfers between devices, move(): return lax.ppermute(x, 'tile', pairs)  34.6 us
    all_to_all x8, starting transfers between devices, exchange(): lax.all_to_all(x, both, split_axis=0, concat_axis=0, axis_index_groups=gr...  33.9 us
    pallas_call x4, Pallas kernels, gather(): pl.pallas_call(functools.partial(gather_kernel, group, cap), grid=(near /...  29.7 us
    pallas_call x2, Pallas kernels, add_rows(): pl.pallas_call(functools.partial(add_rows_kernel, count), grid=(held // b...  25.2 us
    pallas_call x4, Pallas kernels, blend(): pl.pallas_call(functools.partial(last_blend_kernel if last else blend_ker...  23.3 us
    pallas_call x4, Pallas kernels, terms(): pl.pallas_call(terms_kernel, grid=(slots // block,), in_specs=[pl.BlockSp...  20.2 us
  transfers between devices with their start and end apart: 28, of which 9 were waited for; matrix products, arithmetic and copies ran while one was open for 3% of the time, Pallas kernels for 33%

profile of v4, /device:TPU:0, one launch (start us, length us, event | category | flops | bytes accessed | tf_op | source)
XLA Modules:
  0.0 322.3 jit_solution(2271866790127791009)
XLA Ops:
  0.7 0.7 copy-done.6
  1.4 1.2 index.1
  2.8 1.0 dynamic-slice_bitcast_fusion
  4.2 0.6 copy.31
  4.9 7.0 %all-to-all-start = ((s32[32,1,256]{2,1,0:T(1,128)}), s32[32,1,256]{2,1,0:T(1,128)S(1)}, u32[]{:S(2)}, u32[]{:S(2)}) async-start(s32[32,1,256]{2,1,0:T(1,128)} %copy.31), calls=%async_computation | async-start | bytes 65536 | tf_op jit(solution)/shard_map/all_to_all | solution.py:368
  11.8 0.7 weights.1
  12.6 6.5 %all-to-all-done = s32[32,1,256]{2,1,0:T(1,128)S(1)} async-done(((s32[32,1,256]{2,1,0:T(1,128)}), s32[32,1,256]{2,1,0:T(1,128)S(1)}, u32[]{:S(2)}, u32[]{:S(2)}) %all-to-all-start) | async-done | bytes 32800 | tf_op jit(solution)/shard_map/all_to_all | solution.py:368
  19.3 7.5 %gather.4 = bf16[2048,512]{1,0:T(8,128)(2,1)} custom-call(s32[256,8]{1,0:T(8,128)S(1)} %copy.33.asked_ref, bf16[2048,512]{1,0:T(8,128)(2,1)} %rows_ref.7), custom_call_target="tpu_custom_call" | custom-call | flops 100000000 | bytes 1000000 | tf_op jit(solution)/shard_map/gather/pallas_call | solution.py:152
  26.8 3.6 %all-to-all-start.1 = ((bf16[8,256,512]{2,1,0:T(8,128)(2,1)}), bf16[8,256,512]{2,1,0:T(8,128)(2,1)S(1)}, u32[]{:S(2)}, u32[]{:S(2)}) async-start(bf16[8,256,512]{2,1,0:T(8,128)(2,1)} %bitcast.8), calls=%async_computation.1 | async-start | bytes 4194304 | tf_op jit(solution)/shard_map/all_to_all | solution.py:359
  30.4 2.4 collective-permute-start.2
  32.8 4.3 %collective-permute-start.1 = (bf16[1088,128]{1,0:T(8,128)(2,1)S(1)}, bf16[1088,128]{1,0:T(8,128)(2,1)S(1)}, u32[]{:S(2)}, u32[]{:S(2)}) collective-permute-start(bf16[1088,128]{1,0:T(8,128)(2,1)S(1)} %pad_maximum_fusion.refs_0_.refs_1_.refs_2_), channel_id=1, source_target_pairs={{0,6},{1,7},{6,0},{7,1},{8,14},{9,15},{14,8},{15,9},{16,22},{17,23... | collective-permute-start | bytes 835592 | tf_op jit(solution)/shard_map/ppermute | solution.py:356
  37.3 2.6 fusion.1
  39.9 1.4 collective-permute-start.5
  42.1 7.4 %gather.5 = bf16[2048,512]{1,0:T(8,128)(2,1)} custom-call(s32[256,8]{1,0:T(8,128)S(1)} %copy.35.asked_ref, bf16[2048,512]{1,0:T(8,128)(2,1)} %rows_ref.7), custom_call_target="tpu_custom_call" | custom-call | flops 100000000 | bytes 1000000 | tf_op jit(solution)/shard_map/gather/pallas_call | solution.py:152
  49.6 7.4 %gather.6 = bf16[2048,512]{1,0:T(8,128)(2,1)} custom-call(s32[256,8]{1,0:T(8,128)S(1)} %copy.37.asked_ref, bf16[2048,512]{1,0:T(8,128)(2,1)} %rows_ref.7), custom_call_target="tpu_custom_call" | custom-call | flops 100000000 | bytes 1000000 | tf_op jit(solution)/shard_map/gather/pallas_call | solution.py:152
  57.0 3.4 %spread.4.weight_ref = bf16[1024,2048]{1,0:T(8,128)(2,1)} custom-call(s32[8]{0:T(128)S(1)} %add.99.base_ref, bf16[1088,128]{1,0:T(8,128)(2,1)S(1)} %collective-permute-done.1.refs_0_.refs_1_.refs_2_, bf16[1088,128]{1,0:T(8,128)(2,1)S(1)} %collective-permute-done.1.refs_0_.refs_1_.refs_2_, ...), custom_call_target="tpu_custom_call" | custom-call | flops 100000000 | bytes 1000000 | tf_op jit(solution)/shard_map/spread/pallas_call | solution.py:122
  60.4 3.8 %collective-permute-start.8 = (bf16[1088,128]{1,0:T(8,128)(2,1)S(1)}, bf16[1088,128]{1,0:T(8,128)(2,1)S(1)}, u32[]{:S(2)}, u32[]{:S(2)}) collective-permute-start(bf16[1088,128]{1,0:T(8,128)(2,1)S(1)} %pad_maximum_fusion.refs_0_.refs_1_.refs_2_), channel_id=1, source_target_pairs={{0,2},{1,3},{2,0},{3,1},{4,6},{5,7},{6,4},{7,5},{8,10},{9,11},{10,... | collective-permute-start | bytes 835592 | tf_op jit(solution)/shard_map/ppermute | solution.py:356
  64.2 0.7 collective-permute-start.7
  64.9 4.4 %all-to-all-start.2 = ((bf16[8,256,512]{2,1,0:T(8,128)(2,1)}), bf16[8,256,512]{2,1,0:T(8,128)(2,1)}, u32[]{:S(2)}, u32[]{:S(2)}) async-start(bf16[8,256,512]{2,1,0:T(8,128)(2,1)} %bitcast.10), calls=%async_computation.2 | async-start | bytes 4194304 | tf_op jit(solution)/shard_map/all_to_all | solution.py:359
  69.3 5.5 %blend.4 = bf16[1024,512]{1,0:T(8,128)(2,1)} custom-call(bf16[1024,2048]{1,0:T(8,128)(2,1)} %spread.4.weight_ref, bf16[2048,512]{1,0:T(8,128)(2,1)S(1)} %bitcast.57), custom_call_target="tpu_custom_call" | custom-call | flops 4000000000 | bytes 10000000 | tf_op jit(solution)/shard_map/blend/pallas_call | solution.py:199
  74.9 1.3 collective-permute-start.6
  76.2 4.7 %collective-permute-start.10 = (bf16[1024,512]{1,0:T(8,128)(2,1)}, bf16[1024,512]{1,0:T(8,128)(2,1)}, u32[]{:S(2)}, u32[]{:S(2)}) collective-permute-start(bf16[1024,512]{1,0:T(8,128)(2,1)} %blend.4), channel_id=1, source_target_pairs={{0,2},{1,3},{6,4},{7,5},{8,10},{9,11},{14,12},{15,13},{16,18},{17,... | collective-permute-start | bytes 3145736 | tf_op jit(solution)/shard_map/ppermute | solution.py:356
  80.9 1.1 collective-permute-done.4.refs_2_
  82.0 16.5 %encode.1 = bf16[4,256,512]{2,1,0:T(8,128)(2,1)S(1)} custom-call(bf16[256,768]{1,0:T(8,128)(2,1)S(1)} %get-tuple-element.68.refs_0_, bf16[256,768]{1,0:T(8,128)(2,1)} %collective-permute-done.3.refs_1_, bf16[256,768]{1,0:T(8,128)(2,1)} %collective-permute-done.4.refs_2_, bf16[256,768]{1,0:T(8,128)(2,1)} %collective-permute-done.5.refs_3_, ...), custom_call_target="tpu_custom_call" | custom-call | flops 99999997952 | bytes 10000000 | tf_op jit(solution)/shard_map/encode/pallas_call | solution.py:305
  98.5 0.9 copy-done.13
  99.5 4.4 %all-to-all-start.3 = ((bf16[8,256,512]{2,1,0:T(8,128)(2,1)}), bf16[8,256,512]{2,1,0:T(8,128)(2,1)}, u32[]{:S(2)}, u32[]{:S(2)}) async-start(bf16[8,256,512]{2,1,0:T(8,128)(2,1)} %bitcast.18), calls=%async_computation.3 | async-start | bytes 4194304 | tf_op jit(solution)/shard_map/all_to_all | solution.py:359
  103.8 2.8 add.110
  106.6 1.6 collective-permute-start.11
  108.3 3.4 %spread.5.weight_ref = bf16[1024,2048]{1,0:T(8,128)(2,1)} custom-call(s32[8]{0:T(128)S(1)} %add.99.base_ref, bf16[1088,128]{1,0:T(8,128)(2,1)S(1)} %collective-permute-done.6.refs_0_.refs_1_.refs_2_, bf16[1088,128]{1,0:T(8,128)(2,1)S(1)} %collective-permute-done.6.refs_0_.refs_1_.refs_2_, ...), custom_call_target="tpu_custom_call" | custom-call | flops 100000000 | bytes 1000000 | tf_op jit(solution)/shard_map/spread/pallas_call | solution.py:122
  111.6 5.4 %blend.5 = bf16[1024,512]{1,0:T(8,128)(2,1)S(1)} custom-call(bf16[1024,2048]{1,0:T(8,128)(2,1)} %spread.5.weight_ref, bf16[2048,512]{1,0:T(8,128)(2,1)} %bitcast.11.rows_ref), custom_call_target="tpu_custom_call" | custom-call | flops 4000000000 | bytes 10000000 | tf_op jit(solution)/shard_map/blend/pallas_call | solution.py:199
  117.0 7.2 %collective-permute-start.9 = (bf16[1024,512]{1,0:T(8,128)(2,1)S(1)}, bf16[1024,512]{1,0:T(8,128)(2,1)}, u32[]{:S(2)}, u32[]{:S(2)}) collective-permute-start(bf16[1024,512]{1,0:T(8,128)(2,1)S(1)} %blend.5), channel_id=1, source_target_pairs={{0,2},{1,3},{6,4},{7,5},{8,10},{9,11},{14,12},{15,13},{16,18},{17,... | collective-permute-start | bytes 3145736 | tf_op jit(solution)/shard_map/ppermute | solution.py:356
  124.4 7.4 %gather.7 = bf16[2048,512]{1,0:T(8,128)(2,1)} custom-call(s32[256,8]{1,0:T(8,128)S(1)} %copy.39.asked_ref, bf16[2048,512]{1,0:T(8,128)(2,1)} %rows_ref.7), custom_call_target="tpu_custom_call" | custom-call | flops 100000000 | bytes 1000000 | tf_op jit(solution)/shard_map/gather/pallas_call | solution.py:152
  131.8 3.4 %spread.6.weight_ref = bf16[1024,2048]{1,0:T(8,128)(2,1)} custom-call(s32[8]{0:T(128)S(1)} %add.99.base_ref, bf16[1088,128]{1,0:T(8,128)(2,1)S(1)} %collective-permute-done.8.refs_0_.refs_1_.refs_2_, bf16[1088,128]{1,0:T(8,128)(2,1)S(1)} %collective-permute-done.8.refs_0_.refs_1_.refs_2_, bf16[1088,128]{1,0:T(8,128)(2,1)S(1)} %collective-permute-done.8.refs_0_.refs_1_.refs_2_), custom_call_target="tpu_custom_call" | custom-call | flops 100000000 | bytes 1000000 | tf_op jit(solution)/shard_map/spread/pallas_call | solution.py:122
  135.2 4.4 %all-to-all-start.4 = ((bf16[8,256,512]{2,1,0:T(8,128)(2,1)}), bf16[8,256,512]{2,1,0:T(8,128)(2,1)}, u32[]{:S(2)}, u32[]{:S(2)}) async-start(bf16[8,256,512]{2,1,0:T(8,128)(2,1)} %bitcast.20), calls=%async_computation.4 | async-start | bytes 4194304 | tf_op jit(solution)/shard_map/all_to_all | solution.py:359
  139.6 5.5 %blend.6 = bf16[1024,512]{1,0:T(8,128)(2,1)S(1)} custom-call(bf16[1024,2048]{1,0:T(8,128)(2,1)} %spread.6.weight_ref, bf16[2048,512]{1,0:T(8,128)(2,1)} %bitcast.19.rows_ref, bf16[1024,512]{1,0:T(8,128)(2,1)} %collective-permute-done.11.rest_0_), custom_call_target="tpu_custom_call" | custom-call | flops 4000000000 | bytes 10000000 | tf_op jit(solution)/shard_map/blend/pallas_call | solution.py:199
  145.1 1.5 add.111
  146.6 0.7 collective-permute-start.13
  147.4 3.8 %collective-permute-start.12 = (bf16[1024,512]{1,0:T(8,128)(2,1)S(1)}, bf16[1024,512]{1,0:T(8,128)(2,1)S(1)}, u32[]{:S(2)}, u32[]{:S(2)}) collective-permute-start(bf16[1024,512]{1,0:T(8,128)(2,1)S(1)} %blend.6), channel_id=1, source_target_pairs={{0,2},{1,3},{2,0},{3,1},{4,6},{5,7},{6,4},{7,5},{8,10},{9,11},{10,... | collective-permute-start | bytes 3145736 | tf_op jit(solution)/shard_map/ppermute | solution.py:356
  151.2 3.3 %spread.7.weight_ref = bf16[1024,2048]{1,0:T(8,128)(2,1)} custom-call(s32[8]{0:T(128)S(1)} %add.99.base_ref, bf16[1088,128]{1,0:T(8,128)(2,1)S(1)} %pad_maximum_fusion.refs_0_.refs_1_.refs_2_, bf16[1088,128]{1,0:T(8,128)(2,1)S(1)} %pad_maximum_fusion.refs_0_.refs_1_.refs_2_, bf16[1088,128]{1,0:T(8,128)(2,1)S(1)} %pad_maximum_fusion.refs_0_.refs_1_.refs_2_), custom_call_target="tpu_custom_call" | custom-call | flops 100000000 | bytes 1000000 | tf_op jit(solution)/shard_map/spread/pallas_call | solution.py:122
  154.5 19.2 %collective-permute-done.12.rest_0_ = bf16[1024,512]{1,0:T(8,128)(2,1)S(1)} collective-permute-done((bf16[1024,512]{1,0:T(8,128)(2,1)S(1)}, bf16[1024,512]{1,0:T(8,128)(2,1)S(1)}, u32[]{:S(2)}, u32[]{:S(2)}) %collective-permute-start.12) | collective-permute-done | bytes 1048608 | tf_op jit(solution)/shard_map/ppermute | solution.py:356
  173.7 6.8 %blend.7 = (bf16[1024,512]{1,0:T(8,128)(2,1)}, bf16[1024,512]{1,0:T(8,128)(2,1)}) custom-call(s32[8]{0:T(128)S(1)} %fusion.8.place_ref, bf16[1024,2048]{1,0:T(8,128)(2,1)} %spread.7.weight_ref, bf16[2048,512]{1,0:T(8,128)(2,1)} %bitcast.21.rows_ref, bf16[1024,512]{1,0:T(8,128)(2,1)S(1)} %collective-permute-done.12.rest_0_, ...), custom_call_target="tpu_custom_call" | custom-call | flops 4000000000 | bytes 10000000 | tf_op jit(solution)/shard_map/blend/pallas_call | solution.py:199
  180.6 0.7 collective-permute-start.17
  181.3 3.3 %collective-permute-start.14 = (bf16[1024,512]{1,0:T(8,128)(2,1)}, bf16[1024,512]{1,0:T(8,128)(2,1)}, u32[]{:S(2)}, u32[]{:S(2)}) collective-permute-start(bf16[1024,512]{1,0:T(8,128)(2,1)} %get-tuple-element.93.refs_0_), channel_id=1, source_target_pairs={{0,2},{1,3},{2,0},{3,1},{4,6},{5,7},{6,4},{7,5},{8,10},{9,11},{10,... | collective-permute-start | bytes 3145736 | tf_op jit(solution)/shard_map/ppermute | solution.py:356
  184.6 4.5 %terms.7 = bf16[2048,512]{1,0:T(8,128)(2,1)S(1)} custom-call(bf16[1024,2048]{1,0:T(8,128)(2,1)} %spread.7.weight_ref, bf16[1024,512]{1,0:T(8,128)(2,1)} %get-tuple-element.93.refs_0_), custom_call_target="tpu_custom_call" | custom-call | flops 99999997952 | bytes 10000000 | tf_op jit(solution)/shard_map/terms/pallas_call | solution.py:222
  189.1 1.3 copy-done.1
  190.4 3.9 %all-to-all-start.5 = ((bf16[8,256,512]{2,1,0:T(8,128)(2,1)}), bf16[8,256,512]{2,1,0:T(8,128)(2,1)S(1)}, u32[]{:S(2)}, u32[]{:S(2)}) async-start(bf16[8,256,512]{2,1,0:T(8,128)(2,1)} %bitcast.60), calls=%async_computation.5 | async-start | bytes 4194304 | tf_op jit(solution)/shard_map/all_to_all | solution.py:359
  194.3 1.3 collective-permute-start.18
  195.6 10.9 %collective-permute-done.14.refs_0_ = bf16[1024,512]{1,0:T(8,128)(2,1)} collective-permute-done((bf16[1024,512]{1,0:T(8,128)(2,1)}, bf16[1024,512]{1,0:T(8,128)(2,1)}, u32[]{:S(2)}, u32[]{:S(2)}) %collective-permute-start.14) | collective-permute-done | bytes 1048608 | tf_op jit(solution)/shard_map/ppermute | solution.py:356
  206.5 1.7 collective-permute-start.15
  208.1 4.5 %terms.6 = bf16[2048,512]{1,0:T(8,128)(2,1)S(1)} custom-call(bf16[1024,2048]{1,0:T(8,128)(2,1)} %spread.6.weight_ref, bf16[1024,512]{1,0:T(8,128)(2,1)} %collective-permute-done.14.refs_0_), custom_call_target="tpu_custom_call" | custom-call | flops 99999997952 | bytes 10000000 | tf_op jit(solution)/shard_map/terms/pallas_call | solution.py:222
  212.6 1.3 copy-done
  213.9 7.0 %all-to-all-done.5 = bf16[8,256,512]{2,1,0:T(8,128)(2,1)S(1)} async-done(((bf16[8,256,512]{2,1,0:T(8,128)(2,1)}), bf16[8,256,512]{2,1,0:T(8,128)(2,1)S(1)}, u32[]{:S(2)}, u32[]{:S(2)}) %all-to-all-start.5) | async-done | bytes 2097184 | tf_op jit(solution)/shard_map/all_to_all | solution.py:359
  220.9 4.3 %all-to-all-start.6 = ((bf16[8,256,512]{2,1,0:T(8,128)(2,1)}), bf16[8,256,512]{2,1,0:T(8,128)(2,1)}, u32[]{:S(2)}, u32[]{:S(2)}) async-start(bf16[8,256,512]{2,1,0:T(8,128)(2,1)} %bitcast.59), calls=%async_computation.6 | async-start | bytes 4194304 | tf_op jit(solution)/shard_map/all_to_all | solution.py:359
  225.3 1.3 collective-permute-start.16
  226.6 3.4 %collective-permute-done.18.refs_1_ = bf16[1024,512]{1,0:T(8,128)(2,1)} collective-permute-done((bf16[1024,512]{1,0:T(8,128)(2,1)S(1)}, bf16[1024,512]{1,0:T(8,128)(2,1)}, u32[]{:S(2)}, u32[]{:S(2)}) %collective-permute-start.18) | collective-permute-done | bytes 1048608 | tf_op jit(solution)/shard_map/ppermute | solution.py:356
  230.0 5.5 %terms.5 = bf16[2048,512]{1,0:T(8,128)(2,1)} custom-call(bf16[1024,2048]{1,0:T(8,128)(2,1)} %spread.5.weight_ref, bf16[1024,512]{1,0:T(8,128)(2,1)S(1)} %collective-permute-done.17.refs_0_, bf16[1024,512]{1,0:T(8,128)(2,1)} %collective-permute-done.18.refs_1_), custom_call_target="tpu_custom_call" | custom-call | flops 99999997952 | bytes 10000000 | tf_op jit(solution)/shard_map/terms/pallas_call | solution.py:222
  235.5 16.4 %all-to-all-done.6 = bf16[8,256,512]{2,1,0:T(8,128)(2,1)} async-done(((bf16[8,256,512]{2,1,0:T(8,128)(2,1)}), bf16[8,256,512]{2,1,0:T(8,128)(2,1)}, u32[]{:S(2)}, u32[]{:S(2)}) %all-to-all-start.6) | async-done | bytes 2097184 | tf_op jit(solution)/shard_map/all_to_all | solution.py:359
  251.9 4.3 %all-to-all-start.7 = ((bf16[8,256,512]{2,1,0:T(8,128)(2,1)}), bf16[8,256,512]{2,1,0:T(8,128)(2,1)}, u32[]{:S(2)}, u32[]{:S(2)}) async-start(bf16[8,256,512]{2,1,0:T(8,128)(2,1)} %bitcast.69), calls=%async_computation.7 | async-start | bytes 4194304 | tf_op jit(solution)/shard_map/all_to_all | solution.py:359
  256.3 5.7 %terms.4 = bf16[2048,512]{1,0:T(8,128)(2,1)} custom-call(bf16[1024,2048]{1,0:T(8,128)(2,1)} %spread.4.weight_ref, bf16[1024,512]{1,0:T(8,128)(2,1)} %collective-permute-done.15.refs_0_, bf16[1024,512]{1,0:T(8,128)(2,1)} %collective-permute-done.16.refs_1_), custom_call_target="tpu_custom_call" | custom-call | flops 99999997952 | bytes 10000000 | tf_op jit(solution)/shard_map/terms/pallas_call | solution.py:222
  262.0 20.9 %all-to-all-done.7 = bf16[8,256,512]{2,1,0:T(8,128)(2,1)} async-done(((bf16[8,256,512]{2,1,0:T(8,128)(2,1)}), bf16[8,256,512]{2,1,0:T(8,128)(2,1)}, u32[]{:S(2)}, u32[]{:S(2)}) %all-to-all-start.7) | async-done | bytes 2097184 | tf_op jit(solution)/shard_map/all_to_all | solution.py:359
  282.9 4.6 %all-to-all-start.8 = ((bf16[8,256,512]{2,1,0:T(8,128)(2,1)}), bf16[8,256,512]{2,1,0:T(8,128)(2,1)}, u32[]{:S(2)}, u32[]{:S(2)}) async-start(bf16[8,256,512]{2,1,0:T(8,128)(2,1)} %bitcast.70), calls=%async_computation.8 | async-start | bytes 4194304 | tf_op jit(solution)/shard_map/all_to_all | solution.py:359
  287.6 16.9 %add_rows.2.refs_2_ = f32[2048,512]{1,0:T(8,128)} custom-call(s32[8,256]{1,0:T(8,128)S(1)} %reshape.74.refs_0_, s32[8,256]{1,0:T(8,128)S(1)} %reshape.73.refs_1_, s32[8,256]{1,0:T(8,128)S(1)} %reshape.72.refs_2_, bf16[2048,512]{1,0:T(8,128)(2,1)S(1)} %bitcast.58, bf16[2048,512]{1,0:T(8,128)(2,1)} %bitcast.27.refs_4_, bf16[2048,512]{1,0:T(8,128)(2,1)} %bitcast.29.refs_5_), custom_call_target="tpu_custom_call" | custom-call | flops 15000000512 | bytes 10000000 | tf_op jit(solution)/shard_map/add_rows/pallas_call | solution.py:261
  304.4 9.5 %all-to-all-done.8 = bf16[8,256,512]{2,1,0:T(8,128)(2,1)} async-done(((bf16[8,256,512]{2,1,0:T(8,128)(2,1)}), bf16[8,256,512]{2,1,0:T(8,128)(2,1)}, u32[]{:S(2)}, u32[]{:S(2)}) %all-to-all-start.8) | async-done | bytes 2097184 | tf_op jit(solution)/shard_map/all_to_all | solution.py:359
  314.0 8.3 %add_rows.3 = f32[2048,512]{1,0:T(8,128)} custom-call(s32[8,256]{1,0:T(8,128)S(1)} %copy-done.4, bf16[2048,512]{1,0:T(8,128)(2,1)} %bitcast.31.refs_1_, f32[2048,512]{1,0:T(8,128)} %add_rows.2.refs_2_), custom_call_target="tpu_custom_call" | custom-call | flops 5000000000 | bytes 10000000 | tf_op jit(solution)/shard_map/add_rows/pallas_call | solution.py:261
  (66 shorter events, 2.1 us)
Async XLA Ops:
  0.6 0.7 copy-start.6
  1.4 1.4 copy-start.14
  2.6 9.2 %copy-start.2 = (f32[8,4,32,128]{3,2,1,0:T(8,128)S(1)}, f32[8,4,32,128]{3,2,1,0:T(8,128)}, u32[]{:S(2)}) copy-start(f32[8,4,32,128]{3,2,1,0:T(8,128)} %param.25) | copy-start | bytes 1572868
  3.8 15.3 %collective-permute-start = (bf16[4,128,768]{2,1,0:T(8,128)(2,1)S(1)}, bf16[4,128,768]{2,1,0:T(8,128)(2,1)S(1)}, u32[]{:S(2)}, u32[]{:S(2)}) collective-permute-start(bf16[4,128,768]{2,1,0:T(8,128)(2,1)S(1)} %get-tuple-element.105), channel_id=1, source_target_pairs={{0,1},{1,0},{2,3},{3,2},{4,5},{5,4},{6,7},{7,6},{8,9},{9,8},{10,11... | collective-permute-start | bytes 2359304 | tf_op jit(solution)/shard_map/ppermute | solution.py:356
  4.9 14.2 %all-to-all-start = ((s32[32,1,256]{2,1,0:T(1,128)}), s32[32,1,256]{2,1,0:T(1,128)S(1)}, u32[]{:S(2)}, u32[]{:S(2)}) async-start(s32[32,1,256]{2,1,0:T(1,128)} %copy.31), calls=%async_computation | async-start | bytes 65536 | tf_op jit(solution)/shard_map/all_to_all | solution.py:368
  19.1 7.7 %copy-start.15 = (bf16[4,128,768]{2,1,0:T(8,128)(2,1)}, bf16[4,128,768]{2,1,0:T(8,128)(2,1)S(1)}, u32[]{:S(2)}) copy-start(bf16[4,128,768]{2,1,0:T(8,128)(2,1)S(1)} %collective-permute-done) | copy-start | bytes 2359300
  19.2 7.7 %copy-start.3 = (s32[8,256]{1,0:T(8,128)}, s32[8,256]{1,0:T(8,128)S(1)}, u32[]{:S(2)}) copy-start(s32[8,256]{1,0:T(8,128)S(1)} %reshape.71.refs_0_) | copy-start | bytes 24580
  26.8 33.6 %all-to-all-start.1 = ((bf16[8,256,512]{2,1,0:T(8,128)(2,1)}), bf16[8,256,512]{2,1,0:T(8,128)(2,1)S(1)}, u32[]{:S(2)}, u32[]{:S(2)}) async-start(bf16[8,256,512]{2,1,0:T(8,128)(2,1)} %bitcast.8), calls=%async_computation.1 | async-start | bytes 4194304 | tf_op jit(solution)/shard_map/all_to_all | solution.py:359
  30.4 26.6 %collective-permute-start.2 = (bf16[1088,128]{1,0:T(8,128)(2,1)S(1)}, bf16[1088,128]{1,0:T(8,128)(2,1)S(1)}, u32[]{:S(2)}, u32[]{:S(2)}) collective-permute-start(bf16[1088,128]{1,0:T(8,128)(2,1)S(1)} %pad_maximum_fusion.refs_0_.refs_1_.refs_2_), channel_id=1, source_target_pairs={{0,4},{1,5},{6,2},{7,3},{8,12},{9,13},{14,10},{15,11},{16,20},{17,... | collective-permute-start | bytes 835592 | tf_op jit(solution)/shard_map/ppermute | solution.py:356
  32.8 24.2 %collective-permute-start.1 = (bf16[1088,128]{1,0:T(8,128)(2,1)S(1)}, bf16[1088,128]{1,0:T(8,128)(2,1)S(1)}, u32[]{:S(2)}, u32[]{:S(2)}) collective-permute-start(bf16[1088,128]{1,0:T(8,128)(2,1)S(1)} %pad_maximum_fusion.refs_0_.refs_1_.refs_2_), channel_id=1, source_target_pairs={{0,6},{1,7},{6,0},{7,1},{8,14},{9,15},{14,8},{15,9},{16,22},{17,23... | collective-permute-start | bytes 835592 | tf_op jit(solution)/shard_map/ppermute | solution.py:356
  39.9 34.9 %collective-permute-start.5 = (bf16[256,768]{1,0:T(8,128)(2,1)}, bf16[256,768]{1,0:T(8,128)(2,1)}, u32[]{:S(2)}, u32[]{:S(2)}) collective-permute-start(bf16[256,768]{1,0:T(8,128)(2,1)} %get-tuple-element.100), channel_id=1, source_target_pairs={{0,6},{1,7},{2,0},{3,1},{4,2},{5,3},{6,4},{7,5},{8,14},{9,15},{10,... | collective-permute-start | bytes 1179656 | tf_op jit(solution)/shard_map/ppermute | solution.py:356
  41.3 34.8 %collective-permute-start.3 = (bf16[256,768]{1,0:T(8,128)(2,1)}, bf16[256,768]{1,0:T(8,128)(2,1)}, u32[]{:S(2)}, u32[]{:S(2)}) collective-permute-start(bf16[256,768]{1,0:T(8,128)(2,1)} %get-tuple-element.102), channel_id=1, source_target_pairs={{0,2},{1,3},{2,4},{3,5},{4,6},{5,7},{6,0},{7,1},{8,10},{9,11},{10,... | collective-permute-start | bytes 1179656 | tf_op jit(solution)/shard_map/ppermute | solution.py:356
  41.9 40.0 %collective-permute-start.4 = (bf16[256,768]{1,0:T(8,128)(2,1)}, bf16[256,768]{1,0:T(8,128)(2,1)}, u32[]{:S(2)}, u32[]{:S(2)}) collective-permute-start(bf16[256,768]{1,0:T(8,128)(2,1)} %get-tuple-element.103), channel_id=1, source_target_pairs={{0,4},{1,5},{2,6},{3,7},{4,0},{5,1},{6,2},{7,3},{8,12},{9,13},{10,... | collective-permute-start | bytes 1179656 | tf_op jit(solution)/shard_map/ppermute | solution.py:356
  60.4 38.1 %collective-permute-start.8 = (bf16[1088,128]{1,0:T(8,128)(2,1)S(1)}, bf16[1088,128]{1,0:T(8,128)(2,1)S(1)}, u32[]{:S(2)}, u32[]{:S(2)}) collective-permute-start(bf16[1088,128]{1,0:T(8,128)(2,1)S(1)} %pad_maximum_fusion.refs_0_.refs_1_.refs_2_), channel_id=1, source_target_pairs={{0,2},{1,3},{2,0},{3,1},{4,6},{5,7},{6,4},{7,5},{8,10},{9,11},{10,... | collective-permute-start | bytes 835592 | tf_op jit(solution)/shard_map/ppermute | solution.py:356
  64.2 34.3 %collective-permute-start.7 = (bf16[1088,128]{1,0:T(8,128)(2,1)S(1)}, bf16[1088,128]{1,0:T(8,128)(2,1)S(1)}, u32[]{:S(2)}, u32[]{:S(2)}) collective-permute-start(bf16[1088,128]{1,0:T(8,128)(2,1)S(1)} %pad_maximum_fusion.refs_0_.refs_1_.refs_2_), channel_id=1, source_target_pairs={{2,4},{3,5},{4,2},{5,3},{10,12},{11,13},{12,10},{13,11},{18,20},{1... | collective-permute-start | bytes 835592 | tf_op jit(solution)/shard_map/ppermute | solution.py:356
  64.9 33.6 %all-to-all-start.2 = ((bf16[8,256,512]{2,1,0:T(8,128)(2,1)}), bf16[8,256,512]{2,1,0:T(8,128)(2,1)}, u32[]{:S(2)}, u32[]{:S(2)}) async-start(bf16[8,256,512]{2,1,0:T(8,128)(2,1)} %bitcast.10), calls=%async_computation.2 | async-start | bytes 4194304 | tf_op jit(solution)/shard_map/all_to_all | solution.py:359
  69.2 12.7 %copy-start.5 = (bf16[768,512]{1,0:T(8,128)(2,1)S(1)}, bf16[768,512]{1,0:T(8,128)(2,1)}, u32[]{:S(2)}) copy-start(bf16[768,512]{1,0:T(8,128)(2,1)} %refs_12_.1) | copy-start | bytes 2359300
  69.3 12.7 %copy-start.7 = (f32[3072]{0:T(1024)S(1)}, f32[3072]{0:T(1024)}, u32[]{:S(2)}) copy-start(f32[3072]{0:T(1024)} %refs_7_.1) | copy-start | bytes 36868
  69.3 12.7 %copy-start.8 = (f32[768]{0:T(1024)S(1)}, f32[768]{0:T(1024)}, u32[]{:S(2)}) copy-start(f32[768]{0:T(1024)} %refs_4_.1) | copy-start | bytes 9220
  69.3 12.7 %copy-start.9 = (f32[768]{0:T(1024)S(1)}, f32[768]{0:T(1024)}, u32[]{:S(2)}) copy-start(f32[768]{0:T(1024)} %refs_5_.1) | copy-start | bytes 9220
  69.3 12.7 %copy-start.10 = (f32[768]{0:T(1024)S(1)}, f32[768]{0:T(1024)}, u32[]{:S(2)}) copy-start(f32[768]{0:T(1024)} %refs_9_.1) | copy-start | bytes 9220
  69.3 12.7 %copy-start.11 = (f32[768]{0:T(1024)S(1)}, f32[768]{0:T(1024)}, u32[]{:S(2)}) copy-start(f32[768]{0:T(1024)} %refs_10_.1) | copy-start | bytes 9220
  69.3 12.7 %copy-start.12 = (f32[768]{0:T(1024)S(1)}, f32[768]{0:T(1024)}, u32[]{:S(2)}) copy-start(f32[768]{0:T(1024)} %refs_11_.1) | copy-start | bytes 9220
  74.9 23.6 %collective-permute-start.6 = (bf16[1088,128]{1,0:T(8,128)(2,1)S(1)}, bf16[1088,128]{1,0:T(8,128)(2,1)S(1)}, u32[]{:S(2)}, u32[]{:S(2)}) collective-permute-start(bf16[1088,128]{1,0:T(8,128)(2,1)S(1)} %pad_maximum_fusion.refs_0_.refs_1_.refs_2_), channel_id=1, source_target_pairs={{2,6},{3,7},{4,0},{5,1},{10,14},{11,15},{12,8},{13,9},{18,22},{19,... | collective-permute-start | bytes 835592 | tf_op jit(solution)/shard_map/ppermute | solution.py:356
  76.2 27.7 %collective-permute-start.10 = (bf16[1024,512]{1,0:T(8,128)(2,1)}, bf16[1024,512]{1,0:T(8,128)(2,1)}, u32[]{:S(2)}, u32[]{:S(2)}) collective-permute-start(bf16[1024,512]{1,0:T(8,128)(2,1)} %blend.4), channel_id=1, source_target_pairs={{0,2},{1,3},{6,4},{7,5},{8,10},{9,11},{14,12},{15,13},{16,18},{17,... | collective-permute-start | bytes 3145736 | tf_op jit(solution)/shard_map/ppermute | solution.py:356
  98.5 1.0 copy-start.13
  99.5 35.8 %all-to-all-start.3 = ((bf16[8,256,512]{2,1,0:T(8,128)(2,1)}), bf16[8,256,512]{2,1,0:T(8,128)(2,1)}, u32[]{:S(2)}, u32[]{:S(2)}) async-start(bf16[8,256,512]{2,1,0:T(8,128)(2,1)} %bitcast.18), calls=%async_computation.3 | async-start | bytes 4194304 | tf_op jit(solution)/shard_map/all_to_all | solution.py:359
  106.6 28.6 %collective-permute-start.11 = (bf16[1024,512]{1,0:T(8,128)(2,1)}, bf16[1024,512]{1,0:T(8,128)(2,1)}, u32[]{:S(2)}, u32[]{:S(2)}) collective-permute-start(bf16[1024,512]{1,0:T(8,128)(2,1)} %add.110), channel_id=1, source_target_pairs={{2,4},{3,5},{4,2},{5,3},{10,12},{11,13},{12,10},{13,11},{18,20},{1... | collective-permute-start | bytes 3145736 | tf_op jit(solution)/shard_map/ppermute | solution.py:356
  117.0 28.1 %collective-permute-start.9 = (bf16[1024,512]{1,0:T(8,128)(2,1)S(1)}, bf16[1024,512]{1,0:T(8,128)(2,1)}, u32[]{:S(2)}, u32[]{:S(2)}) collective-permute-start(bf16[1024,512]{1,0:T(8,128)(2,1)S(1)} %blend.5), channel_id=1, source_target_pairs={{0,2},{1,3},{6,4},{7,5},{8,10},{9,11},{14,12},{15,13},{16,18},{17,... | collective-permute-start | bytes 3145736 | tf_op jit(solution)/shard_map/ppermute | solution.py:356
  135.2 38.5 %all-to-all-start.4 = ((bf16[8,256,512]{2,1,0:T(8,128)(2,1)}), bf16[8,256,512]{2,1,0:T(8,128)(2,1)}, u32[]{:S(2)}, u32[]{:S(2)}) async-start(bf16[8,256,512]{2,1,0:T(8,128)(2,1)} %bitcast.20), calls=%async_computation.4 | async-start | bytes 4194304 | tf_op jit(solution)/shard_map/all_to_all | solution.py:359
  146.6 7.9 %collective-permute-start.13 = (bf16[1024,512]{1,0:T(8,128)(2,1)S(1)}, bf16[1024,512]{1,0:T(8,128)(2,1)S(1)}, u32[]{:S(2)}, u32[]{:S(2)}) collective-permute-start(bf16[1024,512]{1,0:T(8,128)(2,1)S(1)} %add.111), channel_id=1, source_target_pairs={{2,4},{3,5},{4,2},{5,3},{10,12},{11,13},{12,10},{13,11},{18,20},{1... | collective-permute-start | bytes 3145736 | tf_op jit(solution)/shard_map/ppermute | solution.py:356
  147.4 26.4 %collective-permute-start.12 = (bf16[1024,512]{1,0:T(8,128)(2,1)S(1)}, bf16[1024,512]{1,0:T(8,128)(2,1)S(1)}, u32[]{:S(2)}, u32[]{:S(2)}) collective-permute-start(bf16[1024,512]{1,0:T(8,128)(2,1)S(1)} %blend.6), channel_id=1, source_target_pairs={{0,2},{1,3},{2,0},{3,1},{4,6},{5,7},{6,4},{7,5},{8,10},{9,11},{10,... | collective-permute-start | bytes 3145736 | tf_op jit(solution)/shard_map/ppermute | solution.py:356
  180.6 13.7 %collective-permute-start.17 = (bf16[1024,512]{1,0:T(8,128)(2,1)}, bf16[1024,512]{1,0:T(8,128)(2,1)S(1)}, u32[]{:S(2)}, u32[]{:S(2)}) collective-permute-start(bf16[1024,512]{1,0:T(8,128)(2,1)} %get-tuple-element.93.refs_0_), channel_id=1, source_target_pairs={{2,4},{3,5},{4,2},{5,3},{10,12},{11,13},{12,10},{13,11},{18,20},{1... | collective-permute-start | bytes 3145736 | tf_op jit(solution)/shard_map/ppermute | solution.py:356
  181.3 25.1 %collective-permute-start.14 = (bf16[1024,512]{1,0:T(8,128)(2,1)}, bf16[1024,512]{1,0:T(8,128)(2,1)}, u32[]{:S(2)}, u32[]{:S(2)}) collective-permute-start(bf16[1024,512]{1,0:T(8,128)(2,1)} %get-tuple-element.93.refs_0_), channel_id=1, source_target_pairs={{0,2},{1,3},{2,0},{3,1},{4,6},{5,7},{6,4},{7,5},{8,10},{9,11},{10,... | collective-permute-start | bytes 3145736 | tf_op jit(solution)/shard_map/ppermute | solution.py:356
  189.1 1.3 copy-start.1
  190.4 30.5 %all-to-all-start.5 = ((bf16[8,256,512]{2,1,0:T(8,128)(2,1)}), bf16[8,256,512]{2,1,0:T(8,128)(2,1)S(1)}, u32[]{:S(2)}, u32[]{:S(2)}) async-start(bf16[8,256,512]{2,1,0:T(8,128)(2,1)} %bitcast.60), calls=%async_computation.5 | async-start | bytes 4194304 | tf_op jit(solution)/shard_map/all_to_all | solution.py:359
  194.3 35.7 %collective-permute-start.18 = (bf16[1024,512]{1,0:T(8,128)(2,1)S(1)}, bf16[1024,512]{1,0:T(8,128)(2,1)}, u32[]{:S(2)}, u32[]{:S(2)}) collective-permute-start(bf16[1024,512]{1,0:T(8,128)(2,1)S(1)} %collective-permute-done.17.refs_0_), channel_id=1, source_target_pairs={{2,0},{3,1},{4,6},{5,7},{10,8},{11,9},{12,14},{13,15},{18,16},{19,... | collective-permute-start | bytes 3145736 | tf_op jit(solution)/shard_map/ppermute | solution.py:356
  206.5 18.8 %collective-permute-start.15 = (bf16[1024,512]{1,0:T(8,128)(2,1)}, bf16[1024,512]{1,0:T(8,128)(2,1)}, u32[]{:S(2)}, u32[]{:S(2)}) collective-permute-start(bf16[1024,512]{1,0:T(8,128)(2,1)} %collective-permute-done.14.refs_0_), channel_id=1, source_target_pairs={{2,4},{3,5},{4,2},{5,3},{10,12},{11,13},{12,10},{13,11},{18,20},{1... | collective-permute-start | bytes 3145736 | tf_op jit(solution)/shard_map/ppermute | solution.py:356
  212.6 1.3 copy-start
  220.9 31.0 %all-to-all-start.6 = ((bf16[8,256,512]{2,1,0:T(8,128)(2,1)}), bf16[8,256,512]{2,1,0:T(8,128)(2,1)}, u32[]{:S(2)}, u32[]{:S(2)}) async-start(bf16[8,256,512]{2,1,0:T(8,128)(2,1)} %bitcast.59), calls=%async_computation.6 | async-start | bytes 4194304 | tf_op jit(solution)/shard_map/all_to_all | solution.py:359
  225.3 31.0 %collective-permute-start.16 = (bf16[1024,512]{1,0:T(8,128)(2,1)}, bf16[1024,512]{1,0:T(8,128)(2,1)}, u32[]{:S(2)}, u32[]{:S(2)}) collective-permute-start(bf16[1024,512]{1,0:T(8,128)(2,1)} %collective-permute-done.15.refs_0_), channel_id=1, source_target_pairs={{2,0},{3,1},{4,6},{5,7},{10,8},{11,9},{12,14},{13,15},{18,16},{19,... | collective-permute-start | bytes 3145736 | tf_op jit(solution)/shard_map/ppermute | solution.py:356
  251.9 31.0 %all-to-all-start.7 = ((bf16[8,256,512]{2,1,0:T(8,128)(2,1)}), bf16[8,256,512]{2,1,0:T(8,128)(2,1)}, u32[]{:S(2)}, u32[]{:S(2)}) async-start(bf16[8,256,512]{2,1,0:T(8,128)(2,1)} %bitcast.69), calls=%async_computation.7 | async-start | bytes 4194304 | tf_op jit(solution)/shard_map/all_to_all | solution.py:359
  282.9 31.0 %all-to-all-start.8 = ((bf16[8,256,512]{2,1,0:T(8,128)(2,1)}), bf16[8,256,512]{2,1,0:T(8,128)(2,1)}, u32[]{:S(2)}, u32[]{:S(2)}) async-start(bf16[8,256,512]{2,1,0:T(8,128)(2,1)} %bitcast.70), calls=%async_computation.8 | async-start | bytes 4194304 | tf_op jit(solution)/shard_map/all_to_all | solution.py:359
  287.6 26.4 %copy-start.4 = (s32[8,256]{1,0:T(8,128)S(1)}, s32[8,256]{1,0:T(8,128)}, u32[]{:S(2)}) copy-start(s32[8,256]{1,0:T(8,128)} %copy-done.3) | copy-start | bytes 24580
